TPU v7x, 32 devices: a whole 2x2x4 slice. The times are simulated.
32 devices in a mesh: sp: 8 (over z, x), hd: 4 (over y, core).
Axes of the slice: x: 2, y: 2, z: 4, core: 2. Of those that a mesh axis runs over, the one named last changes fastest.
Arguments:
- cond: bfloat16 [8, 64, 64, 192], P('hd', 'sp'), may hold values from -6 to 6
- resid: bfloat16 [8, 64, 64, 320], P('hd', 'sp'), may hold values from -6 to 6
- context: bfloat16 [8, 1, 77, 768], P('hd'), may hold values from -6 to 6
- noise: float32 [8, 64, 64, 4], P('hd', 'sp'), may hold values from -6 to 6
- timesteps: int32 [8, 1], P('hd'), may hold values from 0 to 999
- step: int32 [1], replicated, may hold values from 1 to 20
- query_weight: bfloat16 [320, 320], replicated, may hold values from -0.3125 to 0.3125
- key_weight: bfloat16 [768, 320], replicated, may hold values from -0.21875 to 0.21875
- value_weight: bfloat16 [768, 320], replicated, may hold values from -0.21875 to 0.21875
- out_weight: bfloat16 [320, 320], replicated, may hold values from -1 to 1
- pred_weight: bfloat16 [320, 4], replicated, may hold values from -0.3125 to 0.3125
- master: float32 [1578240], P(('sp', 'hd')), as said below
- first_moment: float32 [1578240], P(('sp', 'hd')), may hold values from -0.0048828125 to 0.0048828125
- second_moment: float32 [1578240], P(('sp', 'hd')), may hold values from 9.536743e-08 to 3.8146973e-07
Outputs:
- loss: float32 [], replicated
- new_master: float32 [1578240], P(('sp', 'hd'))
- new_first: float32 [1578240], P(('sp', 'hd'))
- new_second: float32 [1578240], P(('sp', 'hd'))
Inputs may be any that keep to these rules, and one draw needn't show every extreme that they name: `master`: adapter parameters in the stated order.
All inputs are finite; a program needn't handle non-finite values.
Results may differ from a plain program's by a relative error of at most 0.024.
Values may be sent and summed in bfloat16 or wider, within the bound.
No kernel may reach another device: no remote copies, remote signals or barrier semaphores. Data moves between devices by JAX's collectives and lax.ppermute only.
A program may use at most 64 MiB of HBM per device.

v0:
```python
import functools

import jax
import jax.numpy as jnp
import numpy as np
from jax import lax
from jax.experimental import pallas as pl
from jax.experimental.pallas import tpu as pltpu
from jax.sharding import PartitionSpec as P

HDIM = 40
LANES = 128
EPS_NORM = 1e-05
RATE = 0.05
DECAY = 0.01
BETA_ONE = 0.5
BETA_TWO = 0.5
EPS_ADAM = 1e-08
SNR_CAP = 5.0
VMEM, HBM, DMA = pltpu.VMEM, pltpu.HBM, pltpu.SemaphoreType.DMA
BF = jnp.bfloat16
F32 = jnp.float32


def mm(a, b):
    return jnp.dot(a, b, preferred_element_type=F32)


def mm_nt(a, b):
    return lax.dot_general(a, b, (((1,), (1,)), ((), ())), preferred_element_type=F32)


def mm_tn(a, b):
    return lax.dot_general(a, b, (((0,), (0,)), ((), ())), preferred_element_type=F32)


def call(
    kernel, outs, ins, scratch=(), far=(), far_out=(), smem=(), free=(), flops=0, limit=40
):
    def space(i):
        return pltpu.SMEM if i in smem else pl.ANY if i in far else VMEM

    def hold(i, x):
        return x if i in smem or i in free else pltpu.with_memory_space_constraint(x, HBM if i in far else VMEM)

    return pl.pallas_call(
        kernel,
        out_shape=[(HBM if i in far_out else VMEM)(*o) for i, o in enumerate(outs)],
        in_specs=[pl.BlockSpec(memory_space=space(i)) for i in range(len(ins))],
        out_specs=[
            pl.BlockSpec(memory_space=pl.ANY if i in far_out else VMEM) for i in range(len(outs))
        ],
        scratch_shapes=list(scratch),
        compiler_params=pltpu.CompilerParams(vmem_limit_bytes=limit * 1024 * 1024),
        cost_estimate=pl.CostEstimate(flops=flops, bytes_accessed=1 << 20, transcendentals=0),
    )(*[hold(i, x) for i, x in enumerate(ins)])


def start(source, target, sem):
    copy = pltpu.make_async_copy(source, target, sem)
    copy.start()
    return copy


class Plan:
    def __init__(self, sp, hd, length, channels):
        self.sp, self.hd, self.count = sp, hd, sp * hd
        self.length, self.channels = length, channels
        self.start = [length * i // channels for i in range(self.count)]
        need = max(
            -(-(length * i % channels + length) // channels) for i in range(self.count)
        )
        self.rows = -(-need // 32) * 32
        self.packed = self.rows * channels // LANES
        self.part_a = -(-self.packed // 32) * 16
        self.part_b = self.packed - self.part_a
        self.table = -(-(self.start[-1] + self.rows) // 8) * 8
        self.nz, self.nx = max(sp // 2, 1), min(sp, 2)
        self.ny, self.nk = max(hd // 2, 1), min(hd, 2)
        self.group_z = ("sp", sp, self.nx, self.nz)
        self.group_x = ("sp", sp, 1, self.nx)
        self.group_y = ("hd", hd, self.nk, self.ny)
        self.group_k = ("hd", hd, 1, self.nk)
        self.half = self.count // self.nk

    def place(self, owner, me):
        off = owner ^ me
        off_sp, off_hd = off // self.hd, off % self.hd
        z, x = off_sp // self.nx, off_sp % self.nx
        y, k = off_hd // self.nk, off_hd % self.nk
        return k, (y * self.nx + x) * self.nz + z, (x * self.ny + y) * self.nz + z


def swap(value, group, step):
    axis, count, stride, _ = group
    return lax.ppermute(value, axis, [(i, i ^ (step * stride)) for i in range(count)])


def spread(block, group):
    return jnp.concatenate([block] + [swap(block, group, e) for e in range(1, group[3])], axis=0)


def collect(total, group):
    size = total.shape[0] // group[3]
    out = total[:size]
    for e in range(1, group[3]):
        out = out + swap(total[e * size : (e + 1) * size].astype(BF), group, e).astype(F32)
    return out


def pack_rows(table):
    rows = table.shape[0]
    tail = table[:, 2 * LANES :]
    tail = jnp.concatenate([tail[: rows // 2], tail[rows // 2 :]], axis=1)
    return jnp.concatenate([table[:, :LANES], table[:, LANES : 2 * LANES], tail], axis=0)


def unpack_rows(packed, rows):
    tail = packed[2 * rows :]
    half = tail.shape[1] // 2
    tail = jnp.concatenate([tail[:, :half], tail[:, half:]], axis=0)
    return jnp.concatenate([packed[:rows], packed[rows : 2 * rows], tail], axis=1)


def gather_parameters(plan, master, edges, prepare):
    me = lax.axis_index("sp") * plan.hd + lax.axis_index("hd")
    shift = lax.rem(me * plan.length, plan.channels)
    flat = jnp.zeros((plan.rows * plan.channels,), F32)
    flat = lax.dynamic_update_slice(flat, master, (shift,))
    packed = pack_rows(flat.reshape(plan.rows, plan.channels).astype(BF))[None]
    packed = spread(packed, plan.group_z)
    packed, edges = lax.optimization_barrier((packed, edges()))
    part_a, part_b = packed[:, : plan.part_a], packed[:, plan.part_a :]
    part_a, part_b = spread(part_a, plan.group_x), spread(part_b, plan.group_y)
    part_a, part_b = spread(part_a, plan.group_y), spread(part_b, plan.group_x)
    part_a, part_b, ready = lax.optimization_barrier((part_a, part_b, prepare(*edges)))
    if plan.nk == 1:
        return (part_a, part_a, part_b, part_b), ready
    other_a, other_b = swap(part_a, plan.group_k, 1), swap(part_b, plan.group_k, 1)
    return (part_a, other_a, part_b, other_b), ready


def scatter_gradient(plan, keep, send):
    total = keep
    if plan.nk > 1:
        total = keep + swap(send, plan.group_k, 1).astype(F32)
    part_a, part_b = total[:, : plan.part_a], total[:, plan.part_a :]
    for group_a, group_b in (
        (plan.group_y, plan.group_x),
        (plan.group_x, plan.group_y),
    ):
        part_a, part_b = collect(part_a, group_a), collect(part_b, group_b)
    packed = collect(jnp.concatenate([part_a, part_b], axis=1), plan.group_z)[0]
    flat = unpack_rows(packed, plan.rows).reshape(-1)
    me = lax.axis_index("sp") * plan.hd + lax.axis_index("hd")
    shift = lax.rem(me * plan.length, plan.channels)
    return lax.dynamic_slice(flat, (shift,), (plan.length,))


def three_columns(values, cols):
    tokens = values.shape[0]
    col = lax.broadcasted_iota(jnp.int32, values.shape, 0) % cols
    left = jnp.where(col == 0, 0.0, pltpu.roll(values, 1, 0))
    right = jnp.where(col == cols - 1, 0.0, pltpu.roll(values, tokens - 1, 0))
    return jnp.concatenate([left, values, right], axis=1).astype(BF)


def lane_pick(row, lane):
    ids = lax.broadcasted_iota(jnp.int32, row.shape, 1)
    return jnp.sum(jnp.where(ids == lane, row, 0.0))


def lane_row(pairs):
    ids = lax.broadcasted_iota(jnp.int32, (1, LANES), 1)
    row = jnp.zeros((1, LANES), F32)
    for lane, value in pairs:
        row = jnp.where(ids == lane, value, row)
    return row


def prepare_kernel(cols, cond, low, high, context, wk_t, wv_t, c3, k_t, v_t):
    images = cond.shape[0]
    channels, words = wk_t.shape[0], context.shape[1]
    pad = jnp.zeros((channels, LANES - words), F32)
    for i in range(images):
        wide = jnp.concatenate([low[i], cond[i], high[i]], axis=0).astype(F32)
        c3[i] = three_columns(wide, cols)
        for weight, out in ((wk_t, k_t), (wv_t, v_t)):
            part = mm_nt(weight[...], context[i])
            out[i] = jnp.concatenate([part, pad], axis=1).astype(BF)


def unpack_table(plan, me, own_a, other_a, own_b, other_b, table):
    rows, split = plan.rows, plan.part_a
    for i in range(plan.count):
        k, at_a, at_b = plan.place(i, me)
        own = jnp.full((1, 1), k, jnp.int32) == 0
        a = jnp.where(own, own_a[at_a].astype(F32), other_a[at_a].astype(F32))
        b = jnp.where(own, own_b[at_b].astype(F32), other_b[at_b].astype(F32))
        begin = plan.start[i]
        old = table[begin : begin + 1, :] if i > 0 else None
        table[begin : begin + rows, :LANES] = a[:rows]
        table[begin : begin + rows, LANES : 2 * LANES] = jnp.concatenate(
            [a[rows:], b[: 2 * rows - split]], axis=0
        )
        tail = b[2 * rows - split :]
        table[begin : begin + rows // 2, 2 * LANES :] = tail[:, : LANES // 2]
        table[begin + rows // 2 : begin + rows, 2 * LANES :] = tail[:, LANES // 2 :]
        if i > 0:
            table[begin : begin + 1, :] += old


def forward_kernel(
    plan, cols, place, snr, own_a, other_a, own_b, other_b, c3_far,
    weights_far, trailing, feature_far, relu_far, x3_far, payload,
    table, weights, c3, feature, relu_low, x3, sems,
):
    me, first, last = place[0], place[1], place[2]
    images, wide, kept_in = c3.shape
    load = [start(c3_far.at[i], c3.at[i], sems.at[i]) for i in range(images)]
    unpack_table(plan, me, own_a, other_a, own_b, other_b, table)
    count = weights.shape[0]
    weights[...] = table[:count].astype(BF)
    stores = [start(weights, weights_far, sems.at[images])]
    trailing[...] = jnp.concatenate(
        [table[count : count + 4], jnp.zeros((4, table.shape[1]), F32)], axis=0
    )
    channels = table.shape[1]
    tokens = wide - 4 * cols
    kept = 3 * channels
    base_one = 3 * kept_in
    base_two = base_one + 3 * kept
    b_in, b_one, b_two = trailing[0:1], trailing[1:2], trailing[2:3]
    square = jnp.zeros((1, 1), F32)
    for i in range(images):
        more = tokens + 2 * cols
        load[i].wait()
        a_one = b_in + sum(
            mm(c3[i, dy * cols : dy * cols + more], weights[dy * kept_in : (dy + 1) * kept_in])
            for dy in range(3)
        )
        row = lax.broadcasted_iota(jnp.int32, a_one.shape, 0) // cols
        outside = ((row == 0) & (first == 1)) | ((row == tokens // cols + 1) & (last == 1))
        a_low = jnp.where(outside, 0.0, a_one).astype(BF).astype(F32)
        x3[i] = three_columns(a_low, cols)
        stores.append(start(x3.at[i], x3_far.at[i], sems.at[images + 1 + 3 * i]))
        pre_relu = b_one + sum(
            mm(
                x3[i, dy * cols : dy * cols + tokens],
                weights[base_one + dy * kept : base_one + (dy + 1) * kept],
            )
            for dy in range(3)
        )
        relu = jnp.maximum(pre_relu, 0.0).astype(BF)
        relu_low[i] = relu
        stores.append(start(relu_low.at[i], relu_far.at[i], sems.at[images + 2 + 3 * i]))
        out = mm(relu, weights[base_two : base_two + channels]) + b_two
        out = out + a_one[cols : cols + tokens]
        feature[i] = out
        stores.append(start(feature.at[i], feature_far.at[i], sems.at[images + 3 + 3 * i]))
        square = square + jnp.sum(out * out)
    total = snr[0]
    for i in range(1, images):
        total = total + snr[i]
    line = lane_row([(0, square), (1, total)])
    payload[...] = jnp.broadcast_to(line[None], payload.shape)
    for copy in stores:
        copy.wait()


def turn_kernel(taps_from, weights_far, w1t_far, weights, w1t, sems):
    size, channels = weights.shape
    start(weights_far.at[taps_from : taps_from + size], weights, sems.at[0]).wait()
    for row in range(9):
        tap = weights[(8 - row) * channels : (9 - row) * channels].astype(F32)
        w1t[row * channels : (row + 1) * channels] = tap.T.astype(BF)
    start(w1t, w1t_far, sems.at[1]).wait()


def norm_of(line, elements):
    return lax.rsqrt(jnp.full((1, 1), lane_pick(line, 0) / elements + EPS_NORM, F32))


def by_head(left, right, turned):
    span = 2 * LANES
    cut = right.shape[1] - span
    if right.shape[0] != span + LANES // 2 or cut != 6 * LANES:
        return mm_nt(left, right) if turned else mm(left, right)
    if not turned:
        most = mm(left[:, :span], right[:span, :cut])
        return jnp.concatenate([most, mm(left[:, LANES:], right[LANES:, cut:])], axis=1)
    most = mm_nt(left[:, :cut], right[:span, :cut])
    rest = mm_nt(left[:, cut:], right[LANES:, cut:])
    return jnp.concatenate(
        [most[:, :LANES], most[:, LANES:] + rest[:, :LANES], rest[:, LANES:]], axis=1
    )


def attention_kernel(
    plan, sizes, snr, sums, trailing, noise_t, k_t, v_t, wp_t, feature_far, resid_far, wq_far, wo_far,
    g_far, u_out, payload, feature, resid, wq, wo, g_out, kbd, vbd, sems,
):
    elements, loss_count, words = sizes
    images, tokens, channels = feature.shape
    heads = kbd.shape[2] // LANES
    loads = [start(wq_far, wq, sems.at[0]), start(wo_far, wo, sems.at[1])]
    for i in range(images):
        loads.append(start(feature_far.at[i], feature.at[i], sems.at[2 + 3 * i]))
        loads.append(start(resid_far.at[i], resid.at[i], sems.at[3 + 3 * i]))
    line = jnp.sum(sums[...], axis=0)
    scale = norm_of(line, elements)
    denom = lane_pick(line, 1) / plan.sp * loss_count
    inject = trailing[3:4]
    root = HDIM ** (-0.5)
    for i in range(images):
        for source, wide in ((k_t, kbd), (v_t, vbd)):
            row_head = lax.broadcasted_iota(jnp.int32, source.shape[1:], 0) // HDIM
            value = source[i].astype(F32)
            for h in range(heads):
                part = jnp.where(row_head == h, value, 0.0).astype(BF)
                wide[i, :, h * LANES : (h + 1) * LANES] = part
    out_chan, width = noise_t.shape[2:]
    spare = jnp.zeros((16 - out_chan, channels), F32)
    wide_pred = jnp.concatenate([wp_t[...].astype(F32), spare], axis=0).astype(BF)
    loss = jnp.zeros((1, 1), F32)
    u = jnp.zeros((1, channels), F32)
    known = lax.broadcasted_iota(jnp.int32, (tokens, LANES), 1) < words
    stores = []
    for i in range(images):
        for copy in loads[:2] * (i == 0) + loads[2 + 2 * i : 4 + 2 * i]:
            copy.wait()
        value = feature[i]
        injected = resid[i].astype(F32) + inject * (value * scale)
        query = mm(injected.astype(BF), wq[...]).astype(BF)
        scores = by_head(query, kbd[i], False) * root
        attn = []
        for h in range(heads):
            part = jnp.where(known, scores[:, h * LANES : (h + 1) * LANES], -1e30)
            part = jnp.exp(part - jnp.max(part, axis=1, keepdims=True))
            attn.append(part / jnp.sum(part, axis=1, keepdims=True))
        low = jnp.concatenate([a.astype(BF) for a in attn], axis=1)
        mixed = by_head(low, vbd[i], True).astype(BF)
        after = injected + mm(mixed, wo[...])
        pred = mm_nt(wide_pred, after.astype(BF))
        noise = jnp.concatenate([noise_t[i, r] for r in range(tokens // width)], axis=1)
        noise = jnp.concatenate([noise, jnp.zeros((16 - out_chan, tokens), F32)], axis=0)
        error = pred - noise
        loss = loss + snr[i] * jnp.sum(error * error)
        g_pred = (2.0 * snr[i] / denom) * error
        g_y = mm_tn(g_pred.astype(BF), wide_pred)
        g_mixed = mm_nt(g_y.astype(BF), wo[...]).astype(BF)
        g_attn = by_head(g_mixed, vbd[i], False)
        g_scores = []
        for h in range(heads):
            part = g_attn[:, h * LANES : (h + 1) * LANES]
            inner = jnp.sum(attn[h] * part, axis=1, keepdims=True)
            g_scores.append((attn[h] * (part - inner)).astype(BF))
        g_query = (by_head(jnp.concatenate(g_scores, axis=1), kbd[i], True) * root).astype(BF)
        g_x = g_y + mm_nt(g_query, wq[...])
        g_out[i] = g_x
        stores.append(start(g_out.at[i], g_far.at[i], sems.at[4 + 3 * i]))
        u = u + jnp.sum(g_x * value, axis=0, keepdims=True)
    u_out[...] = jnp.broadcast_to(u, u_out.shape)
    cross = jnp.sum(inject * u)
    payload[...] = jnp.broadcast_to(lane_row([(0, loss / denom), (1, cross)])[None], payload.shape)
    for copy in stores:
        copy.wait()


def solve_kernel(
    cols, elements, sums, sums_two, trailing, g_far, feature_far, relu_far, weights_far,
    loss, g_f, gz, edge_top, edge_bottom, g_x, feature, relu, w_two, sems,
):
    images, tokens, channels = gz.shape
    base_two = weights_far.shape[0] - channels
    loads = [start(weights_far.at[base_two : base_two + channels], w_two, sems.at[0])]
    for i in range(images):
        for j, (far, near) in enumerate(((g_far, g_x), (feature_far, feature), (relu_far, relu))):
            loads.append(start(far.at[i], near.at[i], sems.at[1 + 3 * i + j]))
    scale = norm_of(jnp.sum(sums[...], axis=0), elements)
    line = jnp.sum(sums_two[...], axis=0)
    loss[...] = jnp.full(loss.shape, lane_pick(line, 0), F32)
    pull = scale * scale * scale * (lane_pick(line, 1) / elements)
    inject = trailing[3:4]
    for i in range(images):
        for copy in loads[:1] * (i == 0) + loads[1 + 3 * i : 4 + 3 * i]:
            copy.wait()
        value = scale * (inject * g_x[i]) - feature[i] * pull
        g_f[i] = value
        back = mm_nt(value.astype(BF), w_two[...])
        back = jnp.where(relu[i].astype(F32) > 0, back, 0.0).astype(BF)
        gz[i] = back
        edge_top[i] = back[:cols]
        edge_bottom[i] = back[tokens - cols :]


def block_weight_kernel(
    cols, elements, sums, u, gz, g_f, relu_far, x3_far, d_block, d_rows, relu, x3, sems
):
    images, tokens, channels = gz.shape
    kept = 3 * channels
    loads = []
    for i in range(images):
        loads.append(start(relu_far.at[i], relu.at[i], sems.at[2 * i]))
        loads.append(start(x3_far.at[i], x3.at[i], sems.at[2 * i + 1]))
    scale = norm_of(jnp.sum(sums[...], axis=0), elements)
    rows = [jnp.zeros((1, channels), F32), jnp.zeros((1, channels), F32)]
    for i in range(images):
        for copy in loads[2 * i : 2 * i + 2]:
            copy.wait()
        back, low = gz[i], g_f[i].astype(BF)
        spans = [
            (x3[i, dy * cols : dy * cols + tokens], back, dy * kept, kept) for dy in range(3)
        ] + [(relu[i], low, 3 * kept, channels)]
        for left, right, at, size in spans:
            part = mm_tn(left, right)
            d_block[at : at + size] = part if i == 0 else d_block[at : at + size] + part
        rows[0] = rows[0] + jnp.sum(back.astype(F32), axis=0, keepdims=True)
        rows[1] = rows[1] + jnp.sum(low.astype(F32), axis=0, keepdims=True)
    d_rows[...] = jnp.concatenate(rows + [scale * u[0:1], jnp.zeros((5, channels), F32)], axis=0)


def pack_table(plan, me, table, keep, send):
    rows, split = plan.rows, plan.part_a
    for i in range(plan.count):
        k, at_a, at_b = plan.place(i, me)
        begin = plan.start[i]
        one = table[begin : begin + rows, :LANES]
        two = table[begin : begin + rows, LANES : 2 * LANES]
        tail = jnp.concatenate(
            [
                table[begin : begin + rows // 2, 2 * LANES :],
                table[begin + rows // 2 : begin + rows, 2 * LANES :],
            ],
            axis=1,
        )
        a = jnp.concatenate([one, two[: split - rows]], axis=0)
        b = jnp.concatenate([two[split - rows :], tail], axis=0)

        @pl.when(k == 0)
        def _():
            keep[at_a, :split] = a
            keep[at_b, split:] = b

        @pl.when(k != 0)
        def _():
            send[at_a, :split] = a.astype(BF)
            send[at_b, split:] = b.astype(BF)


def input_kernel(
    plan, cols, place, gz, above, below, g_f, d_block, d_rows, w1t_far, c3_far,
    keep, send, table, w1t, c3, sems,
):
    me = place[0]
    images, tokens, channels = gz.shape
    kept, kept_in = 3 * channels, c3.shape[2]
    load = start(w1t_far, w1t, sems.at[0])
    late = start(c3_far, c3, sems.at[1])
    n_in, n_block = 3 * kept_in, d_block.shape[0]
    table[n_in : n_in + n_block] = d_block[...]
    wide = []
    for i in range(images):
        part = jnp.concatenate([above[i], gz[i], below[i]], axis=0).astype(F32)
        wide.append(three_columns(part, cols))
    load.wait()
    db_in = jnp.zeros((1, channels), F32)
    for i in range(images):
        total = g_f[i] + sum(
            mm(wide[i][dy * cols : dy * cols + tokens], w1t[dy * kept : (dy + 1) * kept])
            for dy in range(3)
        )
        low = total.astype(BF)
        db_in = db_in + jnp.sum(low.astype(F32), axis=0, keepdims=True)
        if i == 0:
            late.wait()
        for dy in range(3):
            at = slice(dy * kept_in, (dy + 1) * kept_in)
            part = mm_tn(c3[i, (1 + dy) * cols : (1 + dy) * cols + tokens], low)
            table[at] = part if i == 0 else table[at] + part
    at = n_in + n_block
    table[at : at + 8] = jnp.concatenate(
        [db_in, d_rows[0:3], jnp.zeros((4, channels), F32)], axis=0
    )
    pack_table(plan, me, table, keep, send)


def snr_weights(timesteps):
    beta_sched = np.linspace(0.00085**0.5, 0.012**0.5, 1000, dtype=np.float64) ** 2
    alpha_bar = np.cumprod(1.0 - beta_sched)
    snr_value = alpha_bar / (1.0 - alpha_bar)
    lookup = jnp.asarray(np.minimum(snr_value, SNR_CAP) / snr_value, F32)
    hit_table = timesteps[:, None] == jnp.arange(1000, dtype=jnp.int32)[None, :]
    return jnp.sum(jnp.where(hit_table, lookup[None, :], 0.0), axis=1)


def shift_rows(value, step):
    count = lax.axis_size("sp")
    pairs = [(i, i + step) for i in range(count) if 0 <= i + step < count]
    return lax.ppermute(value, "sp", pairs)


def everywhere(payload):
    return lax.all_to_all(payload, ("sp", "hd"), 0, 0, tiled=True)


def body(
    cond, resid, context, noise, timesteps, step, query_weight, key_weight, value_weight,
    out_weight, pred_weight, master, first_moment, second_moment,
):
    images, row_count, cols, in_chan = cond.shape
    channels = resid.shape[-1]
    out_chan = noise.shape[-1]
    words = context.shape[2]
    tokens = row_count * cols
    all_tokens = images * tokens
    sp, hd = lax.axis_size("sp"), lax.axis_size("hd")
    plan = Plan(sp, hd, master.shape[0], channels)
    height = row_count * sp
    elements = images * hd * height * cols * channels
    heads = channels // HDIM
    n_in, n_one, n_two = 9 * in_chan, 9 * channels, channels
    at_sp = lax.axis_index("sp")
    place = jnp.stack(
        [
            at_sp * hd + lax.axis_index("hd"),
            (at_sp == 0).astype(jnp.int32),
            (at_sp == sp - 1).astype(jnp.int32),
        ]
    )
    snr = snr_weights(timesteps.reshape(-1))
    wide, kept, kept_in = tokens + 2 * cols, 3 * channels, 3 * in_chan

    def edges():
        low = shift_rows(cond[:, row_count - 2 :], 1).reshape(images, 2 * cols, in_chan)
        high = shift_rows(cond[:, :2], -1).reshape(images, 2 * cols, in_chan)
        return low, high

    def prepare(low, high):
        return call(
            functools.partial(prepare_kernel, cols),
            [
                ((images, wide + 2 * cols, kept_in), BF),
                ((images, channels, LANES), BF),
                ((images, channels, LANES), BF),
            ],
            [
                cond.reshape(images, tokens, in_chan), low, high,
                context.reshape(images, words, -1), key_weight.T, value_weight.T,
            ],
            free=(0, 3, 4, 5),
            flops=4 << 30,
        )

    gathered, (c3, k_t, v_t) = gather_parameters(plan, master, edges, prepare)
    line = ((plan.count, 1, LANES), F32)
    per_image = (images, tokens, channels)
    weights, trailing, feature, relu_low, x3, payload = call(
        functools.partial(forward_kernel, plan, cols),
        [
            ((n_in + n_one + n_two, channels), BF),
            ((8, channels), F32),
            (per_image, F32),
            (per_image, BF),
            ((images, wide, kept), BF),
            line,
        ],
        [place, snr, *gathered, c3],
        scratch=[
            VMEM((plan.table, channels), F32),
            VMEM((n_in + n_one + n_two, channels), BF),
            VMEM((images, wide + 2 * cols, kept_in), BF),
            VMEM(per_image, F32),
            VMEM(per_image, BF),
            VMEM((images, wide, kept), BF),
            DMA((1 + 4 * images,)),
        ],
        smem=(0, 1),
        far=(6,),
        far_out=(0, 2, 3, 4),
        flops=4 << 30,
    )
    sums = everywhere(payload)
    (w1t,) = call(
        functools.partial(turn_kernel, n_in),
        [((n_one, channels), BF)],
        [weights],
        scratch=[VMEM((n_one, channels), BF), VMEM((n_one, channels), BF), DMA((2,))],
        far=(0,),
        far_out=(0,),
        flops=2 << 30,
    )
    g_x, u, payload = call(
        functools.partial(
            attention_kernel, plan, (elements, height * cols * out_chan, words)
        ),
        [(per_image, F32), ((8, channels), F32), line],
        [
            snr, sums, trailing, jnp.transpose(noise, (0, 1, 3, 2)), k_t, v_t, pred_weight.T,
            feature, resid.reshape(per_image), query_weight, out_weight,
        ],
        scratch=[
            VMEM(per_image, F32),
            VMEM(per_image, BF),
            VMEM((channels, channels), BF),
            VMEM((channels, channels), BF),
            VMEM(per_image, F32),
            VMEM((images, channels, heads * LANES), BF),
            VMEM((images, channels, heads * LANES), BF),
            DMA((2 + 3 * images,)),
        ],
        smem=(0,),
        far=(7, 8, 9, 10),
        far_out=(0,),
        flops=4 << 30,
    )
    sums_two = everywhere(payload)
    loss, g_f, gz, edge_top, edge_bottom = call(
        functools.partial(solve_kernel, cols, elements),
        [
            ((8, LANES), F32),
            (per_image, F32),
            (per_image, BF),
            ((images, cols, channels), BF),
            ((images, cols, channels), BF),
        ],
        [sums, sums_two, trailing, g_x, feature, relu_low, weights],
        scratch=[
            VMEM(per_image, F32),
            VMEM(per_image, F32),
            VMEM(per_image, BF),
            VMEM((channels, channels), BF),
            DMA((1 + 3 * images,)),
        ],
        far=(3, 4, 5, 6),
        flops=1 << 29,
    )
    above = shift_rows(edge_bottom, 1)
    below = shift_rows(edge_top, -1)
    d_block, d_rows = call(
        functools.partial(block_weight_kernel, cols, elements),
        [((n_one + n_two, channels), F32), ((8, channels), F32)],
        [sums, u, gz, g_f, relu_low, x3],
        scratch=[VMEM(per_image, BF), VMEM((images, wide, kept), BF), DMA((2 * images,))],
        far=(4, 5),
        flops=2 << 30,
    )
    keep, send = call(
        functools.partial(input_kernel, plan, cols),
        [
            ((plan.half, plan.packed, LANES), F32),
            ((plan.half, plan.packed, LANES), BF),
        ],
        [place, gz, above, below, g_f, d_block, d_rows, w1t, c3],
        scratch=[
            VMEM((plan.table, channels), F32),
            VMEM((n_one, channels), BF),
            VMEM((images, wide + 2 * cols, kept_in), BF),
            DMA((2,)),
        ],
        smem=(0,),
        far=(7, 8),
        flops=4 << 30,
    )
    grad_share = scatter_gradient(plan, keep, send)
    steps_done = step[0].astype(F32)
    first_new = BETA_ONE * first_moment + (1.0 - BETA_ONE) * grad_share
    second_new = BETA_TWO * second_moment + (1.0 - BETA_TWO) * grad_share * grad_share
    first_hat = first_new / (1.0 - BETA_ONE**steps_done)
    second_hat = second_new / (1.0 - BETA_TWO**steps_done)
    new_master = master - RATE * (first_hat / (jnp.sqrt(second_hat) + EPS_ADAM) + DECAY * master)
    return (loss[0, 0], new_master, first_new, second_new)


def solution(mesh):
    shard = P(("sp", "hd"))
    placed = (
        P("hd", "sp", None, None),
        P("hd", "sp", None, None),
        P("hd", None, None, None),
        P("hd", "sp", None, None),
        P("hd", None),
        P(),
        P(),
        P(),
        P(),
        P(),
        P(),
        shard,
        shard,
        shard,
    )
    return jax.shard_map(
        body,
        mesh=mesh,
        in_specs=placed,
        out_specs=(P(), shard, shard, shard),
        check_vma=False,
    )
```

profile of v0, /device:TPU:0, one launch (start us, length us, event | category | flops | bytes accessed | tf_op | source)
XLA Modules:
  0.0 148.6 jit_solution(8174323934169574211)
XLA Ops:
  0.7 2.4 %dynamic_update_slice.3 = bf16[51200]{0:T(1024)(128)(2,1)S(1)} dynamic-update-slice(bf16[51200]{0:T(1024)(128)(2,1)S(1)} %broadcast_in_dim.22, f32[49320]{0:T(1024)} %param.26, s32[]{:T(128)S(6)} %select_n.9) | dynamic-update-slice | bytes 394564 | tf_op jit(solution)/shard_map/dynamic_update_slice | solution.py:129
  3.4 5.1 %collective-permute-start.2 = (bf16[1,400,128]{2,1,0:T(8,128)(2,1)S(1)}, bf16[1,400,128]{2,1,0:T(8,128)(2,1)S(1)}, u32[]{:S(2)}, u32[]{:S(2)}) collective-permute-start(bf16[1,400,128]{2,1,0:T(8,128)(2,1)S(1)} %maximum_bitcast_fusion), channel_id=1, source_target_pairs={{0,24},{4,28},{8,16},{12,20},{16,8},{20,12},{24,0},{28,4},{1,25},{... | collective-permute-start | bytes 307208 | tf_op jit(solution)/shard_map/ppermute | solution.py:96
  8.5 0.6 collective-permute-start
  9.1 1.0 fusion.9
  10.1 1.3 collective-permute-start.4
  11.4 4.6 %collective-permute-start.3 = (bf16[2,2,64,192]{3,2,1,0:T(8,128)(2,1)S(1)}, bf16[2,2,64,192]{3,2,1,0:T(8,128)(2,1)S(1)}, u32[]{:S(2)}, u32[]{:S(2)}) collective-permute-start(bf16[2,2,64,192]{3,2,1,0:T(8,128)(2,1)S(1)} %get-tuple-element.68), channel_id=1, source_target_pairs={{0,4},{4,8},{8,12},{12,16},{16,20},{20,24},{24,28},{1,5},{5,9},{9,... | collective-permute-start | bytes 294920 | tf_op jit(solution)/shard_map/ppermute | solution.py:500
  16.0 2.1 %collective-permute-done.1 = bf16[1,400,128]{2,1,0:T(8,128)(2,1)S(1)} collective-permute-done((bf16[1,400,128]{2,1,0:T(8,128)(2,1)S(1)}, bf16[1,400,128]{2,1,0:T(8,128)(2,1)S(1)}, u32[]{:S(2)}, u32[]{:S(2)}) %collective-permute-start.1) | collective-permute-done | bytes 102432 | tf_op jit(solution)/shard_map/ppermute | solution.py:96
  18.1 1.9 %collective-permute-done.3 = bf16[2,2,64,192]{3,2,1,0:T(8,128)(2,1)S(1)} collective-permute-done((bf16[2,2,64,192]{3,2,1,0:T(8,128)(2,1)S(1)}, bf16[2,2,64,192]{3,2,1,0:T(8,128)(2,1)S(1)}, u32[]{:S(2)}, u32[]{:S(2)}) %collective-permute-start.3) | collective-permute-done | bytes 98336 | tf_op jit(solution)/shard_map/ppermute | solution.py:500
  20.0 1.6 %collective-permute-start.7 = (bf16[4,192,128]{2,1,0:T(8,128)(2,1)S(1)}, bf16[4,192,128]{2,1,0:T(8,128)(2,1)S(1)}, u32[]{:S(2)}, u32[]{:S(2)}) collective-permute-start(bf16[4,192,128]{2,1,0:T(8,128)(2,1)S(1)} %slice.110), channel_id=1, source_target_pairs={{0,2},{1,3},{2,0},{3,1},{4,6},{5,7},{6,4},{7,5},{8,10},{9,11},{10,... | collective-permute-start | bytes 589832 | tf_op jit(solution)/shard_map/ppermute | solution.py:96
  21.6 2.5 %collective-permute-start.5 = (bf16[4,208,128]{2,1,0:T(8,128)(2,1)S(1)}, bf16[4,208,128]{2,1,0:T(8,128)(2,1)S(1)}, u32[]{:S(2)}, u32[]{:S(2)}) collective-permute-start(bf16[4,208,128]{2,1,0:T(8,128)(2,1)S(1)} %slice.109), channel_id=1, source_target_pairs={{0,4},{4,0},{8,12},{12,8},{16,20},{20,16},{24,28},{28,24},{1,5},{5... | collective-permute-start | bytes 638984 | tf_op jit(solution)/shard_map/ppermute | solution.py:96
  24.2 1.6 %collective-permute-done.7 = bf16[4,192,128]{2,1,0:T(8,128)(2,1)S(1)} collective-permute-done((bf16[4,192,128]{2,1,0:T(8,128)(2,1)S(1)}, bf16[4,192,128]{2,1,0:T(8,128)(2,1)S(1)}, u32[]{:S(2)}, u32[]{:S(2)}) %collective-permute-start.7) | collective-permute-done | bytes 196640 | tf_op jit(solution)/shard_map/ppermute | solution.py:96
  25.8 2.6 %collective-permute-start.8 = (bf16[8,192,128]{2,1,0:T(8,128)(2,1)S(1)}, bf16[8,192,128]{2,1,0:T(8,128)(2,1)S(1)}, u32[]{:S(2)}, u32[]{:S(2)}) collective-permute-start(bf16[8,192,128]{2,1,0:T(8,128)(2,1)S(1)} %pad_maximum_fusion.5), channel_id=1, source_target_pairs={{0,4},{4,0},{8,12},{12,8},{16,20},{20,16},{24,28},{28,24},{1,5},{5... | collective-permute-start | bytes 1179656 | tf_op jit(solution)/shard_map/ppermute | solution.py:96
  28.4 0.8 collective-permute-done.5
  29.3 0.7 collective-permute-start.6
  30.0 0.9 shard_map.174
  31.0 5.6 %collective-permute-done.8 = bf16[8,192,128]{2,1,0:T(8,128)(2,1)S(1)} collective-permute-done((bf16[8,192,128]{2,1,0:T(8,128)(2,1)S(1)}, bf16[8,192,128]{2,1,0:T(8,128)(2,1)S(1)}, u32[]{:S(2)}, u32[]{:S(2)}) %collective-permute-start.8) | collective-permute-done | bytes 393248 | tf_op jit(solution)/shard_map/ppermute | solution.py:96
  36.7 1.2 collective-permute-done.6
  38.1 0.5 collective-permute-start.10
  38.9 2.7 %collective-permute-done.10.other_b = bf16[16,192,128]{2,1,0:T(8,128)(2,1)S(1)} collective-permute-done((bf16[16,192,128]{2,1,0:T(8,128)(2,1)S(1)}, bf16[16,192,128]{2,1,0:T(8,128)(2,1)S(1)}, u32[]{:S(2)}, u32[]{:S(2)}) %collective-permute-start.10) | collective-permute-done | bytes 786464 | tf_op jit(solution)/shard_map/ppermute | solution.py:96
  41.6 12.8 %shard_map.175 = (bf16[4928,320]{1,0:T(8,128)(2,1)}, f32[8,320]{1,0:T(8,128)S(1)}, f32[2,512,320]{2,1,0:T(8,128)}, bf16[2,512,320]{2,1,0:T(8,128)(2,1)}, bf16[2,...) custom-call(s32[3]{0:T(128)S(1)} %pad_add_fusion.place, f32[2]{0:T(128)S(1)} %fusion.6.snr, ...), custom_call_target="tpu_custom_call" | custom-call | flops 4294967296 | bytes 1048576 | tf_op jit(solution)/shard_map/pallas_call | solution.py:46
  54.3 11.9 %all_to_all.10.sums = f32[32,1,128]{2,1,0:T(1,128)S(1)} all-to-all(f32[32,1,128]{2,1,0:T(1,128)S(1)} %get-tuple-element.42), channel_id=1, replica_groups=mesh['sp'=8,'hd'=4] {'sp','hd'}, dimensions={0} | all-to-all | bytes 32768 | tf_op jit(solution)/shard_map/all_to_all | solution.py:504
  66.3 11.4 %shard_map.176 = (f32[2,512,320]{2,1,0:T(8,128)}, f32[8,320]{1,0:T(8,128)S(1)}, f32[32,1,128]{2,1,0:T(1,128)}) custom-call(f32[2]{0:T(128)S(1)} %fusion.6.snr, f32[32,1,128]{2,1,0:T(1,128)S(1)} %all_to_all.10.sums, f32[8,320]{1,0:T(8,128)S(1)} %get-tuple-element.43.trailing, f32[2,8,4,64]{3,2,1,0:T(4,128)S(1)} %bitcast.31, ...), custom_call_target="tpu_custom_call" | custom-call | flops 4294967296 | bytes 1048576 | tf_op jit(solution)/shard_map/pallas_call | solution.py:46
  77.7 2.6 %all-to-all-start.1 = ((f32[32,1,128]{2,1,0:T(1,128)}), f32[32,1,128]{2,1,0:T(1,128)S(1)}, u32[]{:S(2)}, u32[]{:S(2)}) async-start(f32[32,1,128]{2,1,0:T(1,128)} %get-tuple-element.47), calls=%async_computation.1 | async-start | bytes 32768 | tf_op jit(solution)/shard_map/all_to_all | solution.py:504
  80.3 3.8 %shard_map.179.w1t_far = bf16[2880,320]{1,0:T(8,128)(2,1)} custom-call(bf16[4928,320]{1,0:T(8,128)(2,1)} %get-tuple-element.50.weights_far), custom_call_target="tpu_custom_call" | custom-call | flops 2147483648 | bytes 1048576 | tf_op jit(solution)/shard_map/pallas_call | solution.py:46
  84.1 3.3 %all-to-all-done.1.sums_two = f32[32,1,128]{2,1,0:T(1,128)S(1)} async-done(((f32[32,1,128]{2,1,0:T(1,128)}), f32[32,1,128]{2,1,0:T(1,128)S(1)}, u32[]{:S(2)}, u32[]{:S(2)}) %all-to-all-start.1) | async-done | bytes 16416 | tf_op jit(solution)/shard_map/all_to_all | solution.py:504
  87.3 2.8 %shard_map.177 = (f32[8,128]{1,0:T(8,128)S(1)}, f32[2,512,320]{2,1,0:T(8,128)S(1)}, bf16[2,512,320]{2,1,0:T(8,128)(2,1)S(1)}, bf16[2,64,320]{2,1,0:T(8,128)(2,1)S(1)}, bf16[2,64,320]{2,1,0:T(8,128)(2,1)S(1)}) custom-call(f32[32,1,128]{2,1,0:T(1,128)S(1)} %all_to_all.10.sums, f32[32,1,128]{2,1,0:T(1,128)S(1)} %all-to-all-done.1.sums_two, ...), custom_call_target="tpu_custom_call" | custom-call | flops 536870912 | bytes 1048576 | tf_op jit(solution)/shard_map/pallas_call | solution.py:46
  90.1 2.5 %collective-permute-start.11 = (bf16[2,64,320]{2,1,0:T(8,128)(2,1)S(1)}, bf16[2,64,320]{2,1,0:T(8,128)(2,1)S(1)}, u32[]{:S(2)}, u32[]{:S(2)}) collective-permute-start(bf16[2,64,320]{2,1,0:T(8,128)(2,1)S(1)} %get-tuple-element.53), channel_id=1, source_target_pairs={{0,4},{4,8},{8,12},{12,16},{16,20},{20,24},{24,28},{1,5},{5,9},{9,... | collective-permute-start | bytes 245768 | tf_op jit(solution)/shard_map/ppermute | solution.py:500
  92.6 1.5 %collective-permute-start.12 = (bf16[2,64,320]{2,1,0:T(8,128)(2,1)S(1)}, bf16[2,64,320]{2,1,0:T(8,128)(2,1)S(1)}, u32[]{:S(2)}, u32[]{:S(2)}) collective-permute-start(bf16[2,64,320]{2,1,0:T(8,128)(2,1)S(1)} %get-tuple-element.54), channel_id=1, source_target_pairs={{4,0},{8,4},{12,8},{16,12},{20,16},{24,20},{28,24},{5,1},{9,5},{13... | collective-permute-start | bytes 245768 | tf_op jit(solution)/shard_map/ppermute | solution.py:500
  94.1 5.3 %shard_map.178 = (f32[3200,320]{1,0:T(8,128)S(1)}, f32[8,320]{1,0:T(8,128)S(1)}) custom-call(f32[32,1,128]{2,1,0:T(1,128)S(1)} %all_to_all.10.sums, f32[8,320]{1,0:T(8,128)S(1)} %get-tuple-element.56.u, bf16[2,512,320]{2,1,0:T(8,128)(2,1)S(1)} %get-tuple-element.52.gz, f32[2,512,320]{2,1,0:T(8,128)S(1)} %get-tuple-element.55.g_f, ...), custom_call_target="tpu_custom_call" | custom-call | flops 2147483648 | bytes 1048576 | tf_op jit(solution)/shard_map/pallas_call | solution.py:46
  99.5 10.9 %shard_map.180 = (f32[16,400,128]{2,1,0:T(8,128)S(1)}, bf16[16,400,128]{2,1,0:T(8,128)(2,1)S(1)}) custom-call(s32[3]{0:T(128)S(1)} %pad_add_fusion.place, bf16[2,512,320]{2,1,0:T(8,128)(2,1)S(1)} %get-tuple-element.52.gz, bf16[2,64,320]{2,1,0:T(8,128)(2,1)S(1)} %collective-permute-done.11.above, bf16[2,64,320]{2,1,0:T(8,128)(2,1)S(1)} %collective-permute-done.12.below, ...), custom_call_target="tpu_custom_call" | custom-call | flops 4294967296 | bytes 1048576 | tf_op jit(solution)/shard_map/pallas_call | solution.py:46
  110.5 3.5 %collective-permute-done.13 = bf16[16,400,128]{2,1,0:T(8,128)(2,1)S(1)} collective-permute-done((bf16[16,400,128]{2,1,0:T(8,128)(2,1)S(1)}, bf16[16,400,128]{2,1,0:T(8,128)(2,1)S(1)}, u32[]{:S(2)}, u32[]{:S(2)}) %collective-permute-start.13) | collective-permute-done | bytes 1638432 | tf_op jit(solution)/shard_map/ppermute | solution.py:96
  114.0 0.5 fusion.8
  114.5 2.7 %collective-permute-start.16 = (bf16[8,192,128]{2,1,0:T(8,128)(2,1)S(1)}, bf16[8,192,128]{2,1,0:T(8,128)(2,1)S(1)}, u32[]{:S(2)}, u32[]{:S(2)}) collective-permute-start(bf16[8,192,128]{2,1,0:T(8,128)(2,1)S(1)} %slice.141), channel_id=1, source_target_pairs={{0,4},{4,0},{8,12},{12,8},{16,20},{20,16},{24,28},{28,24},{1,5},{5... | collective-permute-start | bytes 1179656 | tf_op jit(solution)/shard_map/ppermute | solution.py:96
  117.2 0.7 collective-permute-start.14
  117.9 8.7 %collective-permute-done.16 = bf16[8,192,128]{2,1,0:T(8,128)(2,1)S(1)} collective-permute-done((bf16[8,192,128]{2,1,0:T(8,128)(2,1)S(1)}, bf16[8,192,128]{2,1,0:T(8,128)(2,1)S(1)}, u32[]{:S(2)}, u32[]{:S(2)}) %collective-permute-start.16) | collective-permute-done | bytes 393248 | tf_op jit(solution)/shard_map/ppermute | solution.py:96
  126.7 0.7 collective-permute-start.17
  127.4 1.5 collective-permute-done.14
  129.0 0.4 collective-permute-start.15
  129.3 3.9 %collective-permute-done.17 = bf16[4,192,128]{2,1,0:T(8,128)(2,1)S(1)} collective-permute-done((bf16[4,192,128]{2,1,0:T(8,128)(2,1)S(1)}, bf16[4,192,128]{2,1,0:T(8,128)(2,1)S(1)}, u32[]{:S(2)}, u32[]{:S(2)}) %collective-permute-start.17) | collective-permute-done | bytes 196640 | tf_op jit(solution)/shard_map/ppermute | solution.py:96
  133.2 1.9 %collective-permute-done.15 = bf16[4,208,128]{2,1,0:T(8,128)(2,1)S(1)} collective-permute-done((bf16[4,208,128]{2,1,0:T(8,128)(2,1)S(1)}, bf16[4,208,128]{2,1,0:T(8,128)(2,1)S(1)}, u32[]{:S(2)}, u32[]{:S(2)}) %collective-permute-start.15) | collective-permute-done | bytes 213024 | tf_op jit(solution)/shard_map/ppermute | solution.py:96
  135.4 1.6 %collective-permute-start.18 = (bf16[1,400,128]{2,1,0:T(8,128)(2,1)S(1)}, bf16[1,400,128]{2,1,0:T(8,128)(2,1)S(1)}, u32[]{:S(2)}, u32[]{:S(2)}) collective-permute-start(bf16[1,400,128]{2,1,0:T(8,128)(2,1)S(1)} %get-tuple-element.69), channel_id=1, source_target_pairs={{0,8},{4,12},{8,0},{12,4},{16,24},{20,28},{24,16},{28,20},{1,9},{5... | collective-permute-start | bytes 307208 | tf_op jit(solution)/shard_map/ppermute | solution.py:96
  137.0 1.5 collective-permute-start.20
  138.4 0.5 collective-permute-start.19
  139.6 0.5 slice.111
  140.1 1.6 %collective-permute-done.18 = bf16[1,400,128]{2,1,0:T(8,128)(2,1)S(1)} collective-permute-done((bf16[1,400,128]{2,1,0:T(8,128)(2,1)S(1)}, bf16[1,400,128]{2,1,0:T(8,128)(2,1)S(1)}, u32[]{:S(2)}, u32[]{:S(2)}) %collective-permute-start.18) | collective-permute-done | bytes 102432 | tf_op jit(solution)/shard_map/ppermute | solution.py:96
  141.7 2.1 %collective-permute-done.20 = bf16[1,400,128]{2,1,0:T(8,128)(2,1)S(1)} collective-permute-done((bf16[1,400,128]{2,1,0:T(8,128)(2,1)S(1)}, bf16[1,400,128]{2,1,0:T(8,128)(2,1)S(1)}, u32[]{:S(2)}, u32[]{:S(2)}) %collective-permute-start.20) | collective-permute-done | bytes 102432 | tf_op jit(solution)/shard_map/ppermute | solution.py:96
  143.9 3.3 %collective-permute-done.19 = bf16[1,400,128]{2,1,0:T(8,128)(2,1)S(1)} collective-permute-done((bf16[1,400,128]{2,1,0:T(8,128)(2,1)S(1)}, bf16[1,400,128]{2,1,0:T(8,128)(2,1)S(1)}, u32[]{:S(2)}, u32[]{:S(2)}) %collective-permute-start.19) | collective-permute-done | bytes 102432 | tf_op jit(solution)/shard_map/ppermute | solution.py:96
  147.6 1.0 multiply_subtract_fusion
  (68 shorter events, 1.9 us)
Async XLA Ops:
  0.6 23.6 %copy-start.9 = (bf16[2,1,77,768]{3,0,2,1:T(2,128)(2,1)S(1)}, bf16[2,1,77,768]{3,0,2,1:T(2,128)(2,1)}, u32[]{:S(2)}) copy-start(bf16[2,1,77,768]{3,0,2,1:T(2,128)(2,1)} %param.17) | copy-start | bytes 709636
  0.7 29.3 %copy-start = (bf16[2,8,64,192]{3,2,1,0:T(8,128)(2,1)S(1)}, bf16[2,8,64,192]{3,2,1,0:T(8,128)(2,1)}, u32[]{:S(2)}) copy-start(bf16[2,8,64,192]{3,2,1,0:T(8,128)(2,1)} %param.15) | copy-start | bytes 1179652
  0.7 29.3 %copy-start.1 = (bf16[768,320]{0,1:T(8,128)(2,1)S(1)}, bf16[768,320]{0,1:T(8,128)(2,1)}, u32[]{:S(2)}) copy-start(bf16[768,320]{0,1:T(8,128)(2,1)} %param.22) | copy-start | bytes 1474564
  0.7 29.3 %copy-start.2 = (bf16[768,320]{0,1:T(8,128)(2,1)S(1)}, bf16[768,320]{0,1:T(8,128)(2,1)}, u32[]{:S(2)}) copy-start(bf16[768,320]{0,1:T(8,128)(2,1)} %param.23) | copy-start | bytes 1474564
  3.4 12.6 %collective-permute-start.2 = (bf16[1,400,128]{2,1,0:T(8,128)(2,1)S(1)}, bf16[1,400,128]{2,1,0:T(8,128)(2,1)S(1)}, u32[]{:S(2)}, u32[]{:S(2)}) collective-permute-start(bf16[1,400,128]{2,1,0:T(8,128)(2,1)S(1)} %maximum_bitcast_fusion), channel_id=1, source_target_pairs={{0,24},{4,28},{8,16},{12,20},{16,8},{20,12},{24,0},{28,4},{1,25},{... | collective-permute-start | bytes 307208 | tf_op jit(solution)/shard_map/ppermute | solution.py:96
  8.5 9.6 %collective-permute-start.1 = (bf16[1,400,128]{2,1,0:T(8,128)(2,1)S(1)}, bf16[1,400,128]{2,1,0:T(8,128)(2,1)S(1)}, u32[]{:S(2)}, u32[]{:S(2)}) collective-permute-start(bf16[1,400,128]{2,1,0:T(8,128)(2,1)S(1)} %maximum_bitcast_fusion), channel_id=1, source_target_pairs={{0,16},{4,20},{8,24},{12,28},{16,0},{20,4},{24,8},{28,12},{1,17},{... | collective-permute-start | bytes 307208 | tf_op jit(solution)/shard_map/ppermute | solution.py:96
  8.5 9.6 %collective-permute-start = (bf16[1,400,128]{2,1,0:T(8,128)(2,1)S(1)}, bf16[1,400,128]{2,1,0:T(8,128)(2,1)S(1)}, u32[]{:S(2)}, u32[]{:S(2)}) collective-permute-start(bf16[1,400,128]{2,1,0:T(8,128)(2,1)S(1)} %maximum_bitcast_fusion), channel_id=1, source_target_pairs={{0,8},{4,12},{8,0},{12,4},{16,24},{20,28},{24,16},{28,20},{1,9},{5... | collective-permute-start | bytes 307208 | tf_op jit(solution)/shard_map/ppermute | solution.py:96
  10.1 8.0 %collective-permute-start.4 = (bf16[2,2,64,192]{3,2,1,0:T(8,128)(2,1)S(1)}, bf16[2,2,64,192]{3,2,1,0:T(8,128)(2,1)S(1)}, u32[]{:S(2)}, u32[]{:S(2)}) collective-permute-start(bf16[2,2,64,192]{3,2,1,0:T(8,128)(2,1)S(1)} %get-tuple-element.67), channel_id=1, source_target_pairs={{4,0},{8,4},{12,8},{16,12},{20,16},{24,20},{28,24},{5,1},{9,5},{13... | collective-permute-start | bytes 294920 | tf_op jit(solution)/shard_map/ppermute | solution.py:500
  11.4 8.6 %collective-permute-start.3 = (bf16[2,2,64,192]{3,2,1,0:T(8,128)(2,1)S(1)}, bf16[2,2,64,192]{3,2,1,0:T(8,128)(2,1)S(1)}, u32[]{:S(2)}, u32[]{:S(2)}) collective-permute-start(bf16[2,2,64,192]{3,2,1,0:T(8,128)(2,1)S(1)} %get-tuple-element.68), channel_id=1, source_target_pairs={{0,4},{4,8},{8,12},{12,16},{16,20},{20,24},{24,28},{1,5},{5,9},{9,... | collective-permute-start | bytes 294920 | tf_op jit(solution)/shard_map/ppermute | solution.py:500
  20.0 5.7 %collective-permute-start.7 = (bf16[4,192,128]{2,1,0:T(8,128)(2,1)S(1)}, bf16[4,192,128]{2,1,0:T(8,128)(2,1)S(1)}, u32[]{:S(2)}, u32[]{:S(2)}) collective-permute-start(bf16[4,192,128]{2,1,0:T(8,128)(2,1)S(1)} %slice.110), channel_id=1, source_target_pairs={{0,2},{1,3},{2,0},{3,1},{4,6},{5,7},{6,4},{7,5},{8,10},{9,11},{10,... | collective-permute-start | bytes 589832 | tf_op jit(solution)/shard_map/ppermute | solution.py:96
  21.6 7.6 %collective-permute-start.5 = (bf16[4,208,128]{2,1,0:T(8,128)(2,1)S(1)}, bf16[4,208,128]{2,1,0:T(8,128)(2,1)S(1)}, u32[]{:S(2)}, u32[]{:S(2)}) collective-permute-start(bf16[4,208,128]{2,1,0:T(8,128)(2,1)S(1)} %slice.109), channel_id=1, source_target_pairs={{0,4},{4,0},{8,12},{12,8},{16,20},{20,16},{24,28},{28,24},{1,5},{5... | collective-permute-start | bytes 638984 | tf_op jit(solution)/shard_map/ppermute | solution.py:96
  25.8 10.8 %collective-permute-start.8 = (bf16[8,192,128]{2,1,0:T(8,128)(2,1)S(1)}, bf16[8,192,128]{2,1,0:T(8,128)(2,1)S(1)}, u32[]{:S(2)}, u32[]{:S(2)}) collective-permute-start(bf16[8,192,128]{2,1,0:T(8,128)(2,1)S(1)} %pad_maximum_fusion.5), channel_id=1, source_target_pairs={{0,4},{4,0},{8,12},{12,8},{16,20},{20,16},{24,28},{28,24},{1,5},{5... | collective-permute-start | bytes 1179656 | tf_op jit(solution)/shard_map/ppermute | solution.py:96
  29.3 8.6 %collective-permute-start.6 = (bf16[8,208,128]{2,1,0:T(8,128)(2,1)S(1)}, bf16[8,208,128]{2,1,0:T(8,128)(2,1)S(1)}, u32[]{:S(2)}, u32[]{:S(2)}) collective-permute-start(bf16[8,208,128]{2,1,0:T(8,128)(2,1)S(1)} %pad_maximum_fusion.3), channel_id=1, source_target_pairs={{0,2},{1,3},{2,0},{3,1},{4,6},{5,7},{6,4},{7,5},{8,10},{9,11},{10,... | collective-permute-start | bytes 1277960 | tf_op jit(solution)/shard_map/ppermute | solution.py:96
  30.9 7.1 %copy-start.5 = (bf16[2,768,576]{2,1,0:T(8,128)(2,1)}, bf16[2,768,576]{2,1,0:T(8,128)(2,1)S(1)}, u32[]{:S(2)}) copy-start(bf16[2,768,576]{2,1,0:T(8,128)(2,1)S(1)} %get-tuple-element.41.c3_far) | copy-start | bytes 5308420
  30.9 7.1 %copy-start.6 = (bf16[2,320,128]{2,1,0:T(8,128)(2,1)}, bf16[2,320,128]{2,1,0:T(8,128)(2,1)S(1)}, u32[]{:S(2)}) copy-start(bf16[2,320,128]{2,1,0:T(8,128)(2,1)S(1)} %get-tuple-element.45.v_t) | copy-start | bytes 491524
  30.9 7.7 %copy-start.12 = (f32[1000]{0:T(1024)S(1)}, f32[1000]{0:T(1024)}, u32[]{:S(2)}) copy-start(f32[1000]{0:T(1024)} %constant.40.clone) | copy-start | bytes 12004
  31.0 7.7 %copy-start.13 = (s32[2,1]{0,1:T(1,128)S(1)}, s32[2,1]{0,1:T(1,128)}, u32[]{:S(2)}) copy-start(s32[2,1]{0,1:T(1,128)} %param.19) | copy-start | bytes 28
  38.0 3.6 %collective-permute-start.9 = (bf16[16,208,128]{2,1,0:T(8,128)(2,1)S(1)}, bf16[16,208,128]{2,1,0:T(8,128)(2,1)S(1)}, u32[]{:S(2)}, u32[]{:S(2)}) collective-permute-start(bf16[16,208,128]{2,1,0:T(8,128)(2,1)S(1)} %pad_maximum_fusion.1.own_a), channel_id=1, source_target_pairs={{0,1},{1,0},{2,3},{3,2},{4,5},{5,4},{6,7},{7,6},{8,9},{9,8},{10,11... | collective-permute-start | bytes 2555912 | tf_op jit(solution)/shard_map/ppermute | solution.py:96
  38.1 3.5 %collective-permute-start.10 = (bf16[16,192,128]{2,1,0:T(8,128)(2,1)S(1)}, bf16[16,192,128]{2,1,0:T(8,128)(2,1)S(1)}, u32[]{:S(2)}, u32[]{:S(2)}) collective-permute-start(bf16[16,192,128]{2,1,0:T(8,128)(2,1)S(1)} %pad_maximum_fusion.2.own_b), channel_id=1, source_target_pairs={{0,1},{1,0},{2,3},{3,2},{4,5},{5,4},{6,7},{7,6},{8,9},{9,8},{10,11... | collective-permute-start | bytes 2359304 | tf_op jit(solution)/shard_map/ppermute | solution.py:96
  38.8 27.4 %copy-start.3 = (f32[2,8,64,4]{2,3,1,0:T(4,128)S(1)}, f32[2,8,64,4]{2,3,1,0:T(4,128)}, u32[]{:S(2)}) copy-start(f32[2,8,64,4]{2,3,1,0:T(4,128)} %param.18) | copy-start | bytes 49156
  38.8 27.4 %copy-start.4 = (bf16[320,4]{0,1:T(4,128)(2,1)S(1)}, bf16[320,4]{0,1:T(4,128)(2,1)}, u32[]{:S(2)}) copy-start(bf16[320,4]{0,1:T(4,128)(2,1)} %param.25) | copy-start | bytes 7684
  38.9 27.4 %copy-start.7 = (bf16[2,320,128]{2,1,0:T(8,128)(2,1)S(1)}, bf16[2,320,128]{2,1,0:T(8,128)(2,1)}, u32[]{:S(2)}) copy-start(bf16[2,320,128]{2,1,0:T(8,128)(2,1)} %copy-done.6) | copy-start | bytes 491524
  77.7 9.6 %all-to-all-start.1 = ((f32[32,1,128]{2,1,0:T(1,128)}), f32[32,1,128]{2,1,0:T(1,128)S(1)}, u32[]{:S(2)}, u32[]{:S(2)}) async-start(f32[32,1,128]{2,1,0:T(1,128)} %get-tuple-element.47), calls=%async_computation.1 | async-start | bytes 32768 | tf_op jit(solution)/shard_map/all_to_all | solution.py:504
  90.1 9.3 %collective-permute-start.11 = (bf16[2,64,320]{2,1,0:T(8,128)(2,1)S(1)}, bf16[2,64,320]{2,1,0:T(8,128)(2,1)S(1)}, u32[]{:S(2)}, u32[]{:S(2)}) collective-permute-start(bf16[2,64,320]{2,1,0:T(8,128)(2,1)S(1)} %get-tuple-element.53), channel_id=1, source_target_pairs={{0,4},{4,8},{8,12},{12,16},{16,20},{20,24},{24,28},{1,5},{5,9},{9,... | collective-permute-start | bytes 245768 | tf_op jit(solution)/shard_map/ppermute | solution.py:500
  92.6 6.9 %collective-permute-start.12 = (bf16[2,64,320]{2,1,0:T(8,128)(2,1)S(1)}, bf16[2,64,320]{2,1,0:T(8,128)(2,1)S(1)}, u32[]{:S(2)}, u32[]{:S(2)}) collective-permute-start(bf16[2,64,320]{2,1,0:T(8,128)(2,1)S(1)} %get-tuple-element.54), channel_id=1, source_target_pairs={{4,0},{8,4},{12,8},{16,12},{20,16},{24,20},{28,24},{5,1},{9,5},{13... | collective-permute-start | bytes 245768 | tf_op jit(solution)/shard_map/ppermute | solution.py:500
  110.4 3.6 %collective-permute-start.13 = (bf16[16,400,128]{2,1,0:T(8,128)(2,1)S(1)}, bf16[16,400,128]{2,1,0:T(8,128)(2,1)S(1)}, u32[]{:S(2)}, u32[]{:S(2)}) collective-permute-start(bf16[16,400,128]{2,1,0:T(8,128)(2,1)S(1)} %get-tuple-element.61), channel_id=1, source_target_pairs={{0,1},{1,0},{2,3},{3,2},{4,5},{5,4},{6,7},{7,6},{8,9},{9,8},{10,11... | collective-permute-start | bytes 4915208 | tf_op jit(solution)/shard_map/ppermute | solution.py:96
  114.5 12.1 %collective-permute-start.16 = (bf16[8,192,128]{2,1,0:T(8,128)(2,1)S(1)}, bf16[8,192,128]{2,1,0:T(8,128)(2,1)S(1)}, u32[]{:S(2)}, u32[]{:S(2)}) collective-permute-start(bf16[8,192,128]{2,1,0:T(8,128)(2,1)S(1)} %slice.141), channel_id=1, source_target_pairs={{0,4},{4,0},{8,12},{12,8},{16,20},{20,16},{24,28},{28,24},{1,5},{5... | collective-permute-start | bytes 1179656 | tf_op jit(solution)/shard_map/ppermute | solution.py:96
  117.2 11.6 %collective-permute-start.14 = (bf16[8,208,128]{2,1,0:T(8,128)(2,1)S(1)}, bf16[8,208,128]{2,1,0:T(8,128)(2,1)S(1)}, u32[]{:S(2)}, u32[]{:S(2)}) collective-permute-start(bf16[8,208,128]{2,1,0:T(8,128)(2,1)S(1)} %slice.137), channel_id=1, source_target_pairs={{0,2},{1,3},{2,0},{3,1},{4,6},{5,7},{6,4},{7,5},{8,10},{9,11},{10,... | collective-permute-start | bytes 1277960 | tf_op jit(solution)/shard_map/ppermute | solution.py:96
  126.7 6.5 %collective-permute-start.17 = (bf16[4,192,128]{2,1,0:T(8,128)(2,1)S(1)}, bf16[4,192,128]{2,1,0:T(8,128)(2,1)S(1)}, u32[]{:S(2)}, u32[]{:S(2)}) collective-permute-start(bf16[4,192,128]{2,1,0:T(8,128)(2,1)S(1)} %slice.176), channel_id=1, source_target_pairs={{0,2},{1,3},{2,0},{3,1},{4,6},{5,7},{6,4},{7,5},{8,10},{9,11},{10,... | collective-permute-start | bytes 589832 | tf_op jit(solution)/shard_map/ppermute | solution.py:96
  129.0 6.2 %collective-permute-start.15 = (bf16[4,208,128]{2,1,0:T(8,128)(2,1)S(1)}, bf16[4,208,128]{2,1,0:T(8,128)(2,1)S(1)}, u32[]{:S(2)}, u32[]{:S(2)}) collective-permute-start(bf16[4,208,128]{2,1,0:T(8,128)(2,1)S(1)} %slice.175), channel_id=1, source_target_pairs={{0,4},{4,0},{8,12},{12,8},{16,20},{20,16},{24,28},{28,24},{1,5},{5... | collective-permute-start | bytes 638984 | tf_op jit(solution)/shard_map/ppermute | solution.py:96
  135.2 12.3 %copy-start.8 = (f32[49320]{0:T(1024)S(1)}, f32[49320]{0:T(1024)}, u32[]{:S(2)}) copy-start(f32[49320]{0:T(1024)} %param.26) | copy-start | bytes 591844
  135.2 12.3 %copy-start.10 = (f32[49320]{0:T(1024)S(1)}, f32[49320]{0:T(1024)}, u32[]{:S(2)}) copy-start(f32[49320]{0:T(1024)} %param.28) | copy-start | bytes 591844
  135.2 12.3 %copy-start.11 = (f32[49320]{0:T(1024)S(1)}, f32[49320]{0:T(1024)}, u32[]{:S(2)}) copy-start(f32[49320]{0:T(1024)} %param.27) | copy-start | bytes 591844
  135.4 6.4 %collective-permute-start.18 = (bf16[1,400,128]{2,1,0:T(8,128)(2,1)S(1)}, bf16[1,400,128]{2,1,0:T(8,128)(2,1)S(1)}, u32[]{:S(2)}, u32[]{:S(2)}) collective-permute-start(bf16[1,400,128]{2,1,0:T(8,128)(2,1)S(1)} %get-tuple-element.69), channel_id=1, source_target_pairs={{0,8},{4,12},{8,0},{12,4},{16,24},{20,28},{24,16},{28,20},{1,9},{5... | collective-permute-start | bytes 307208 | tf_op jit(solution)/shard_map/ppermute | solution.py:96
  137.0 6.9 %collective-permute-start.20 = (bf16[1,400,128]{2,1,0:T(8,128)(2,1)S(1)}, bf16[1,400,128]{2,1,0:T(8,128)(2,1)S(1)}, u32[]{:S(2)}, u32[]{:S(2)}) collective-permute-start(bf16[1,400,128]{2,1,0:T(8,128)(2,1)S(1)} %get-tuple-element.70), channel_id=1, source_target_pairs={{0,24},{4,28},{8,16},{12,20},{16,8},{20,12},{24,0},{28,4},{1,25},{... | collective-permute-start | bytes 307208 | tf_op jit(solution)/shard_map/ppermute | solution.py:96
  138.4 8.7 %collective-permute-start.19 = (bf16[1,400,128]{2,1,0:T(8,128)(2,1)S(1)}, bf16[1,400,128]{2,1,0:T(8,128)(2,1)S(1)}, u32[]{:S(2)}, u32[]{:S(2)}) collective-permute-start(bf16[1,400,128]{2,1,0:T(8,128)(2,1)S(1)} %get-tuple-element.71), channel_id=1, source_target_pairs={{0,16},{4,20},{8,24},{12,28},{16,0},{20,4},{24,8},{28,12},{1,17},{... | collective-permute-start | bytes 307208 | tf_op jit(solution)/shard_map/ppermute | solution.py:96
where the time goes:
time: 149 us
  Pallas kernels  47.9 us (32%)
  waiting for transfers between devices  45.7 us (31%)
  starting transfers between devices  34.1 us (23%)
  blocking collectives  11.9 us (8%)
  local copies, waits for them, and re-layouts  4.6 us (3%)
  other arithmetic  2.51 us (2%)
  between operations  1.82 us (1%)
    pallas_call x7, Pallas kernels, call(): pl.pallas_call(kernel, out_shape=[(HBM if i in far_out else VMEM)(*o) for...  47.9 us
    ppermute x17, waiting for transfers between devices, swap(): lax.ppermute(value, axis, [(i, i ^ step * stride) for i in range(count)])  40.5 us
    ppermute x17, starting transfers between devices, swap(): lax.ppermute(value, axis, [(i, i ^ step * stride) for i in range(count)])  21.7 us
    all_to_all x1, blocking collectives, everywhere(): return lax.all_to_all(payload, ('sp', 'hd'), 0, 0, tiled=True)  11.9 us
    ppermute x4, starting transfers between devices, shift_rows(): return lax.ppermute(value, 'sp', pairs)  9.83 us
    all_to_all x1, waiting for transfers between devices, everywhere(): return lax.all_to_all(payload, ('sp', 'hd'), 0, 0, tiled=True)  3.27 us
  transfers between devices with their start and end apart: 22, of which 16 were waited for; matrix products, arithmetic and copies ran while one was open for 2% of the time, Pallas kernels for 7%

commit v1 on v0

--- a/solution.py
+++ b/solution.py
@@ -125,8 +125,9 @@
 def gather_parameters(plan, master, edges, prepare):
     me = lax.axis_index("sp") * plan.hd + lax.axis_index("hd")
     shift = lax.rem(me * plan.length, plan.channels)
-    flat = jnp.zeros((plan.rows * plan.channels,), F32)
-    flat = lax.dynamic_update_slice(flat, master, (shift,))
+    total = plan.rows * plan.channels
+    flat = jnp.pad(master, (plan.channels, total - plan.length))
+    flat = lax.dynamic_slice(flat, (plan.channels - shift,), (total,))
     packed = pack_rows(flat.reshape(plan.rows, plan.channels).astype(BF))[None]
     packed = spread(packed, plan.group_z)
     packed, edges = lax.optimization_barrier((packed, edges()))
@@ -141,9 +142,9 @@
 
 
 def scatter_gradient(plan, keep, send):
-    total = keep
+    total = keep[: plan.half].astype(F32)
     if plan.nk > 1:
-        total = keep + swap(send, plan.group_k, 1).astype(F32)
+        total = total + swap(send, plan.group_k, 1)[: plan.half].astype(F32)
     part_a, part_b = total[:, : plan.part_a], total[:, plan.part_a :]
     for group_a, group_b in (
         (plan.group_y, plan.group_x),
@@ -190,9 +191,9 @@
             out[i] = jnp.concatenate([part, pad], axis=1).astype(BF)
 
 
-def unpack_table(plan, me, own_a, other_a, own_b, other_b, table):
+def unpack_table(plan, me, own_a, other_a, own_b, other_b, table, owners):
     rows, split = plan.rows, plan.part_a
-    for i in range(plan.count):
+    for i in owners:
         k, at_a, at_b = plan.place(i, me)
         own = jnp.full((1, 1), k, jnp.int32) == 0
         a = jnp.where(own, own_a[at_a].astype(F32), other_a[at_a].astype(F32))
@@ -212,42 +213,53 @@
 
 def forward_kernel(
     plan, cols, place, snr, own_a, other_a, own_b, other_b, c3_far,
-    weights_far, trailing, feature_far, relu_far, x3_far, payload,
-    table, weights, c3, feature, relu_low, x3, sems,
+    w1t_far, w_two_far, trailing, feature_far, relu_far, x3_far, payload,
+    table, weights, w1t, c3, feature, relu_low, x3, sems,
 ):
     me, first, last = place[0], place[1], place[2]
     images, wide, kept_in = c3.shape
     load = [start(c3_far.at[i], c3.at[i], sems.at[i]) for i in range(images)]
-    unpack_table(plan, me, own_a, other_a, own_b, other_b, table)
-    count = weights.shape[0]
-    weights[...] = table[:count].astype(BF)
-    stores = [start(weights, weights_far, sems.at[images])]
-    trailing[...] = jnp.concatenate(
-        [table[count : count + 4], jnp.zeros((4, table.shape[1]), F32)], axis=0
-    )
-    channels = table.shape[1]
+    count, channels = weights.shape
     tokens = wide - 4 * cols
+    more = tokens + 2 * cols
     kept = 3 * channels
-    base_one = 3 * kept_in
-    base_two = base_one + 3 * kept
-    b_in, b_one, b_two = trailing[0:1], trailing[1:2], trailing[2:3]
-    square = jnp.zeros((1, 1), F32)
-    for i in range(images):
-        more = tokens + 2 * cols
-        load[i].wait()
-        a_one = b_in + sum(
+    n_in = 3 * kept_in
+    base_two = n_in + 3 * kept
+    blocks = (own_a, other_a, own_b, other_b, table)
+    early = [i for i in range(plan.count) if plan.start[i] < n_in]
+    unpack_table(plan, me, *blocks, early)
+    weights[:n_in] = table[:n_in].astype(BF)
+    for copy in load:
+        copy.wait()
+    a_one = [
+        sum(
             mm(c3[i, dy * cols : dy * cols + more], weights[dy * kept_in : (dy + 1) * kept_in])
             for dy in range(3)
         )
-        row = lax.broadcasted_iota(jnp.int32, a_one.shape, 0) // cols
-        outside = ((row == 0) & (first == 1)) | ((row == tokens // cols + 1) & (last == 1))
-        a_low = jnp.where(outside, 0.0, a_one).astype(BF).astype(F32)
+        for i in range(images)
+    ]
+    unpack_table(plan, me, *blocks, range(len(early), plan.count))
+    weights[n_in:] = table[n_in:count].astype(BF)
+    for row in range(9):
+        at = n_in + (8 - row) * channels
+        w1t[row * channels : (row + 1) * channels] = table[at : at + channels].T.astype(BF)
+    first_store = start(w1t, w1t_far, sems.at[1 + 4 * images])
+    stores = [first_store, start(weights.at[base_two : base_two + channels], w_two_far, sems.at[images])]
+    trailing[...] = jnp.concatenate([table[count : count + 4], jnp.zeros((4, channels), F32)], axis=0)
+    b_in, b_one, b_two = trailing[0:1], trailing[1:2], trailing[2:3]
+    square = jnp.zeros((1, 1), F32)
+    row = lax.broadcasted_iota(jnp.int32, (more, channels), 0) // cols
+    outside = ((row == 0) & (first == 1)) | ((row == tokens // cols + 1) & (last == 1))
+    for i in range(images):
+        a_one[i] = a_one[i] + b_in
+        a_low = jnp.where(outside, 0.0, a_one[i]).astype(BF).astype(F32)
         x3[i] = three_columns(a_low, cols)
         stores.append(start(x3.at[i], x3_far.at[i], sems.at[images + 1 + 3 * i]))
+    for i in range(images):
         pre_relu = b_one + sum(
             mm(
                 x3[i, dy * cols : dy * cols + tokens],
-                weights[base_one + dy * kept : base_one + (dy + 1) * kept],
+                weights[n_in + dy * kept : n_in + (dy + 1) * kept],
             )
             for dy in range(3)
         )
@@ -255,7 +267,7 @@
         relu_low[i] = relu
         stores.append(start(relu_low.at[i], relu_far.at[i], sems.at[images + 2 + 3 * i]))
         out = mm(relu, weights[base_two : base_two + channels]) + b_two
-        out = out + a_one[cols : cols + tokens]
+        out = out + a_one[i][cols : cols + tokens]
         feature[i] = out
         stores.append(start(feature.at[i], feature_far.at[i], sems.at[images + 3 + 3 * i]))
         square = square + jnp.sum(out * out)
@@ -266,15 +278,6 @@
     payload[...] = jnp.broadcast_to(line[None], payload.shape)
     for copy in stores:
         copy.wait()
-
-
-def turn_kernel(taps_from, weights_far, w1t_far, weights, w1t, sems):
-    size, channels = weights.shape
-    start(weights_far.at[taps_from : taps_from + size], weights, sems.at[0]).wait()
-    for row in range(9):
-        tap = weights[(8 - row) * channels : (9 - row) * channels].astype(F32)
-        w1t[row * channels : (row + 1) * channels] = tap.T.astype(BF)
-    start(w1t, w1t_far, sems.at[1]).wait()
 
 
 def norm_of(line, elements):
@@ -305,8 +308,8 @@
     heads = kbd.shape[2] // LANES
     loads = [start(wq_far, wq, sems.at[0]), start(wo_far, wo, sems.at[1])]
     for i in range(images):
-        loads.append(start(feature_far.at[i], feature.at[i], sems.at[2 + 3 * i]))
-        loads.append(start(resid_far.at[i], resid.at[i], sems.at[3 + 3 * i]))
+        loads.append(start(feature_far.at[i], feature.at[i], sems.at[2 + 2 * i]))
+        loads.append(start(resid_far.at[i], resid.at[i], sems.at[3 + 2 * i]))
     line = jnp.sum(sums[...], axis=0)
     scale = norm_of(line, elements)
     denom = lane_pick(line, 1) / plan.sp * loss_count
@@ -322,44 +325,52 @@
     out_chan, width = noise_t.shape[2:]
     spare = jnp.zeros((16 - out_chan, channels), F32)
     wide_pred = jnp.concatenate([wp_t[...].astype(F32), spare], axis=0).astype(BF)
-    loss = jnp.zeros((1, 1), F32)
-    u = jnp.zeros((1, channels), F32)
     known = lax.broadcasted_iota(jnp.int32, (tokens, LANES), 1) < words
-    stores = []
-    for i in range(images):
+    each = range(images)
+    injected, scores = [], []
+    for i in each:
         for copy in loads[:2] * (i == 0) + loads[2 + 2 * i : 4 + 2 * i]:
             copy.wait()
-        value = feature[i]
-        injected = resid[i].astype(F32) + inject * (value * scale)
-        query = mm(injected.astype(BF), wq[...]).astype(BF)
-        scores = by_head(query, kbd[i], False) * root
-        attn = []
+        injected.append(resid[i].astype(F32) + inject * (feature[i] * scale))
+        query = mm(injected[i].astype(BF), wq[...]).astype(BF)
+        scores.append(by_head(query, kbd[i], False))
+    attn = []
+    for i in each:
+        attn.append([])
         for h in range(heads):
-            part = jnp.where(known, scores[:, h * LANES : (h + 1) * LANES], -1e30)
+            part = jnp.where(known, scores[i][:, h * LANES : (h + 1) * LANES] * root, -1e30)
             part = jnp.exp(part - jnp.max(part, axis=1, keepdims=True))
-            attn.append(part / jnp.sum(part, axis=1, keepdims=True))
-        low = jnp.concatenate([a.astype(BF) for a in attn], axis=1)
+            attn[i].append(part / jnp.sum(part, axis=1, keepdims=True))
+    loss = jnp.zeros((1, 1), F32)
+    g_y, g_attn = [], []
+    for i in each:
+        low = jnp.concatenate([part.astype(BF) for part in attn[i]], axis=1)
         mixed = by_head(low, vbd[i], True).astype(BF)
-        after = injected + mm(mixed, wo[...])
+        after = injected[i] + mm(mixed, wo[...])
         pred = mm_nt(wide_pred, after.astype(BF))
         noise = jnp.concatenate([noise_t[i, r] for r in range(tokens // width)], axis=1)
         noise = jnp.concatenate([noise, jnp.zeros((16 - out_chan, tokens), F32)], axis=0)
         error = pred - noise
         loss = loss + snr[i] * jnp.sum(error * error)
         g_pred = (2.0 * snr[i] / denom) * error
-        g_y = mm_tn(g_pred.astype(BF), wide_pred)
-        g_mixed = mm_nt(g_y.astype(BF), wo[...]).astype(BF)
-        g_attn = by_head(g_mixed, vbd[i], False)
-        g_scores = []
+        g_y.append(mm_tn(g_pred.astype(BF), wide_pred))
+        g_mixed = mm_nt(g_y[i].astype(BF), wo[...]).astype(BF)
+        g_attn.append(by_head(g_mixed, vbd[i], False))
+    g_scores = []
+    for i in each:
+        g_scores.append([])
         for h in range(heads):
-            part = g_attn[:, h * LANES : (h + 1) * LANES]
-            inner = jnp.sum(attn[h] * part, axis=1, keepdims=True)
-            g_scores.append((attn[h] * (part - inner)).astype(BF))
-        g_query = (by_head(jnp.concatenate(g_scores, axis=1), kbd[i], True) * root).astype(BF)
-        g_x = g_y + mm_nt(g_query, wq[...])
-        g_out[i] = g_x
-        stores.append(start(g_out.at[i], g_far.at[i], sems.at[4 + 3 * i]))
-        u = u + jnp.sum(g_x * value, axis=0, keepdims=True)
+            part = g_attn[i][:, h * LANES : (h + 1) * LANES]
+            inner = jnp.sum(attn[i][h] * part, axis=1, keepdims=True)
+            g_scores[i].append((attn[i][h] * (part - inner)).astype(BF))
+    u = jnp.zeros((1, channels), F32)
+    stores = []
+    for i in each:
+        g_query = by_head(jnp.concatenate(g_scores[i], axis=1), kbd[i], True) * root
+        g_x = g_y[i] + mm_nt(g_query.astype(BF), wq[...])
+        g_out[i] = scale * (inject * g_x)
+        stores.append(start(g_out.at[i], g_far.at[i], sems.at[2 + 2 * images + i]))
+        u = u + jnp.sum(g_x * feature[i], axis=0, keepdims=True)
     u_out[...] = jnp.broadcast_to(u, u_out.shape)
     cross = jnp.sum(inject * u)
     payload[...] = jnp.broadcast_to(lane_row([(0, loss / denom), (1, cross)])[None], payload.shape)
@@ -367,85 +378,88 @@
         copy.wait()
 
 
+def back_kernel(
+    g_far, feature_far, relu_far, w_two_far, by_g, by_feature, g, feature, relu, w_two, sems
+):
+    images, tokens, channels = by_g.shape
+    loads = [start(w_two_far, w_two, sems.at[0])]
+    pairs = ((feature_far, feature), (relu_far, relu), (g_far, g))
+    for j, (far, near) in enumerate(pairs):
+        loads.append(start(far, near, sems.at[1 + j]))
+    for copy in loads[:3]:
+        copy.wait()
+    for i in range(images):
+        back = mm_nt(feature[i].astype(BF), w_two[...])
+        by_feature[i] = jnp.where(relu[i].astype(F32) > 0, back, 0.0)
+    loads[3].wait()
+    for i in range(images):
+        back = mm_nt(g[i].astype(BF), w_two[...])
+        by_g[i] = jnp.where(relu[i].astype(F32) > 0, back, 0.0)
+
+
 def solve_kernel(
-    cols, elements, sums, sums_two, trailing, g_far, feature_far, relu_far, weights_far,
-    loss, g_f, gz, edge_top, edge_bottom, g_x, feature, relu, w_two, sems,
+    cols, elements, sums, sums_two, by_g, by_feature, scalars, gz, edge_top, edge_bottom
 ):
     images, tokens, channels = gz.shape
-    base_two = weights_far.shape[0] - channels
-    loads = [start(weights_far.at[base_two : base_two + channels], w_two, sems.at[0])]
-    for i in range(images):
-        for j, (far, near) in enumerate(((g_far, g_x), (feature_far, feature), (relu_far, relu))):
-            loads.append(start(far.at[i], near.at[i], sems.at[1 + 3 * i + j]))
     scale = norm_of(jnp.sum(sums[...], axis=0), elements)
     line = jnp.sum(sums_two[...], axis=0)
-    loss[...] = jnp.full(loss.shape, lane_pick(line, 0), F32)
     pull = scale * scale * scale * (lane_pick(line, 1) / elements)
-    inject = trailing[3:4]
-    for i in range(images):
-        for copy in loads[:1] * (i == 0) + loads[1 + 3 * i : 4 + 3 * i]:
-            copy.wait()
-        value = scale * (inject * g_x[i]) - feature[i] * pull
-        g_f[i] = value
-        back = mm_nt(value.astype(BF), w_two[...])
-        back = jnp.where(relu[i].astype(F32) > 0, back, 0.0).astype(BF)
+    pairs = [(0, jnp.full((1, 1), lane_pick(line, 0), F32)), (1, pull), (2, scale)]
+    scalars[...] = jnp.broadcast_to(lane_row(pairs), scalars.shape)
+    for i in range(images):
+        back = (by_g[i] - pull * by_feature[i]).astype(BF)
         gz[i] = back
         edge_top[i] = back[:cols]
         edge_bottom[i] = back[tokens - cols :]
 
 
 def block_weight_kernel(
-    cols, elements, sums, u, gz, g_f, relu_far, x3_far, d_block, d_rows, relu, x3, sems
+    cols, scalars, u, gz, x3_far, relu_far, g_far, feature_far,
+    d_block, d_rows, g_f, x3, relu, g, feature, sems,
 ):
     images, tokens, channels = gz.shape
     kept = 3 * channels
-    loads = []
-    for i in range(images):
-        loads.append(start(relu_far.at[i], relu.at[i], sems.at[2 * i]))
-        loads.append(start(x3_far.at[i], x3.at[i], sems.at[2 * i + 1]))
-    scale = norm_of(jnp.sum(sums[...], axis=0), elements)
+    loads = [start(x3_far.at[i], x3.at[i], sems.at[i]) for i in range(images)]
+    late = [
+        start(far, near, sems.at[images + j])
+        for j, (far, near) in enumerate(((relu_far, relu), (g_far, g), (feature_far, feature)))
+    ]
+    pull, scale = scalars[0:1, 1:2], scalars[0:1, 2:3]
     rows = [jnp.zeros((1, channels), F32), jnp.zeros((1, channels), F32)]
     for i in range(images):
-        for copy in loads[2 * i : 2 * i + 2]:
-            copy.wait()
-        back, low = gz[i], g_f[i].astype(BF)
-        spans = [
-            (x3[i, dy * cols : dy * cols + tokens], back, dy * kept, kept) for dy in range(3)
-        ] + [(relu[i], low, 3 * kept, channels)]
-        for left, right, at, size in spans:
-            part = mm_tn(left, right)
-            d_block[at : at + size] = part if i == 0 else d_block[at : at + size] + part
-        rows[0] = rows[0] + jnp.sum(back.astype(F32), axis=0, keepdims=True)
+        loads[i].wait()
+        for dy in range(3):
+            at = slice(dy * kept, (dy + 1) * kept)
+            part = mm_tn(x3[i, dy * cols : dy * cols + tokens], gz[i])
+            d_block[at] = part if i == 0 else d_block[at] + part
+        rows[0] = rows[0] + jnp.sum(gz[i].astype(F32), axis=0, keepdims=True)
+    for copy in late:
+        copy.wait()
+    at = slice(3 * kept, 3 * kept + channels)
+    for i in range(images):
+        g_f[i] = g[i] - pull * feature[i]
+        low = g_f[i].astype(BF)
+        part = mm_tn(relu[i], low)
+        d_block[at] = part if i == 0 else d_block[at] + part
         rows[1] = rows[1] + jnp.sum(low.astype(F32), axis=0, keepdims=True)
     d_rows[...] = jnp.concatenate(rows + [scale * u[0:1], jnp.zeros((5, channels), F32)], axis=0)
 
 
-def pack_table(plan, me, table, keep, send):
+def pack_rows_of(plan, me, i, table, begin, keep, send):
     rows, split = plan.rows, plan.part_a
-    for i in range(plan.count):
-        k, at_a, at_b = plan.place(i, me)
-        begin = plan.start[i]
-        one = table[begin : begin + rows, :LANES]
-        two = table[begin : begin + rows, LANES : 2 * LANES]
-        tail = jnp.concatenate(
-            [
-                table[begin : begin + rows // 2, 2 * LANES :],
-                table[begin + rows // 2 : begin + rows, 2 * LANES :],
-            ],
-            axis=1,
-        )
-        a = jnp.concatenate([one, two[: split - rows]], axis=0)
-        b = jnp.concatenate([two[split - rows :], tail], axis=0)
-
-        @pl.when(k == 0)
-        def _():
-            keep[at_a, :split] = a
-            keep[at_b, split:] = b
-
-        @pl.when(k != 0)
-        def _():
-            send[at_a, :split] = a.astype(BF)
-            send[at_b, split:] = b.astype(BF)
+    k, at_a, at_b = plan.place(i, me)
+    half = begin + rows // 2
+    one = table[begin : begin + rows, :LANES]
+    two = table[begin : begin + rows, LANES : 2 * LANES]
+    tail = jnp.concatenate(
+        [table[begin:half, 2 * LANES :], table[half : begin + rows, 2 * LANES :]], axis=1
+    )
+    a = jnp.concatenate([one, two[: split - rows]], axis=0).astype(BF)
+    b = jnp.concatenate([two[split - rows :], tail], axis=0).astype(BF)
+    for wanted, out in ((0, keep), (1, send)):
+        hit = k == wanted
+        out[jnp.where(hit, at_a, plan.half), :split] = a
+        out[jnp.where(hit, at_b, plan.half), split:] = b
 
 
 def input_kernel(
@@ -458,7 +472,18 @@
     load = start(w1t_far, w1t, sems.at[0])
     late = start(c3_far, c3, sems.at[1])
     n_in, n_block = 3 * kept_in, d_block.shape[0]
-    table[n_in : n_in + n_block] = d_block[...]
+    inner = [
+        i for i in range(plan.count)
+        if n_in <= plan.start[i] and plan.start[i] + plan.rows <= n_in + n_block
+    ]
+    outer = [i for i in range(plan.count) if i not in inner]
+    for i in inner:
+        pack_rows_of(plan, me, i, d_block, plan.start[i] - n_in, keep, send)
+    for i in outer:
+        low = max(plan.start[i], n_in) // 8 * 8
+        high = min(-(-(plan.start[i] + plan.rows) // 8) * 8, n_in + n_block)
+        if low < high:
+            table[low:high] = d_block[low - n_in : high - n_in]
     wide = []
     for i in range(images):
         part = jnp.concatenate([above[i], gz[i], below[i]], axis=0).astype(F32)
@@ -482,7 +507,8 @@
     table[at : at + 8] = jnp.concatenate(
         [db_in, d_rows[0:3], jnp.zeros((4, channels), F32)], axis=0
     )
-    pack_table(plan, me, table, keep, send)
+    for i in outer:
+        pack_rows_of(plan, me, i, table, plan.start[i], keep, send)
 
 
 def snr_weights(timesteps):
@@ -555,10 +581,11 @@
     gathered, (c3, k_t, v_t) = gather_parameters(plan, master, edges, prepare)
     line = ((plan.count, 1, LANES), F32)
     per_image = (images, tokens, channels)
-    weights, trailing, feature, relu_low, x3, payload = call(
+    w1t, w_two, trailing, feature, relu_low, x3, payload = call(
         functools.partial(forward_kernel, plan, cols),
         [
-            ((n_in + n_one + n_two, channels), BF),
+            ((n_one, channels), BF),
+            ((n_two, channels), BF),
             ((8, channels), F32),
             (per_image, F32),
             (per_image, BF),
@@ -569,28 +596,20 @@
         scratch=[
             VMEM((plan.table, channels), F32),
             VMEM((n_in + n_one + n_two, channels), BF),
+            VMEM((n_one, channels), BF),
             VMEM((images, wide + 2 * cols, kept_in), BF),
             VMEM(per_image, F32),
             VMEM(per_image, BF),
             VMEM((images, wide, kept), BF),
-            DMA((1 + 4 * images,)),
+            DMA((2 + 4 * images,)),
         ],
         smem=(0, 1),
         far=(6,),
-        far_out=(0, 2, 3, 4),
+        far_out=(0, 1, 3, 4, 5),
         flops=4 << 30,
     )
     sums = everywhere(payload)
-    (w1t,) = call(
-        functools.partial(turn_kernel, n_in),
-        [((n_one, channels), BF)],
-        [weights],
-        scratch=[VMEM((n_one, channels), BF), VMEM((n_one, channels), BF), DMA((2,))],
-        far=(0,),
-        far_out=(0,),
-        flops=2 << 30,
-    )
-    g_x, u, payload = call(
+    g, u, payload = call(
         functools.partial(
             attention_kernel, plan, (elements, height * cols * out_chan, words)
         ),
@@ -615,41 +634,52 @@
         flops=4 << 30,
     )
     sums_two = everywhere(payload)
-    loss, g_f, gz, edge_top, edge_bottom = call(
-        functools.partial(solve_kernel, cols, elements),
-        [
-            ((8, LANES), F32),
-            (per_image, F32),
-            (per_image, BF),
-            ((images, cols, channels), BF),
-            ((images, cols, channels), BF),
-        ],
-        [sums, sums_two, trailing, g_x, feature, relu_low, weights],
+    by_g, by_feature = call(
+        back_kernel,
+        [(per_image, F32), (per_image, F32)],
+        [g, feature, relu_low, w_two],
         scratch=[
             VMEM(per_image, F32),
             VMEM(per_image, F32),
             VMEM(per_image, BF),
             VMEM((channels, channels), BF),
-            DMA((1 + 3 * images,)),
-        ],
-        far=(3, 4, 5, 6),
+            DMA((4,)),
+        ],
+        far=(0, 1, 2, 3),
+        flops=4 << 30,
+    )
+    scalars, gz, edge_top, edge_bottom = call(
+        functools.partial(solve_kernel, cols, elements),
+        [
+            ((8, LANES), F32),
+            (per_image, BF),
+            ((images, cols, channels), BF),
+            ((images, cols, channels), BF),
+        ],
+        [sums, sums_two, by_g, by_feature],
         flops=1 << 29,
     )
     above = shift_rows(edge_bottom, 1)
     below = shift_rows(edge_top, -1)
-    d_block, d_rows = call(
-        functools.partial(block_weight_kernel, cols, elements),
-        [((n_one + n_two, channels), F32), ((8, channels), F32)],
-        [sums, u, gz, g_f, relu_low, x3],
-        scratch=[VMEM(per_image, BF), VMEM((images, wide, kept), BF), DMA((2 * images,))],
-        far=(4, 5),
+    d_block, d_rows, g_f = call(
+        functools.partial(block_weight_kernel, cols),
+        [((n_one + n_two, channels), F32), ((8, channels), F32), (per_image, F32)],
+        [scalars, u, gz, x3, relu_low, g, feature],
+        scratch=[
+            VMEM((images, wide, kept), BF),
+            VMEM(per_image, BF),
+            VMEM(per_image, F32),
+            VMEM(per_image, F32),
+            DMA((images + 3,)),
+        ],
+        far=(3, 4, 5, 6),
         flops=2 << 30,
     )
     keep, send = call(
         functools.partial(input_kernel, plan, cols),
         [
-            ((plan.half, plan.packed, LANES), F32),
-            ((plan.half, plan.packed, LANES), BF),
+            ((plan.half + 1, plan.packed, LANES), BF),
+            ((plan.half + 1, plan.packed, LANES), BF),
         ],
         [place, gz, above, below, g_f, d_block, d_rows, w1t, c3],
         scratch=[
@@ -669,7 +699,7 @@
     first_hat = first_new / (1.0 - BETA_ONE**steps_done)
     second_hat = second_new / (1.0 - BETA_TWO**steps_done)
     new_master = master - RATE * (first_hat / (jnp.sqrt(second_hat) + EPS_ADAM) + DECAY * master)
-    return (loss[0, 0], new_master, first_new, second_new)
+    return (scalars[0, 0], new_master, first_new, second_new)
 
 
 def solution(mesh):

time: 149 us -> 144 us (0.966)
  Pallas kernels: 47.9 us -> 41.6 us
  waiting for transfers between devices: 45.7 us -> 48.8 us
  starting transfers between devices: 34.1 us -> 31.6 us
  blocking collectives: 11.9 us -> 13.6 us
    pallas_call x7, Pallas kernels: 47.9 us -> 41.6 us  [call(): pl.pallas_call(kernel, out_shape=[(HBM if i in far_out else VMEM)(*o) for...]
    dynamic_update_slice x1 -> x0, local copies, waits for them, and re-layouts: 2.44 us -> none  [gather_parameters(): flat = lax.dynamic_update_slice(flat, master, (shift,))]
    all_to_all x1, blocking collectives: 11.9 us -> 13.6 us  [everywhere(): return lax.all_to_all(payload, ('sp', 'hd'), 0, 0, tiled=True)]
    ppermute x17, starting transfers between devices: 21.7 us -> 20 us  [swap(): lax.ppermute(value, axis, [(i, i ^ step * stride) for i in range(count)])]
    ppermute x4, waiting for transfers between devices: 1.92 us -> 3.44 us  [shift_rows(): return lax.ppermute(value, 'sp', pairs)]
  transfers between devices with their start and end apart: 22 -> 22, of which waited for: 16 -> 15; matrix products, arithmetic and copies ran while one was open for 2% -> 2% of each run, Pallas kernels for 7% -> 7%
where the time goes in v1:
time: 144 us; the launch traced here: 143 us
  waiting for transfers between devices  48.8 us (34%)
  Pallas kernels  41.6 us (29%)
  starting transfers between devices  31.6 us (22%)
  blocking collectives  13.6 us (9%)
  local copies, waits for them, and re-layouts  3.28 us (2%)
  other arithmetic  2.52 us (2%)
  between operations  1.81 us (1%)
    pallas_call x7, Pallas kernels, call(): pl.pallas_call(kernel, out_shape=[(HBM if i in far_out else VMEM)(*o) for...  41.6 us
    ppermute x17, waiting for transfers between devices, swap(): lax.ppermute(value, axis, [(i, i ^ step * stride) for i in range(count)])  41.4 us
    ppermute x17, starting transfers between devices, swap(): lax.ppermute(value, axis, [(i, i ^ step * stride) for i in range(count)])  20 us
    all_to_all x1, blocking collectives, everywhere(): return lax.all_to_all(payload, ('sp', 'hd'), 0, 0, tiled=True)  13.6 us
    ppermute x4, starting transfers between devices, shift_rows(): return lax.ppermute(value, 'sp', pairs)  9.03 us
    all_to_all x1, waiting for transfers between devices, everywhere(): return lax.all_to_all(payload, ('sp', 'hd'), 0, 0, tiled=True)  3.94 us
    ppermute x4, waiting for transfers between devices, shift_rows(): return lax.ppermute(value, 'sp', pairs)  3.44 us
  transfers between devices with their start and end apart: 22, of which 15 were waited for; matrix products, arithmetic and copies ran while one was open for 2% of the time, Pallas kernels for 7%

profile of v1, /device:TPU:0, one launch (start us, length us, event | category | flops | bytes accessed | tf_op | source)
XLA Modules:
  0.0 143.3 jit_solution(7860862428797610337)
XLA Ops:
  0.7 1.1 fusion.1
  2.0 3.0 %collective-permute-start = (bf16[1,400,128]{2,1,0:T(8,128)(2,1)S(1)}, bf16[1,400,128]{2,1,0:T(8,128)(2,1)S(1)}, u32[]{:S(2)}, u32[]{:S(2)}) collective-permute-start(bf16[1,400,128]{2,1,0:T(8,128)(2,1)S(1)} %maximum_bitcast_fusion), channel_id=1, source_target_pairs={{0,8},{4,12},{8,0},{12,4},{16,24},{20,28},{24,16},{28,20},{1,9},{5... | collective-permute-start | bytes 307208 | tf_op jit(solution)/shard_map/ppermute | solution.py:96
  5.1 2.6 %collective-permute-start.1 = (bf16[1,400,128]{2,1,0:T(8,128)(2,1)S(1)}, bf16[1,400,128]{2,1,0:T(8,128)(2,1)S(1)}, u32[]{:S(2)}, u32[]{:S(2)}) collective-permute-start(bf16[1,400,128]{2,1,0:T(8,128)(2,1)S(1)} %maximum_bitcast_fusion), channel_id=1, source_target_pairs={{0,16},{4,20},{8,24},{12,28},{16,0},{20,4},{24,8},{28,12},{1,17},{... | collective-permute-start | bytes 307208 | tf_op jit(solution)/shard_map/ppermute | solution.py:96
  7.7 1.0 fusion.10
  8.7 3.6 %collective-permute-start.3 = (bf16[2,2,64,192]{3,2,1,0:T(8,128)(2,1)S(1)}, bf16[2,2,64,192]{3,2,1,0:T(8,128)(2,1)S(1)}, u32[]{:S(2)}, u32[]{:S(2)}) collective-permute-start(bf16[2,2,64,192]{3,2,1,0:T(8,128)(2,1)S(1)} %get-tuple-element.74), channel_id=1, source_target_pairs={{0,4},{4,8},{8,12},{12,16},{16,20},{20,24},{24,28},{1,5},{5,9},{9,... | collective-permute-start | bytes 294920 | tf_op jit(solution)/shard_map/ppermute | solution.py:526
  12.3 1.4 collective-permute-start.4
  13.8 2.0 %collective-permute-done.1 = bf16[1,400,128]{2,1,0:T(8,128)(2,1)S(1)} collective-permute-done((bf16[1,400,128]{2,1,0:T(8,128)(2,1)S(1)}, bf16[1,400,128]{2,1,0:T(8,128)(2,1)S(1)}, u32[]{:S(2)}, u32[]{:S(2)}) %collective-permute-start.1) | collective-permute-done | bytes 102432 | tf_op jit(solution)/shard_map/ppermute | solution.py:96
  15.9 3.4 %collective-permute-done.4 = bf16[2,2,64,192]{3,2,1,0:T(8,128)(2,1)S(1)} collective-permute-done((bf16[2,2,64,192]{3,2,1,0:T(8,128)(2,1)S(1)}, bf16[2,2,64,192]{3,2,1,0:T(8,128)(2,1)S(1)}, u32[]{:S(2)}, u32[]{:S(2)}) %collective-permute-start.4) | collective-permute-done | bytes 98336 | tf_op jit(solution)/shard_map/ppermute | solution.py:526
  19.3 1.6 %collective-permute-start.7 = (bf16[4,192,128]{2,1,0:T(8,128)(2,1)S(1)}, bf16[4,192,128]{2,1,0:T(8,128)(2,1)S(1)}, u32[]{:S(2)}, u32[]{:S(2)}) collective-permute-start(bf16[4,192,128]{2,1,0:T(8,128)(2,1)S(1)} %slice.116), channel_id=1, source_target_pairs={{0,2},{1,3},{2,0},{3,1},{4,6},{5,7},{6,4},{7,5},{8,10},{9,11},{10,... | collective-permute-start | bytes 589832 | tf_op jit(solution)/shard_map/ppermute | solution.py:96
  20.9 1.6 %collective-permute-start.5 = (bf16[4,208,128]{2,1,0:T(8,128)(2,1)S(1)}, bf16[4,208,128]{2,1,0:T(8,128)(2,1)S(1)}, u32[]{:S(2)}, u32[]{:S(2)}) collective-permute-start(bf16[4,208,128]{2,1,0:T(8,128)(2,1)S(1)} %slice.115), channel_id=1, source_target_pairs={{0,4},{4,0},{8,12},{12,8},{16,20},{20,16},{24,28},{28,24},{1,5},{5... | collective-permute-start | bytes 638984 | tf_op jit(solution)/shard_map/ppermute | solution.py:96
  22.6 2.5 %collective-permute-done.7 = bf16[4,192,128]{2,1,0:T(8,128)(2,1)S(1)} collective-permute-done((bf16[4,192,128]{2,1,0:T(8,128)(2,1)S(1)}, bf16[4,192,128]{2,1,0:T(8,128)(2,1)S(1)}, u32[]{:S(2)}, u32[]{:S(2)}) %collective-permute-start.7) | collective-permute-done | bytes 196640 | tf_op jit(solution)/shard_map/ppermute | solution.py:96
  25.1 1.6 %collective-permute-start.8 = (bf16[8,192,128]{2,1,0:T(8,128)(2,1)S(1)}, bf16[8,192,128]{2,1,0:T(8,128)(2,1)S(1)}, u32[]{:S(2)}, u32[]{:S(2)}) collective-permute-start(bf16[8,192,128]{2,1,0:T(8,128)(2,1)S(1)} %pad_maximum_fusion.5), channel_id=1, source_target_pairs={{0,4},{4,0},{8,12},{12,8},{16,20},{20,16},{24,28},{28,24},{1,5},{5... | collective-permute-start | bytes 1179656 | tf_op jit(solution)/shard_map/ppermute | solution.py:96
  26.7 2.4 %collective-permute-done.5 = bf16[4,208,128]{2,1,0:T(8,128)(2,1)S(1)} collective-permute-done((bf16[4,208,128]{2,1,0:T(8,128)(2,1)S(1)}, bf16[4,208,128]{2,1,0:T(8,128)(2,1)S(1)}, u32[]{:S(2)}, u32[]{:S(2)}) %collective-permute-start.5) | collective-permute-done | bytes 213024 | tf_op jit(solution)/shard_map/ppermute | solution.py:96
  29.3 0.9 shard_map.174
  30.2 4.7 %collective-permute-done.8 = bf16[8,192,128]{2,1,0:T(8,128)(2,1)S(1)} collective-permute-done((bf16[8,192,128]{2,1,0:T(8,128)(2,1)S(1)}, bf16[8,192,128]{2,1,0:T(8,128)(2,1)S(1)}, u32[]{:S(2)}, u32[]{:S(2)}) %collective-permute-start.8) | collective-permute-done | bytes 393248 | tf_op jit(solution)/shard_map/ppermute | solution.py:96
  35.0 2.3 %collective-permute-done.6 = bf16[8,208,128]{2,1,0:T(8,128)(2,1)S(1)} collective-permute-done((bf16[8,208,128]{2,1,0:T(8,128)(2,1)S(1)}, bf16[8,208,128]{2,1,0:T(8,128)(2,1)S(1)}, u32[]{:S(2)}, u32[]{:S(2)}) %collective-permute-start.6) | collective-permute-done | bytes 426016 | tf_op jit(solution)/shard_map/ppermute | solution.py:96
  37.5 0.5 collective-permute-start.10
  38.1 0.2 fusion.7.snr
  38.3 2.8 %collective-permute-done.10.other_b = bf16[16,192,128]{2,1,0:T(8,128)(2,1)} collective-permute-done((bf16[16,192,128]{2,1,0:T(8,128)(2,1)S(1)}, bf16[16,192,128]{2,1,0:T(8,128)(2,1)}, u32[]{:S(2)}, u32[]{:S(2)}) %collective-permute-start.10) | collective-permute-done | bytes 786464 | tf_op jit(solution)/shard_map/ppermute | solution.py:96
  41.2 12.1 %shard_map.175 = (bf16[2880,320]{1,0:T(8,128)(2,1)}, bf16[320,320]{1,0:T(8,128)(2,1)}, f32[8,320]{1,0:T(8,128)S(1)}, f32[2,512,320]{2,1,0:T(8,128)}, bf16[2,512,...) custom-call(s32[3]{0:T(128)S(1)} %pad_add_fusion.place, f32[2]{0:T(128)S(1)} %fusion.7.snr, ...), custom_call_target="tpu_custom_call" | custom-call | flops 4294967296 | bytes 1048576 | tf_op jit(solution)/shard_map/pallas_call | solution.py:46
  53.3 13.6 %all_to_all.10.sums = f32[32,1,128]{2,1,0:T(1,128)S(1)} all-to-all(f32[32,1,128]{2,1,0:T(1,128)S(1)} %get-tuple-element.45), channel_id=1, replica_groups=mesh['sp'=8,'hd'=4] {'sp','hd'}, dimensions={0} | all-to-all | bytes 32768 | tf_op jit(solution)/shard_map/all_to_all | solution.py:530
  66.9 10.6 %shard_map.176 = (f32[2,512,320]{2,1,0:T(8,128)}, f32[8,320]{1,0:T(8,128)S(1)}, f32[32,1,128]{2,1,0:T(1,128)}) custom-call(f32[2]{0:T(128)S(1)} %fusion.7.snr, f32[32,1,128]{2,1,0:T(1,128)S(1)} %all_to_all.10.sums, f32[8,320]{1,0:T(8,128)S(1)} %get-tuple-element.46.trailing, f32[2,8,4,64]{3,2,1,0:T(4,128)S(1)} %bitcast.31, ...), custom_call_target="tpu_custom_call" | custom-call | flops 4294967296 | bytes 1048576 | tf_op jit(solution)/shard_map/pallas_call | solution.py:46
  77.5 2.6 %all-to-all-start.1 = ((f32[32,1,128]{2,1,0:T(1,128)}), f32[32,1,128]{2,1,0:T(1,128)S(1)}, u32[]{:S(2)}, u32[]{:S(2)}) async-start(f32[32,1,128]{2,1,0:T(1,128)} %get-tuple-element.50), calls=%async_computation.1 | async-start | bytes 32768 | tf_op jit(solution)/shard_map/all_to_all | solution.py:530
  80.1 3.1 %shard_map.177 = (f32[2,512,320]{2,1,0:T(8,128)S(1)}, f32[2,512,320]{2,1,0:T(8,128)S(1)}) custom-call(f32[2,512,320]{2,1,0:T(8,128)} %get-tuple-element.51.g_far, f32[2,512,320]{2,1,0:T(8,128)} %get-tuple-element.49.feature_far, bf16[2,512,320]{2,1,0:T(8,128)(2,1)} %get-tuple-element.52.relu_far, bf16[320,320]{1,0:T(8,128)(2,1)} %get-tuple-element.53.w_two_far), custom_call_target="tpu_custom_call" | custom-call | flops 4294967296 | bytes 1048576 | tf_op jit(solution)/shard_map/pallas_call | solution.py:46
  83.2 3.9 %all-to-all-done.1.sums_two = f32[32,1,128]{2,1,0:T(1,128)S(1)} async-done(((f32[32,1,128]{2,1,0:T(1,128)}), f32[32,1,128]{2,1,0:T(1,128)S(1)}, u32[]{:S(2)}, u32[]{:S(2)}) %all-to-all-start.1) | async-done | bytes 16416 | tf_op jit(solution)/shard_map/all_to_all | solution.py:530
  87.2 0.5 shard_map.178
  87.6 2.5 %collective-permute-start.11 = (bf16[2,64,320]{2,1,0:T(8,128)(2,1)S(1)}, bf16[2,64,320]{2,1,0:T(8,128)(2,1)S(1)}, u32[]{:S(2)}, u32[]{:S(2)}) collective-permute-start(bf16[2,64,320]{2,1,0:T(8,128)(2,1)S(1)} %get-tuple-element.58), channel_id=1, source_target_pairs={{0,4},{4,8},{8,12},{12,16},{16,20},{20,24},{24,28},{1,5},{5,9},{9,... | collective-permute-start | bytes 245768 | tf_op jit(solution)/shard_map/ppermute | solution.py:526
  90.1 1.5 %collective-permute-start.12 = (bf16[2,64,320]{2,1,0:T(8,128)(2,1)S(1)}, bf16[2,64,320]{2,1,0:T(8,128)(2,1)S(1)}, u32[]{:S(2)}, u32[]{:S(2)}) collective-permute-start(bf16[2,64,320]{2,1,0:T(8,128)(2,1)S(1)} %get-tuple-element.59), channel_id=1, source_target_pairs={{4,0},{8,4},{12,8},{16,12},{20,16},{24,20},{28,24},{5,1},{9,5},{13... | collective-permute-start | bytes 245768 | tf_op jit(solution)/shard_map/ppermute | solution.py:526
  91.6 5.6 %shard_map.179 = (f32[3200,320]{1,0:T(8,128)S(1)}, f32[8,320]{1,0:T(8,128)S(1)}, f32[2,512,320]{2,1,0:T(8,128)S(1)}) custom-call(f32[8,128]{1,0:T(8,128)S(1)} %get-tuple-element.56.scalars, f32[8,320]{1,0:T(8,128)S(1)} %get-tuple-element.60.u, bf16[2,512,320]{2,1,0:T(8,128)(2,1)S(1)} %get-tuple-element.57.gz, bf16[2,640,960]{2,1,0:T(8,128)(2,1)} %get-tuple-element.61.x3_far, ...), custom_call_target="tpu_custom_call" | custom-call | flops 2147483648 | bytes 1048576 | tf_op jit(solution)/shard_map/pallas_call | solution.py:46
  97.3 8.7 %shard_map.180 = (bf16[17,400,128]{2,1,0:T(8,128)(2,1)S(1)}, bf16[17,400,128]{2,1,0:T(8,128)(2,1)S(1)}) custom-call(s32[3]{0:T(128)S(1)} %pad_add_fusion.place, bf16[2,512,320]{2,1,0:T(8,128)(2,1)S(1)} %get-tuple-element.57.gz, bf16[2,64,320]{2,1,0:T(8,128)(2,1)S(1)} %collective-permute-done.11.above, bf16[2,64,320]{2,1,0:T(8,128)(2,1)S(1)} %collective-permute-done.12.below, ...), custom_call_target="tpu_custom_call" | custom-call | flops 4294967296 | bytes 1048576 | tf_op jit(solution)/shard_map/pallas_call | solution.py:46
  106.1 3.6 %collective-permute-done.13 = bf16[17,400,128]{2,1,0:T(8,128)(2,1)S(1)} collective-permute-done((bf16[17,400,128]{2,1,0:T(8,128)(2,1)S(1)}, bf16[17,400,128]{2,1,0:T(8,128)(2,1)S(1)}, u32[]{:S(2)}, u32[]{:S(2)}) %collective-permute-start.13) | collective-permute-done | bytes 1740832 | tf_op jit(solution)/shard_map/ppermute | solution.py:96
  109.8 0.5 fusion.8
  110.3 2.7 %collective-permute-start.16 = (bf16[8,192,128]{2,1,0:T(8,128)(2,1)S(1)}, bf16[8,192,128]{2,1,0:T(8,128)(2,1)S(1)}, u32[]{:S(2)}, u32[]{:S(2)}) collective-permute-start(bf16[8,192,128]{2,1,0:T(8,128)(2,1)S(1)} %slice.150), channel_id=1, source_target_pairs={{0,4},{4,0},{8,12},{12,8},{16,20},{20,16},{24,28},{28,24},{1,5},{5... | collective-permute-start | bytes 1179656 | tf_op jit(solution)/shard_map/ppermute | solution.py:96
  113.0 0.7 collective-permute-start.14
  113.7 8.7 %collective-permute-done.16 = bf16[8,192,128]{2,1,0:T(8,128)(2,1)S(1)} collective-permute-done((bf16[8,192,128]{2,1,0:T(8,128)(2,1)S(1)}, bf16[8,192,128]{2,1,0:T(8,128)(2,1)S(1)}, u32[]{:S(2)}, u32[]{:S(2)}) %collective-permute-start.16) | collective-permute-done | bytes 393248 | tf_op jit(solution)/shard_map/ppermute | solution.py:96
  122.5 0.7 collective-permute-start.17
  123.2 1.5 %collective-permute-done.14 = bf16[8,208,128]{2,1,0:T(8,128)(2,1)S(1)} collective-permute-done((bf16[8,208,128]{2,1,0:T(8,128)(2,1)S(1)}, bf16[8,208,128]{2,1,0:T(8,128)(2,1)S(1)}, u32[]{:S(2)}, u32[]{:S(2)}) %collective-permute-start.14) | collective-permute-done | bytes 426016 | tf_op jit(solution)/shard_map/ppermute | solution.py:96
  124.8 0.4 collective-permute-start.15
  125.2 3.9 %collective-permute-done.17 = bf16[4,192,128]{2,1,0:T(8,128)(2,1)S(1)} collective-permute-done((bf16[4,192,128]{2,1,0:T(8,128)(2,1)S(1)}, bf16[4,192,128]{2,1,0:T(8,128)(2,1)S(1)}, u32[]{:S(2)}, u32[]{:S(2)}) %collective-permute-start.17) | collective-permute-done | bytes 196640 | tf_op jit(solution)/shard_map/ppermute | solution.py:96
  129.1 1.9 %collective-permute-done.15 = bf16[4,208,128]{2,1,0:T(8,128)(2,1)S(1)} collective-permute-done((bf16[4,208,128]{2,1,0:T(8,128)(2,1)S(1)}, bf16[4,208,128]{2,1,0:T(8,128)(2,1)S(1)}, u32[]{:S(2)}, u32[]{:S(2)}) %collective-permute-start.15) | collective-permute-done | bytes 213024 | tf_op jit(solution)/shard_map/ppermute | solution.py:96
  131.2 1.6 %collective-permute-start.18 = (bf16[1,400,128]{2,1,0:T(8,128)(2,1)S(1)}, bf16[1,400,128]{2,1,0:T(8,128)(2,1)S(1)}, u32[]{:S(2)}, u32[]{:S(2)}) collective-permute-start(bf16[1,400,128]{2,1,0:T(8,128)(2,1)S(1)} %get-tuple-element.75), channel_id=1, source_target_pairs={{0,8},{4,12},{8,0},{12,4},{16,24},{20,28},{24,16},{28,20},{1,9},{5... | collective-permute-start | bytes 307208 | tf_op jit(solution)/shard_map/ppermute | solution.py:96
  132.8 0.6 collective-permute-start.19
  133.4 2.3 %collective-permute-start.20 = (bf16[1,400,128]{2,1,0:T(8,128)(2,1)S(1)}, bf16[1,400,128]{2,1,0:T(8,128)(2,1)S(1)}, u32[]{:S(2)}, u32[]{:S(2)}) collective-permute-start(bf16[1,400,128]{2,1,0:T(8,128)(2,1)S(1)} %get-tuple-element.76), channel_id=1, source_target_pairs={{0,24},{4,28},{8,16},{12,20},{16,8},{20,12},{24,0},{28,4},{1,25},{... | collective-permute-start | bytes 307208 | tf_op jit(solution)/shard_map/ppermute | solution.py:96
  136.3 0.5 slice.117
  136.9 1.3 collective-permute-done.18
  138.2 3.7 %collective-permute-done.19 = bf16[1,400,128]{2,1,0:T(8,128)(2,1)S(1)} collective-permute-done((bf16[1,400,128]{2,1,0:T(8,128)(2,1)S(1)}, bf16[1,400,128]{2,1,0:T(8,128)(2,1)S(1)}, u32[]{:S(2)}, u32[]{:S(2)}) %collective-permute-start.19) | collective-permute-done | bytes 102432 | tf_op jit(solution)/shard_map/ppermute | solution.py:96
  142.1 0.1 reshape.42
  142.2 1.0 multiply_subtract_fusion
  (63 shorter events, 1.6 us)
Async XLA Ops:
  0.6 21.9 %copy-start.7 = (bf16[2,1,77,768]{3,0,2,1:T(2,128)(2,1)S(1)}, bf16[2,1,77,768]{3,0,2,1:T(2,128)(2,1)}, u32[]{:S(2)}) copy-start(bf16[2,1,77,768]{3,0,2,1:T(2,128)(2,1)} %param.17) | copy-start | bytes 709636
  2.0 11.7 %collective-permute-start = (bf16[1,400,128]{2,1,0:T(8,128)(2,1)S(1)}, bf16[1,400,128]{2,1,0:T(8,128)(2,1)S(1)}, u32[]{:S(2)}, u32[]{:S(2)}) collective-permute-start(bf16[1,400,128]{2,1,0:T(8,128)(2,1)S(1)} %maximum_bitcast_fusion), channel_id=1, source_target_pairs={{0,8},{4,12},{8,0},{12,4},{16,24},{20,28},{24,16},{28,20},{1,9},{5... | collective-permute-start | bytes 307208 | tf_op jit(solution)/shard_map/ppermute | solution.py:96
  5.1 10.7 %collective-permute-start.1 = (bf16[1,400,128]{2,1,0:T(8,128)(2,1)S(1)}, bf16[1,400,128]{2,1,0:T(8,128)(2,1)S(1)}, u32[]{:S(2)}, u32[]{:S(2)}) collective-permute-start(bf16[1,400,128]{2,1,0:T(8,128)(2,1)S(1)} %maximum_bitcast_fusion), channel_id=1, source_target_pairs={{0,16},{4,20},{8,24},{12,28},{16,0},{20,4},{24,8},{28,12},{1,17},{... | collective-permute-start | bytes 307208 | tf_op jit(solution)/shard_map/ppermute | solution.py:96
  7.7 8.1 %collective-permute-start.2 = (bf16[1,400,128]{2,1,0:T(8,128)(2,1)S(1)}, bf16[1,400,128]{2,1,0:T(8,128)(2,1)S(1)}, u32[]{:S(2)}, u32[]{:S(2)}) collective-permute-start(bf16[1,400,128]{2,1,0:T(8,128)(2,1)S(1)} %maximum_bitcast_fusion), channel_id=1, source_target_pairs={{0,24},{4,28},{8,16},{12,20},{16,8},{20,12},{24,0},{28,4},{1,25},{... | collective-permute-start | bytes 307208 | tf_op jit(solution)/shard_map/ppermute | solution.py:96
  8.7 7.2 %collective-permute-start.3 = (bf16[2,2,64,192]{3,2,1,0:T(8,128)(2,1)S(1)}, bf16[2,2,64,192]{3,2,1,0:T(8,128)(2,1)S(1)}, u32[]{:S(2)}, u32[]{:S(2)}) collective-permute-start(bf16[2,2,64,192]{3,2,1,0:T(8,128)(2,1)S(1)} %get-tuple-element.74), channel_id=1, source_target_pairs={{0,4},{4,8},{8,12},{12,16},{16,20},{20,24},{24,28},{1,5},{5,9},{9,... | collective-permute-start | bytes 294920 | tf_op jit(solution)/shard_map/ppermute | solution.py:526
  12.3 17.0 %copy-start = (bf16[2,8,64,192]{3,2,1,0:T(8,128)(2,1)S(1)}, bf16[2,8,64,192]{3,2,1,0:T(8,128)(2,1)}, u32[]{:S(2)}) copy-start(bf16[2,8,64,192]{3,2,1,0:T(8,128)(2,1)} %param.15) | copy-start | bytes 1179652
  12.3 17.0 %copy-start.1 = (bf16[768,320]{0,1:T(8,128)(2,1)S(1)}, bf16[768,320]{0,1:T(8,128)(2,1)}, u32[]{:S(2)}) copy-start(bf16[768,320]{0,1:T(8,128)(2,1)} %param.22) | copy-start | bytes 1474564
  12.3 17.0 %copy-start.2 = (bf16[768,320]{0,1:T(8,128)(2,1)S(1)}, bf16[768,320]{0,1:T(8,128)(2,1)}, u32[]{:S(2)}) copy-start(bf16[768,320]{0,1:T(8,128)(2,1)} %param.23) | copy-start | bytes 1474564
  12.3 7.0 %collective-permute-start.4 = (bf16[2,2,64,192]{3,2,1,0:T(8,128)(2,1)S(1)}, bf16[2,2,64,192]{3,2,1,0:T(8,128)(2,1)S(1)}, u32[]{:S(2)}, u32[]{:S(2)}) collective-permute-start(bf16[2,2,64,192]{3,2,1,0:T(8,128)(2,1)S(1)} %get-tuple-element.73), channel_id=1, source_target_pairs={{4,0},{8,4},{12,8},{16,12},{20,16},{24,20},{28,24},{5,1},{9,5},{13... | collective-permute-start | bytes 294920 | tf_op jit(solution)/shard_map/ppermute | solution.py:526
  19.3 5.7 %collective-permute-start.7 = (bf16[4,192,128]{2,1,0:T(8,128)(2,1)S(1)}, bf16[4,192,128]{2,1,0:T(8,128)(2,1)S(1)}, u32[]{:S(2)}, u32[]{:S(2)}) collective-permute-start(bf16[4,192,128]{2,1,0:T(8,128)(2,1)S(1)} %slice.116), channel_id=1, source_target_pairs={{0,2},{1,3},{2,0},{3,1},{4,6},{5,7},{6,4},{7,5},{8,10},{9,11},{10,... | collective-permute-start | bytes 589832 | tf_op jit(solution)/shard_map/ppermute | solution.py:96
  20.9 8.2 %collective-permute-start.5 = (bf16[4,208,128]{2,1,0:T(8,128)(2,1)S(1)}, bf16[4,208,128]{2,1,0:T(8,128)(2,1)S(1)}, u32[]{:S(2)}, u32[]{:S(2)}) collective-permute-start(bf16[4,208,128]{2,1,0:T(8,128)(2,1)S(1)} %slice.115), channel_id=1, source_target_pairs={{0,4},{4,0},{8,12},{12,8},{16,20},{20,16},{24,28},{28,24},{1,5},{5... | collective-permute-start | bytes 638984 | tf_op jit(solution)/shard_map/ppermute | solution.py:96
  25.1 9.8 %collective-permute-start.8 = (bf16[8,192,128]{2,1,0:T(8,128)(2,1)S(1)}, bf16[8,192,128]{2,1,0:T(8,128)(2,1)S(1)}, u32[]{:S(2)}, u32[]{:S(2)}) collective-permute-start(bf16[8,192,128]{2,1,0:T(8,128)(2,1)S(1)} %pad_maximum_fusion.5), channel_id=1, source_target_pairs={{0,4},{4,0},{8,12},{12,8},{16,20},{20,16},{24,28},{28,24},{1,5},{5... | collective-permute-start | bytes 1179656 | tf_op jit(solution)/shard_map/ppermute | solution.py:96
  29.2 8.2 %collective-permute-start.6 = (bf16[8,208,128]{2,1,0:T(8,128)(2,1)S(1)}, bf16[8,208,128]{2,1,0:T(8,128)(2,1)S(1)}, u32[]{:S(2)}, u32[]{:S(2)}) collective-permute-start(bf16[8,208,128]{2,1,0:T(8,128)(2,1)S(1)} %pad_maximum_fusion.3), channel_id=1, source_target_pairs={{0,2},{1,3},{2,0},{3,1},{4,6},{5,7},{6,4},{7,5},{8,10},{9,11},{10,... | collective-permute-start | bytes 1277960 | tf_op jit(solution)/shard_map/ppermute | solution.py:96
  30.2 7.3 %copy-start.5 = (bf16[2,768,576]{2,1,0:T(8,128)(2,1)}, bf16[2,768,576]{2,1,0:T(8,128)(2,1)S(1)}, u32[]{:S(2)}) copy-start(bf16[2,768,576]{2,1,0:T(8,128)(2,1)S(1)} %get-tuple-element.44.c3_far) | copy-start | bytes 5308420
  30.2 7.9 %copy-start.10 = (f32[1000]{0:T(1024)S(1)}, f32[1000]{0:T(1024)}, u32[]{:S(2)}) copy-start(f32[1000]{0:T(1024)} %constant.43.clone) | copy-start | bytes 12004
  30.2 7.9 %copy-start.11 = (s32[2,1]{0,1:T(1,128)S(1)}, s32[2,1]{0,1:T(1,128)}, u32[]{:S(2)}) copy-start(s32[2,1]{0,1:T(1,128)} %param.19) | copy-start | bytes 28
  37.5 3.7 %collective-permute-start.9 = (bf16[16,208,128]{2,1,0:T(8,128)(2,1)S(1)}, bf16[16,208,128]{2,1,0:T(8,128)(2,1)S(1)}, u32[]{:S(2)}, u32[]{:S(2)}) collective-permute-start(bf16[16,208,128]{2,1,0:T(8,128)(2,1)S(1)} %pad_maximum_fusion.1.own_a), channel_id=1, source_target_pairs={{0,1},{1,0},{2,3},{3,2},{4,5},{5,4},{6,7},{7,6},{8,9},{9,8},{10,11... | collective-permute-start | bytes 2555912 | tf_op jit(solution)/shard_map/ppermute | solution.py:96
  37.5 3.6 %collective-permute-start.10 = (bf16[16,192,128]{2,1,0:T(8,128)(2,1)S(1)}, bf16[16,192,128]{2,1,0:T(8,128)(2,1)}, u32[]{:S(2)}, u32[]{:S(2)}) collective-permute-start(bf16[16,192,128]{2,1,0:T(8,128)(2,1)S(1)} %pad_maximum_fusion.2.own_b), channel_id=1, source_target_pairs={{0,1},{1,0},{2,3},{3,2},{4,5},{5,4},{6,7},{7,6},{8,9},{9,8},{10,11... | collective-permute-start | bytes 2359304 | tf_op jit(solution)/shard_map/ppermute | solution.py:96
  38.3 28.6 %copy-start.3 = (f32[2,8,64,4]{2,3,1,0:T(4,128)S(1)}, f32[2,8,64,4]{2,3,1,0:T(4,128)}, u32[]{:S(2)}) copy-start(f32[2,8,64,4]{2,3,1,0:T(4,128)} %param.18) | copy-start | bytes 49156
  38.3 28.6 %copy-start.4 = (bf16[320,4]{0,1:T(4,128)(2,1)S(1)}, bf16[320,4]{0,1:T(4,128)(2,1)}, u32[]{:S(2)}) copy-start(bf16[320,4]{0,1:T(4,128)(2,1)} %param.25) | copy-start | bytes 7684
  77.5 9.6 %all-to-all-start.1 = ((f32[32,1,128]{2,1,0:T(1,128)}), f32[32,1,128]{2,1,0:T(1,128)S(1)}, u32[]{:S(2)}, u32[]{:S(2)}) async-start(f32[32,1,128]{2,1,0:T(1,128)} %get-tuple-element.50), calls=%async_computation.1 | async-start | bytes 32768 | tf_op jit(solution)/shard_map/all_to_all | solution.py:530
  87.6 9.7 %collective-permute-start.11 = (bf16[2,64,320]{2,1,0:T(8,128)(2,1)S(1)}, bf16[2,64,320]{2,1,0:T(8,128)(2,1)S(1)}, u32[]{:S(2)}, u32[]{:S(2)}) collective-permute-start(bf16[2,64,320]{2,1,0:T(8,128)(2,1)S(1)} %get-tuple-element.58), channel_id=1, source_target_pairs={{0,4},{4,8},{8,12},{12,16},{16,20},{20,24},{24,28},{1,5},{5,9},{9,... | collective-permute-start | bytes 245768 | tf_op jit(solution)/shard_map/ppermute | solution.py:526
  90.1 7.2 %collective-permute-start.12 = (bf16[2,64,320]{2,1,0:T(8,128)(2,1)S(1)}, bf16[2,64,320]{2,1,0:T(8,128)(2,1)S(1)}, u32[]{:S(2)}, u32[]{:S(2)}) collective-permute-start(bf16[2,64,320]{2,1,0:T(8,128)(2,1)S(1)} %get-tuple-element.59), channel_id=1, source_target_pairs={{4,0},{8,4},{12,8},{16,12},{20,16},{24,20},{28,24},{5,1},{9,5},{13... | collective-permute-start | bytes 245768 | tf_op jit(solution)/shard_map/ppermute | solution.py:526
  106.1 3.7 %collective-permute-start.13 = (bf16[17,400,128]{2,1,0:T(8,128)(2,1)S(1)}, bf16[17,400,128]{2,1,0:T(8,128)(2,1)S(1)}, u32[]{:S(2)}, u32[]{:S(2)}) collective-permute-start(bf16[17,400,128]{2,1,0:T(8,128)(2,1)S(1)} %get-tuple-element.67), channel_id=1, source_target_pairs={{0,1},{1,0},{2,3},{3,2},{4,5},{5,4},{6,7},{7,6},{8,9},{9,8},{10,11... | collective-permute-start | bytes 5222408 | tf_op jit(solution)/shard_map/ppermute | solution.py:96
  110.3 12.1 %collective-permute-start.16 = (bf16[8,192,128]{2,1,0:T(8,128)(2,1)S(1)}, bf16[8,192,128]{2,1,0:T(8,128)(2,1)S(1)}, u32[]{:S(2)}, u32[]{:S(2)}) collective-permute-start(bf16[8,192,128]{2,1,0:T(8,128)(2,1)S(1)} %slice.150), channel_id=1, source_target_pairs={{0,4},{4,0},{8,12},{12,8},{16,20},{20,16},{24,28},{28,24},{1,5},{5... | collective-permute-start | bytes 1179656 | tf_op jit(solution)/shard_map/ppermute | solution.py:96
  113.0 11.6 %collective-permute-start.14 = (bf16[8,208,128]{2,1,0:T(8,128)(2,1)S(1)}, bf16[8,208,128]{2,1,0:T(8,128)(2,1)S(1)}, u32[]{:S(2)}, u32[]{:S(2)}) collective-permute-start(bf16[8,208,128]{2,1,0:T(8,128)(2,1)S(1)} %slice.146), channel_id=1, source_target_pairs={{0,2},{1,3},{2,0},{3,1},{4,6},{5,7},{6,4},{7,5},{8,10},{9,11},{10,... | collective-permute-start | bytes 1277960 | tf_op jit(solution)/shard_map/ppermute | solution.py:96
  122.5 6.5 %collective-permute-start.17 = (bf16[4,192,128]{2,1,0:T(8,128)(2,1)S(1)}, bf16[4,192,128]{2,1,0:T(8,128)(2,1)S(1)}, u32[]{:S(2)}, u32[]{:S(2)}) collective-permute-start(bf16[4,192,128]{2,1,0:T(8,128)(2,1)S(1)} %slice.191), channel_id=1, source_target_pairs={{0,2},{1,3},{2,0},{3,1},{4,6},{5,7},{6,4},{7,5},{8,10},{9,11},{10,... | collective-permute-start | bytes 589832 | tf_op jit(solution)/shard_map/ppermute | solution.py:96
  124.8 6.2 %collective-permute-start.15 = (bf16[4,208,128]{2,1,0:T(8,128)(2,1)S(1)}, bf16[4,208,128]{2,1,0:T(8,128)(2,1)S(1)}, u32[]{:S(2)}, u32[]{:S(2)}) collective-permute-start(bf16[4,208,128]{2,1,0:T(8,128)(2,1)S(1)} %slice.190), channel_id=1, source_target_pairs={{0,4},{4,0},{8,12},{12,8},{16,20},{20,16},{24,28},{28,24},{1,5},{5... | collective-permute-start | bytes 638984 | tf_op jit(solution)/shard_map/ppermute | solution.py:96
  131.1 11.1 %copy-start.6 = (f32[49320]{0:T(1024)S(1)}, f32[49320]{0:T(1024)}, u32[]{:S(2)}) copy-start(f32[49320]{0:T(1024)} %param.26) | copy-start | bytes 591844
  131.1 11.1 %copy-start.8 = (f32[49320]{0:T(1024)S(1)}, f32[49320]{0:T(1024)}, u32[]{:S(2)}) copy-start(f32[49320]{0:T(1024)} %param.28) | copy-start | bytes 591844
  131.1 11.1 %copy-start.9 = (f32[49320]{0:T(1024)S(1)}, f32[49320]{0:T(1024)}, u32[]{:S(2)}) copy-start(f32[49320]{0:T(1024)} %param.27) | copy-start | bytes 591844
  131.2 7.0 %collective-permute-start.18 = (bf16[1,400,128]{2,1,0:T(8,128)(2,1)S(1)}, bf16[1,400,128]{2,1,0:T(8,128)(2,1)S(1)}, u32[]{:S(2)}, u32[]{:S(2)}) collective-permute-start(bf16[1,400,128]{2,1,0:T(8,128)(2,1)S(1)} %get-tuple-element.75), channel_id=1, source_target_pairs={{0,8},{4,12},{8,0},{12,4},{16,24},{20,28},{24,16},{28,20},{1,9},{5... | collective-permute-start | bytes 307208 | tf_op jit(solution)/shard_map/ppermute | solution.py:96
  132.8 9.1 %collective-permute-start.19 = (bf16[1,400,128]{2,1,0:T(8,128)(2,1)S(1)}, bf16[1,400,128]{2,1,0:T(8,128)(2,1)S(1)}, u32[]{:S(2)}, u32[]{:S(2)}) collective-permute-start(bf16[1,400,128]{2,1,0:T(8,128)(2,1)S(1)} %get-tuple-element.77), channel_id=1, source_target_pairs={{0,16},{4,20},{8,24},{12,28},{16,0},{20,4},{24,8},{28,12},{1,17},{... | collective-permute-start | bytes 307208 | tf_op jit(solution)/shard_map/ppermute | solution.py:96
  133.4 8.5 %collective-permute-start.20 = (bf16[1,400,128]{2,1,0:T(8,128)(2,1)S(1)}, bf16[1,400,128]{2,1,0:T(8,128)(2,1)S(1)}, u32[]{:S(2)}, u32[]{:S(2)}) collective-permute-start(bf16[1,400,128]{2,1,0:T(8,128)(2,1)S(1)} %get-tuple-element.76), channel_id=1, source_target_pairs={{0,24},{4,28},{8,16},{12,20},{16,8},{20,12},{24,0},{28,4},{1,25},{... | collective-permute-start | bytes 307208 | tf_op jit(solution)/shard_map/ppermute | solution.py:96

commit v2 on v1

--- a/solution.py
+++ b/solution.py
@@ -35,7 +35,8 @@
 
 
 def call(
-    kernel, outs, ins, scratch=(), far=(), far_out=(), smem=(), free=(), flops=0, limit=40
+    kernel, outs, ins, scratch=(), far=(), far_out=(), smem=(), free=(), far_like=(), flops=0,
+    limit=40,
 ):
     def space(i):
         return pltpu.SMEM if i in smem else pl.ANY if i in far else VMEM
@@ -45,7 +46,10 @@
 
     return pl.pallas_call(
         kernel,
-        out_shape=[(HBM if i in far_out else VMEM)(*o) for i, o in enumerate(outs)],
+        out_shape=[
+            jax.ShapeDtypeStruct(*o) if i in far_like else (HBM if i in far_out else VMEM)(*o)
+            for i, o in enumerate(outs)
+        ],
         in_specs=[pl.BlockSpec(memory_space=space(i)) for i in range(len(ins))],
         out_specs=[
             pl.BlockSpec(memory_space=pl.ANY if i in far_out else VMEM) for i in range(len(outs))
@@ -179,16 +183,27 @@
     return row
 
 
-def prepare_kernel(cols, cond, low, high, context, wk_t, wv_t, c3, k_t, v_t):
+def prepare_kernel(
+    cols, heads, cond, low, high, context, wk_t, wv_t, resid, wq, wo,
+    c3, keys, keys_t, values, values_t, resid_t, wq_t, wo_t,
+):
     images = cond.shape[0]
     channels, words = wk_t.shape[0], context.shape[1]
+    room = keys.shape[2]
     pad = jnp.zeros((channels, LANES - words), F32)
     for i in range(images):
         wide = jnp.concatenate([low[i], cond[i], high[i]], axis=0).astype(F32)
         c3[i] = three_columns(wide, cols)
-        for weight, out in ((wk_t, k_t), (wv_t, v_t)):
-            part = mm_nt(weight[...], context[i])
-            out[i] = jnp.concatenate([part, pad], axis=1).astype(BF)
+        for weight, flat, tall in ((wk_t, keys, keys_t), (wv_t, values, values_t)):
+            turned = jnp.concatenate([mm_nt(weight[...], context[i]), pad], axis=1)
+            for h in range(heads):
+                part = turned[h * HDIM : (h + 1) * HDIM]
+                tall[i, h] = part[:, :room].astype(BF)
+                part = jnp.concatenate([part, jnp.zeros((LANES - HDIM, LANES), F32)], axis=0)
+                flat[i, h] = part.T[:room, :HDIM].astype(BF)
+        resid_t[i] = resid[i].astype(F32).T.astype(BF)
+    wq_t[...] = wq[...].astype(F32).T.astype(BF)
+    wo_t[...] = wo[...].astype(F32).T.astype(BF)
 
 
 def unpack_table(plan, me, own_a, other_a, own_b, other_b, table, owners):
@@ -284,92 +299,85 @@
     return lax.rsqrt(jnp.full((1, 1), lane_pick(line, 0) / elements + EPS_NORM, F32))
 
 
-def by_head(left, right, turned):
-    span = 2 * LANES
-    cut = right.shape[1] - span
-    if right.shape[0] != span + LANES // 2 or cut != 6 * LANES:
-        return mm_nt(left, right) if turned else mm(left, right)
-    if not turned:
-        most = mm(left[:, :span], right[:span, :cut])
-        return jnp.concatenate([most, mm(left[:, LANES:], right[LANES:, cut:])], axis=1)
-    most = mm_nt(left[:, :cut], right[:span, :cut])
-    rest = mm_nt(left[:, cut:], right[LANES:, cut:])
-    return jnp.concatenate(
-        [most[:, :LANES], most[:, LANES:] + rest[:, :LANES], rest[:, LANES:]], axis=1
-    )
-
-
 def attention_kernel(
-    plan, sizes, snr, sums, trailing, noise_t, k_t, v_t, wp_t, feature_far, resid_far, wq_far, wo_far,
-    g_far, u_out, payload, feature, resid, wq, wo, g_out, kbd, vbd, sems,
+    plan, sizes, snr, sums, trailing, noise_t, wp_t,
+    feature_far, resid_far, wqt_far, keys_far, valuest_far, wot_far, wo_far, values_far, keyst_far, wq_far,
+    g_far, u_out, payload,
+    feature, resid, wqt, keys, valuest, wot, wo, values, keyst, wq, g_out, sems,
 ):
     elements, loss_count, words = sizes
     images, tokens, channels = feature.shape
-    heads = kbd.shape[2] // LANES
-    loads = [start(wq_far, wq, sems.at[0]), start(wo_far, wo, sems.at[1])]
-    for i in range(images):
-        loads.append(start(feature_far.at[i], feature.at[i], sems.at[2 + 2 * i]))
-        loads.append(start(resid_far.at[i], resid.at[i], sems.at[3 + 2 * i]))
+    heads, room = keys.shape[1:3]
+    each = range(images)
+    loads = [[], [], []]
+    pairs = (
+        (wqt_far, wqt, 0), (keys_far, keys, 0), (valuest_far, valuest, 1), (wot_far, wot, 1),
+        (wo_far, wo, 2), (values_far, values, 2), (keyst_far, keyst, 2), (wq_far, wq, 2),
+    )
+    for i in each:
+        loads[0].append(start(feature_far.at[i], feature.at[i], sems.at[2 * i]))
+        loads[0].append(start(resid_far.at[i], resid.at[i], sems.at[2 * i + 1]))
+    for j, (far, near, group) in enumerate(pairs):
+        loads[group].append(start(far, near, sems.at[2 * images + j]))
     line = jnp.sum(sums[...], axis=0)
     scale = norm_of(line, elements)
     denom = lane_pick(line, 1) / plan.sp * loss_count
     inject = trailing[3:4]
+    column = jnp.broadcast_to(inject, (LANES, channels)).T[:, 0:1] * scale
     root = HDIM ** (-0.5)
-    for i in range(images):
-        for source, wide in ((k_t, kbd), (v_t, vbd)):
-            row_head = lax.broadcasted_iota(jnp.int32, source.shape[1:], 0) // HDIM
-            value = source[i].astype(F32)
-            for h in range(heads):
-                part = jnp.where(row_head == h, value, 0.0).astype(BF)
-                wide[i, :, h * LANES : (h + 1) * LANES] = part
     out_chan, width = noise_t.shape[2:]
     spare = jnp.zeros((16 - out_chan, channels), F32)
     wide_pred = jnp.concatenate([wp_t[...].astype(F32), spare], axis=0).astype(BF)
-    known = lax.broadcasted_iota(jnp.int32, (tokens, LANES), 1) < words
-    each = range(images)
+    known = lax.broadcasted_iota(jnp.int32, (room, tokens), 0) < words
+    for copy in loads[0]:
+        copy.wait()
     injected, scores = [], []
     for i in each:
-        for copy in loads[:2] * (i == 0) + loads[2 + 2 * i : 4 + 2 * i]:
-            copy.wait()
-        injected.append(resid[i].astype(F32) + inject * (feature[i] * scale))
-        query = mm(injected[i].astype(BF), wq[...]).astype(BF)
-        scores.append(by_head(query, kbd[i], False))
+        injected.append(resid[i].astype(F32) + column * feature[i].T)
+        query = mm(wqt[...], injected[i].astype(BF))
+        parts = [query[h * HDIM : (h + 1) * HDIM].astype(BF) for h in range(heads)]
+        scores.append([mm(keys[i, h], parts[h]) for h in range(heads)])
     attn = []
     for i in each:
         attn.append([])
         for h in range(heads):
-            part = jnp.where(known, scores[i][:, h * LANES : (h + 1) * LANES] * root, -1e30)
-            part = jnp.exp(part - jnp.max(part, axis=1, keepdims=True))
-            attn[i].append(part / jnp.sum(part, axis=1, keepdims=True))
+            part = jnp.where(known, scores[i][h] * root, -1e30)
+            part = jnp.exp(part - jnp.max(part, axis=0, keepdims=True))
+            attn[i].append(part / jnp.sum(part, axis=0, keepdims=True))
+    for copy in loads[1]:
+        copy.wait()
     loss = jnp.zeros((1, 1), F32)
     g_y, g_attn = [], []
     for i in each:
-        low = jnp.concatenate([part.astype(BF) for part in attn[i]], axis=1)
-        mixed = by_head(low, vbd[i], True).astype(BF)
-        after = injected[i] + mm(mixed, wo[...])
-        pred = mm_nt(wide_pred, after.astype(BF))
+        mixed = [mm(valuest[i, h], attn[i][h].astype(BF)) for h in range(heads)]
+        after = injected[i] + mm(wot[...], jnp.concatenate(mixed, axis=0).astype(BF))
+        pred = mm(wide_pred, after.astype(BF))
         noise = jnp.concatenate([noise_t[i, r] for r in range(tokens // width)], axis=1)
         noise = jnp.concatenate([noise, jnp.zeros((16 - out_chan, tokens), F32)], axis=0)
         error = pred - noise
         loss = loss + snr[i] * jnp.sum(error * error)
         g_pred = (2.0 * snr[i] / denom) * error
-        g_y.append(mm_tn(g_pred.astype(BF), wide_pred))
-        g_mixed = mm_nt(g_y[i].astype(BF), wo[...]).astype(BF)
-        g_attn.append(by_head(g_mixed, vbd[i], False))
+        g_y.append(mm_tn(wide_pred, g_pred.astype(BF)))
+        if i == 0:
+            for copy in loads[2]:
+                copy.wait()
+        g_mixed = mm(wo[...], g_y[i].astype(BF))
+        parts = [g_mixed[h * HDIM : (h + 1) * HDIM].astype(BF) for h in range(heads)]
+        g_attn.append([mm(values[i, h], parts[h]) for h in range(heads)])
     g_scores = []
     for i in each:
         g_scores.append([])
         for h in range(heads):
-            part = g_attn[i][:, h * LANES : (h + 1) * LANES]
-            inner = jnp.sum(attn[i][h] * part, axis=1, keepdims=True)
-            g_scores[i].append((attn[i][h] * (part - inner)).astype(BF))
+            inner = jnp.sum(attn[i][h] * g_attn[i][h], axis=0, keepdims=True)
+            g_scores[i].append((attn[i][h] * (g_attn[i][h] - inner)).astype(BF))
     u = jnp.zeros((1, channels), F32)
     stores = []
     for i in each:
-        g_query = by_head(jnp.concatenate(g_scores[i], axis=1), kbd[i], True) * root
-        g_x = g_y[i] + mm_nt(g_query.astype(BF), wq[...])
+        parts = [mm(keyst[i, h], g_scores[i][h]) * root for h in range(heads)]
+        g_x = g_y[i] + mm(wq[...], jnp.concatenate(parts, axis=0).astype(BF))
+        g_x = g_x.T
         g_out[i] = scale * (inject * g_x)
-        stores.append(start(g_out.at[i], g_far.at[i], sems.at[2 + 2 * images + i]))
+        stores.append(start(g_out.at[i], g_far.at[i], sems.at[2 * images + len(pairs) + i]))
         u = u + jnp.sum(g_x * feature[i], axis=0, keepdims=True)
     u_out[...] = jnp.broadcast_to(u, u_out.shape)
     cross = jnp.sum(inject * u)
@@ -379,11 +387,12 @@
 
 
 def back_kernel(
-    g_far, feature_far, relu_far, w_two_far, by_g, by_feature, g, feature, relu, w_two, sems
+    g_far, feature_far, relu_far, w_two_far, x3_far, by_g, by_feature, x3,
+    g, feature, relu, w_two, sems,
 ):
     images, tokens, channels = by_g.shape
     loads = [start(w_two_far, w_two, sems.at[0])]
-    pairs = ((feature_far, feature), (relu_far, relu), (g_far, g))
+    pairs = ((feature_far, feature), (relu_far, relu), (g_far, g), (x3_far, x3))
     for j, (far, near) in enumerate(pairs):
         loads.append(start(far, near, sems.at[1 + j]))
     for copy in loads[:3]:
@@ -395,6 +404,7 @@
     for i in range(images):
         back = mm_nt(g[i].astype(BF), w_two[...])
         by_g[i] = jnp.where(relu[i].astype(F32) > 0, back, 0.0)
+    loads[4].wait()
 
 
 def solve_kernel(
@@ -414,20 +424,18 @@
 
 
 def block_weight_kernel(
-    cols, scalars, u, gz, x3_far, relu_far, g_far, feature_far,
-    d_block, d_rows, g_f, x3, relu, g, feature, sems,
+    cols, scalars, u, gz, x3, relu_far, g_far, feature_far,
+    d_block, d_rows, g_f, relu, g, feature, sems,
 ):
     images, tokens, channels = gz.shape
     kept = 3 * channels
-    loads = [start(x3_far.at[i], x3.at[i], sems.at[i]) for i in range(images)]
     late = [
-        start(far, near, sems.at[images + j])
+        start(far, near, sems.at[j])
         for j, (far, near) in enumerate(((relu_far, relu), (g_far, g), (feature_far, feature)))
     ]
     pull, scale = scalars[0:1, 1:2], scalars[0:1, 2:3]
     rows = [jnp.zeros((1, channels), F32), jnp.zeros((1, channels), F32)]
     for i in range(images):
-        loads[i].wait()
         for dy in range(3):
             at = slice(dy * kept, (dy + 1) * kept)
             part = mm_tn(x3[i, dy * cols : dy * cols + tokens], gz[i])
@@ -564,21 +572,30 @@
 
     def prepare(low, high):
         return call(
-            functools.partial(prepare_kernel, cols),
+            functools.partial(prepare_kernel, cols, heads),
             [
                 ((images, wide + 2 * cols, kept_in), BF),
-                ((images, channels, LANES), BF),
-                ((images, channels, LANES), BF),
+                ((images, heads, room, HDIM), BF),
+                ((images, heads, HDIM, room), BF),
+                ((images, heads, room, HDIM), BF),
+                ((images, heads, HDIM, room), BF),
+                ((images, channels, tokens), BF),
+                ((channels, channels), BF),
+                ((channels, channels), BF),
             ],
             [
                 cond.reshape(images, tokens, in_chan), low, high,
                 context.reshape(images, words, -1), key_weight.T, value_weight.T,
+                resid.reshape(images, tokens, channels), query_weight, out_weight,
             ],
-            free=(0, 3, 4, 5),
+            free=(0, 3, 4, 5, 6, 7, 8),
+            far_like=(0, 1, 2, 3, 4, 5, 6, 7),
             flops=4 << 30,
         )
 
-    gathered, (c3, k_t, v_t) = gather_parameters(plan, master, edges, prepare)
+    room = -(-words // 16) * 16
+    gathered, prepared = gather_parameters(plan, master, edges, prepare)
+    c3, keys, keys_t, values, values_t, resid_t, wq_t, wo_t = prepared
     line = ((plan.count, 1, LANES), F32)
     per_image = (images, tokens, channels)
     w1t, w_two, trailing, feature, relu_low, x3, payload = call(
@@ -609,43 +626,48 @@
         flops=4 << 30,
     )
     sums = everywhere(payload)
+    square = (channels, channels)
     g, u, payload = call(
         functools.partial(
             attention_kernel, plan, (elements, height * cols * out_chan, words)
         ),
         [(per_image, F32), ((8, channels), F32), line],
         [
-            snr, sums, trailing, jnp.transpose(noise, (0, 1, 3, 2)), k_t, v_t, pred_weight.T,
-            feature, resid.reshape(per_image), query_weight, out_weight,
+            snr, sums, trailing, jnp.transpose(noise, (0, 1, 3, 2)), pred_weight.T,
+            feature, resid_t, wq_t, keys, values_t, wo_t, out_weight, values, keys_t, query_weight,
         ],
         scratch=[
             VMEM(per_image, F32),
-            VMEM(per_image, BF),
-            VMEM((channels, channels), BF),
-            VMEM((channels, channels), BF),
+            VMEM((images, channels, tokens), BF),
+            VMEM(square, BF),
+            VMEM((images, heads, room, HDIM), BF),
+            VMEM((images, heads, HDIM, room), BF),
+            VMEM(square, BF),
+            VMEM(square, BF),
+            VMEM((images, heads, room, HDIM), BF),
+            VMEM((images, heads, HDIM, room), BF),
+            VMEM(square, BF),
             VMEM(per_image, F32),
-            VMEM((images, channels, heads * LANES), BF),
-            VMEM((images, channels, heads * LANES), BF),
-            DMA((2 + 3 * images,)),
+            DMA((3 * images + 8,)),
         ],
         smem=(0,),
-        far=(7, 8, 9, 10),
+        far=tuple(range(5, 15)),
         far_out=(0,),
         flops=4 << 30,
     )
     sums_two = everywhere(payload)
-    by_g, by_feature = call(
+    by_g, by_feature, x3 = call(
         back_kernel,
-        [(per_image, F32), (per_image, F32)],
-        [g, feature, relu_low, w_two],
+        [(per_image, F32), (per_image, F32), ((images, wide, kept), BF)],
+        [g, feature, relu_low, w_two, x3],
         scratch=[
             VMEM(per_image, F32),
             VMEM(per_image, F32),
             VMEM(per_image, BF),
             VMEM((channels, channels), BF),
-            DMA((4,)),
-        ],
-        far=(0, 1, 2, 3),
+            DMA((5,)),
+        ],
+        far=(0, 1, 2, 3, 4),
         flops=4 << 30,
     )
     scalars, gz, edge_top, edge_bottom = call(
@@ -666,13 +688,12 @@
         [((n_one + n_two, channels), F32), ((8, channels), F32), (per_image, F32)],
         [scalars, u, gz, x3, relu_low, g, feature],
         scratch=[
-            VMEM((images, wide, kept), BF),
             VMEM(per_image, BF),
             VMEM(per_image, F32),
             VMEM(per_image, F32),
-            DMA((images + 3,)),
-        ],
-        far=(3, 4, 5, 6),
+            DMA((3,)),
+        ],
+        far=(4, 5, 6),
         flops=2 << 30,
     )
     keep, send = call(

time: 144 us -> 140 us (0.972)
  waiting for transfers between devices: 48.8 us -> 44.2 us
  local copies, waits for them, and re-layouts: 3.28 us -> 7.51 us
  Pallas kernels: 41.6 us -> 39.3 us
    unnamed x25 -> x49, local copies, waits for them, and re-layouts: 0.1 us -> 4.33 us
    ppermute x17, waiting for transfers between devices: 41.4 us -> 37.3 us  [swap(): lax.ppermute(value, axis, [(i, i ^ step * stride) for i in range(count)])]
    pallas_call x7, Pallas kernels: 41.6 us -> 39.3 us  [call(): pl.pallas_call(kernel, out_shape=[jax.ShapeDtypeStruct(*o) if i in far_li...]
    all_to_all x1, waiting for transfers between devices: 3.94 us -> 2.45 us  [everywhere(): return lax.all_to_all(payload, ('sp', 'hd'), 0, 0, tiled=True)]
  transfers between devices with their start and end apart: 22 -> 22, of which waited for: 15 -> 15; matrix products, arithmetic and copies ran while one was open for 2% -> 2% of each run, Pallas kernels for 7% -> 6%
where the time goes in v2:
time: 140 us
  waiting for transfers between devices  44.2 us (32%)
  Pallas kernels  39.3 us (28%)
  starting transfers between devices  31.1 us (22%)
  blocking collectives  13.4 us (10%)
  local copies, waits for them, and re-layouts  7.51 us (5%)
  other arithmetic  2.52 us (2%)
  between operations  1.9 us (1%)
    pallas_call x7, Pallas kernels, call(): pl.pallas_call(kernel, out_shape=[jax.ShapeDtypeStruct(*o) if i in far_li...  39.3 us
    ppermute x17, waiting for transfers between devices, swap(): lax.ppermute(value, axis, [(i, i ^ step * stride) for i in range(count)])  37.3 us
    ppermute x17, starting transfers between devices, swap(): lax.ppermute(value, axis, [(i, i ^ step * stride) for i in range(count)])  19.6 us
    all_to_all x1, blocking collectives, everywhere(): return lax.all_to_all(payload, ('sp', 'hd'), 0, 0, tiled=True)  13.4 us
    ppermute x4, starting transfers between devices, shift_rows(): return lax.ppermute(value, 'sp', pairs)  8.94 us
    ppermute x4, waiting for transfers between devices, shift_rows(): return lax.ppermute(value, 'sp', pairs)  4.53 us
    unnamed x49, local copies, waits for them, and re-layouts  4.33 us
  transfers between devices with their start and end apart: 22, of which 15 were waited for; matrix products, arithmetic and copies ran while one was open for 2% of the time, Pallas kernels for 6%

profile of v2, /device:TPU:0, one launch (start us, length us, event | category | flops | bytes accessed | tf_op | source)
XLA Modules:
  0.0 140.0 jit_solution(15523182402488099662)
XLA Ops:
  0.7 1.1 fusion.1
  2.0 3.0 %collective-permute-start = (bf16[1,400,128]{2,1,0:T(8,128)(2,1)S(1)}, bf16[1,400,128]{2,1,0:T(8,128)(2,1)S(1)}, u32[]{:S(2)}, u32[]{:S(2)}) collective-permute-start(bf16[1,400,128]{2,1,0:T(8,128)(2,1)S(1)} %maximum_bitcast_fusion), channel_id=1, source_target_pairs={{0,8},{4,12},{8,0},{12,4},{16,24},{20,28},{24,16},{28,20},{1,9},{5... | collective-permute-start | bytes 307208 | tf_op jit(solution)/shard_map/ppermute | solution.py:100
  5.1 2.6 %collective-permute-start.1 = (bf16[1,400,128]{2,1,0:T(8,128)(2,1)S(1)}, bf16[1,400,128]{2,1,0:T(8,128)(2,1)S(1)}, u32[]{:S(2)}, u32[]{:S(2)}) collective-permute-start(bf16[1,400,128]{2,1,0:T(8,128)(2,1)S(1)} %maximum_bitcast_fusion), channel_id=1, source_target_pairs={{0,16},{4,20},{8,24},{12,28},{16,0},{20,4},{24,8},{28,12},{1,17},{... | collective-permute-start | bytes 307208 | tf_op jit(solution)/shard_map/ppermute | solution.py:100
  7.7 1.0 fusion.10
  8.7 3.6 %collective-permute-start.3 = (bf16[2,2,64,192]{3,2,1,0:T(8,128)(2,1)S(1)}, bf16[2,2,64,192]{3,2,1,0:T(8,128)(2,1)S(1)}, u32[]{:S(2)}, u32[]{:S(2)}) collective-permute-start(bf16[2,2,64,192]{3,2,1,0:T(8,128)(2,1)S(1)} %get-tuple-element.96), channel_id=1, source_target_pairs={{0,4},{4,8},{8,12},{12,16},{16,20},{20,24},{24,28},{1,5},{5,9},{9,... | collective-permute-start | bytes 294920 | tf_op jit(solution)/shard_map/ppermute | solution.py:534
  12.4 1.4 %collective-permute-start.4 = (bf16[2,2,64,192]{3,2,1,0:T(8,128)(2,1)S(1)}, bf16[2,2,64,192]{3,2,1,0:T(8,128)(2,1)S(1)}, u32[]{:S(2)}, u32[]{:S(2)}) collective-permute-start(bf16[2,2,64,192]{3,2,1,0:T(8,128)(2,1)S(1)} %get-tuple-element.95), channel_id=1, source_target_pairs={{4,0},{8,4},{12,8},{16,12},{20,16},{24,20},{28,24},{5,1},{9,5},{13... | collective-permute-start | bytes 294920 | tf_op jit(solution)/shard_map/ppermute | solution.py:534
  13.8 2.0 %collective-permute-done.1 = bf16[1,400,128]{2,1,0:T(8,128)(2,1)S(1)} collective-permute-done((bf16[1,400,128]{2,1,0:T(8,128)(2,1)S(1)}, bf16[1,400,128]{2,1,0:T(8,128)(2,1)S(1)}, u32[]{:S(2)}, u32[]{:S(2)}) %collective-permute-start.1) | collective-permute-done | bytes 102432 | tf_op jit(solution)/shard_map/ppermute | solution.py:100
  15.9 3.5 %collective-permute-done.4 = bf16[2,2,64,192]{3,2,1,0:T(8,128)(2,1)S(1)} collective-permute-done((bf16[2,2,64,192]{3,2,1,0:T(8,128)(2,1)S(1)}, bf16[2,2,64,192]{3,2,1,0:T(8,128)(2,1)S(1)}, u32[]{:S(2)}, u32[]{:S(2)}) %collective-permute-start.4) | collective-permute-done | bytes 98336 | tf_op jit(solution)/shard_map/ppermute | solution.py:534
  19.4 1.6 %collective-permute-start.7 = (bf16[4,192,128]{2,1,0:T(8,128)(2,1)S(1)}, bf16[4,192,128]{2,1,0:T(8,128)(2,1)S(1)}, u32[]{:S(2)}, u32[]{:S(2)}) collective-permute-start(bf16[4,192,128]{2,1,0:T(8,128)(2,1)S(1)} %slice.116), channel_id=1, source_target_pairs={{0,2},{1,3},{2,0},{3,1},{4,6},{5,7},{6,4},{7,5},{8,10},{9,11},{10,... | collective-permute-start | bytes 589832 | tf_op jit(solution)/shard_map/ppermute | solution.py:100
  21.0 1.6 %collective-permute-start.5 = (bf16[4,208,128]{2,1,0:T(8,128)(2,1)S(1)}, bf16[4,208,128]{2,1,0:T(8,128)(2,1)S(1)}, u32[]{:S(2)}, u32[]{:S(2)}) collective-permute-start(bf16[4,208,128]{2,1,0:T(8,128)(2,1)S(1)} %slice.115), channel_id=1, source_target_pairs={{0,4},{4,0},{8,12},{12,8},{16,20},{20,16},{24,28},{28,24},{1,5},{5... | collective-permute-start | bytes 638984 | tf_op jit(solution)/shard_map/ppermute | solution.py:100
  22.6 2.5 %collective-permute-done.7 = bf16[4,192,128]{2,1,0:T(8,128)(2,1)S(1)} collective-permute-done((bf16[4,192,128]{2,1,0:T(8,128)(2,1)S(1)}, bf16[4,192,128]{2,1,0:T(8,128)(2,1)S(1)}, u32[]{:S(2)}, u32[]{:S(2)}) %collective-permute-start.7) | collective-permute-done | bytes 196640 | tf_op jit(solution)/shard_map/ppermute | solution.py:100
  25.2 1.6 %collective-permute-start.8 = (bf16[8,192,128]{2,1,0:T(8,128)(2,1)S(1)}, bf16[8,192,128]{2,1,0:T(8,128)(2,1)S(1)}, u32[]{:S(2)}, u32[]{:S(2)}) collective-permute-start(bf16[8,192,128]{2,1,0:T(8,128)(2,1)S(1)} %pad_maximum_fusion.5), channel_id=1, source_target_pairs={{0,4},{4,0},{8,12},{12,8},{16,20},{20,16},{24,28},{28,24},{1,5},{5... | collective-permute-start | bytes 1179656 | tf_op jit(solution)/shard_map/ppermute | solution.py:100
  26.8 2.4 %collective-permute-done.5 = bf16[4,208,128]{2,1,0:T(8,128)(2,1)S(1)} collective-permute-done((bf16[4,208,128]{2,1,0:T(8,128)(2,1)S(1)}, bf16[4,208,128]{2,1,0:T(8,128)(2,1)S(1)}, u32[]{:S(2)}, u32[]{:S(2)}) %collective-permute-start.5) | collective-permute-done | bytes 213024 | tf_op jit(solution)/shard_map/ppermute | solution.py:100
  29.4 1.3 shard_map.174
  30.7 0.7 copy-done.14
  31.4 0.7 copy-done.15
  32.1 0.7 copy-done.16
  32.7 0.7 copy-done.17
  33.4 1.5 %collective-permute-done.8 = bf16[8,192,128]{2,1,0:T(8,128)(2,1)S(1)} collective-permute-done((bf16[8,192,128]{2,1,0:T(8,128)(2,1)S(1)}, bf16[8,192,128]{2,1,0:T(8,128)(2,1)S(1)}, u32[]{:S(2)}, u32[]{:S(2)}) %collective-permute-start.8) | collective-permute-done | bytes 393248 | tf_op jit(solution)/shard_map/ppermute | solution.py:100
  35.1 2.3 %collective-permute-done.6 = bf16[8,208,128]{2,1,0:T(8,128)(2,1)S(1)} collective-permute-done((bf16[8,208,128]{2,1,0:T(8,128)(2,1)S(1)}, bf16[8,208,128]{2,1,0:T(8,128)(2,1)S(1)}, u32[]{:S(2)}, u32[]{:S(2)}) %collective-permute-start.6) | collective-permute-done | bytes 426016 | tf_op jit(solution)/shard_map/ppermute | solution.py:100
  37.6 0.5 collective-permute-start.10
  38.4 2.8 %collective-permute-done.10.other_b = bf16[16,192,128]{2,1,0:T(8,128)(2,1)} collective-permute-done((bf16[16,192,128]{2,1,0:T(8,128)(2,1)S(1)}, bf16[16,192,128]{2,1,0:T(8,128)(2,1)}, u32[]{:S(2)}, u32[]{:S(2)}) %collective-permute-start.10) | collective-permute-done | bytes 786464 | tf_op jit(solution)/shard_map/ppermute | solution.py:100
  41.2 12.1 %shard_map.175 = (bf16[2880,320]{1,0:T(8,128)(2,1)}, bf16[320,320]{1,0:T(8,128)(2,1)}, f32[8,320]{1,0:T(8,128)S(1)}, f32[2,512,320]{2,1,0:T(8,128)}, bf16[2,512,...) custom-call(s32[3]{0:T(128)S(1)} %pad_add_fusion.place, f32[2]{0:T(128)S(1)} %fusion.7.snr, ...), custom_call_target="tpu_custom_call" | custom-call | flops 4294967296 | bytes 1048576 | tf_op jit(solution)/shard_map/pallas_call | solution.py:47
  53.3 13.4 %all_to_all.10.sums = f32[32,1,128]{2,1,0:T(1,128)S(1)} all-to-all(f32[32,1,128]{2,1,0:T(1,128)S(1)} %get-tuple-element.61), channel_id=1, replica_groups=mesh['sp'=8,'hd'=4] {'sp','hd'}, dimensions={0} | all-to-all | bytes 32768 | tf_op jit(solution)/shard_map/all_to_all | solution.py:538
  66.8 9.4 %shard_map.176 = (f32[2,512,320]{2,1,0:T(8,128)}, f32[8,320]{1,0:T(8,128)S(1)}, f32[32,1,128]{2,1,0:T(1,128)}) custom-call(f32[2]{0:T(128)S(1)} %fusion.7.snr, f32[32,1,128]{2,1,0:T(1,128)S(1)} %all_to_all.10.sums, f32[8,320]{1,0:T(8,128)S(1)} %get-tuple-element.62.trailing, f32[2,8,4,64]{3,2,1,0:T(4,128)S(1)} %bitcast.32, bf16[4,320]{1,0:T(4,128)(2,1)S(1)} %bitcast.33, ...), custom_call_target="tpu_custom_call" | custom-call | flops 4294967296 | bytes 1048576 | tf_op jit(solution)/shard_map/pallas_call | solution.py:47
  76.2 2.6 %all-to-all-start.1 = ((f32[32,1,128]{2,1,0:T(1,128)}), f32[32,1,128]{2,1,0:T(1,128)S(1)}, u32[]{:S(2)}, u32[]{:S(2)}) async-start(f32[32,1,128]{2,1,0:T(1,128)} %get-tuple-element.71), calls=%async_computation.1 | async-start | bytes 32768 | tf_op jit(solution)/shard_map/all_to_all | solution.py:538
  78.8 3.1 %shard_map.177 = (f32[2,512,320]{2,1,0:T(8,128)S(1)}, f32[2,512,320]{2,1,0:T(8,128)S(1)}, bf16[2,640,960]{2,1,0:T(8,128)(2,1)S(1)}) custom-call(f32[2,512,320]{2,1,0:T(8,128)} %get-tuple-element.72.g_far, f32[2,512,320]{2,1,0:T(8,128)} %get-tuple-element.63.feature_far, bf16[2,512,320]{2,1,0:T(8,128)(2,1)} %get-tuple-element.73.relu_far, ...), custom_call_target="tpu_custom_call" | custom-call | flops 4294967296 | bytes 1048576 | tf_op jit(solution)/shard_map/pallas_call | solution.py:47
  81.9 1.5 %copy-done.8 = bf16[2,640,960]{2,1,0:T(8,128)(2,1)} copy-done((bf16[2,640,960]{2,1,0:T(8,128)(2,1)}, bf16[2,640,960]{2,1,0:T(8,128)(2,1)S(1)}, u32[]{:S(2)}) %copy-start.8) | copy-done | bytes 2457624
  83.4 2.5 %all-to-all-done.1.sums_two = f32[32,1,128]{2,1,0:T(1,128)S(1)} async-done(((f32[32,1,128]{2,1,0:T(1,128)}), f32[32,1,128]{2,1,0:T(1,128)S(1)}, u32[]{:S(2)}, u32[]{:S(2)}) %all-to-all-start.1) | async-done | bytes 16416 | tf_op jit(solution)/shard_map/all_to_all | solution.py:538
  86.3 2.6 %collective-permute-start.11 = (bf16[2,64,320]{2,1,0:T(8,128)(2,1)S(1)}, bf16[2,64,320]{2,1,0:T(8,128)(2,1)S(1)}, u32[]{:S(2)}, u32[]{:S(2)}) collective-permute-start(bf16[2,64,320]{2,1,0:T(8,128)(2,1)S(1)} %get-tuple-element.80), channel_id=1, source_target_pairs={{0,4},{4,8},{8,12},{12,16},{16,20},{20,24},{24,28},{1,5},{5,9},{9,... | collective-permute-start | bytes 245768 | tf_op jit(solution)/shard_map/ppermute | solution.py:534
  88.9 1.3 collective-permute-start.12
  90.3 4.1 %shard_map.179 = (f32[3200,320]{1,0:T(8,128)S(1)}, f32[8,320]{1,0:T(8,128)S(1)}, f32[2,512,320]{2,1,0:T(8,128)S(1)}) custom-call(f32[8,128]{1,0:T(8,128)S(1)} %get-tuple-element.78.scalars, f32[8,320]{1,0:T(8,128)S(1)} %get-tuple-element.82.u, bf16[2,512,320]{2,1,0:T(8,128)(2,1)S(1)} %get-tuple-element.79.gz, bf16[2,640,960]{2,1,0:T(8,128)(2,1)S(1)} %copy-done.9, ...), custom_call_target="tpu_custom_call" | custom-call | flops 2147483648 | bytes 1048576 | tf_op jit(solution)/shard_map/pallas_call | solution.py:47
  94.4 1.0 collective-permute-done.12.below
  95.5 8.7 %shard_map.180 = (bf16[17,400,128]{2,1,0:T(8,128)(2,1)S(1)}, bf16[17,400,128]{2,1,0:T(8,128)(2,1)S(1)}) custom-call(s32[3]{0:T(128)S(1)} %pad_add_fusion.place, bf16[2,512,320]{2,1,0:T(8,128)(2,1)S(1)} %get-tuple-element.79.gz, bf16[2,64,320]{2,1,0:T(8,128)(2,1)S(1)} %collective-permute-done.11.above, bf16[2,64,320]{2,1,0:T(8,128)(2,1)S(1)} %collective-permute-done.12.below, ...), custom_call_target="tpu_custom_call" | custom-call | flops 4294967296 | bytes 1048576 | tf_op jit(solution)/shard_map/pallas_call | solution.py:47
  104.2 3.6 %collective-permute-done.13 = bf16[17,400,128]{2,1,0:T(8,128)(2,1)S(1)} collective-permute-done((bf16[17,400,128]{2,1,0:T(8,128)(2,1)S(1)}, bf16[17,400,128]{2,1,0:T(8,128)(2,1)S(1)}, u32[]{:S(2)}, u32[]{:S(2)}) %collective-permute-start.13) | collective-permute-done | bytes 1740832 | tf_op jit(solution)/shard_map/ppermute | solution.py:100
  108.4 2.4 %collective-permute-start.16 = (bf16[8,192,128]{2,1,0:T(8,128)(2,1)S(1)}, bf16[8,192,128]{2,1,0:T(8,128)(2,1)S(1)}, u32[]{:S(2)}, u32[]{:S(2)}) collective-permute-start(bf16[8,192,128]{2,1,0:T(8,128)(2,1)S(1)} %slice.150), channel_id=1, source_target_pairs={{0,4},{4,0},{8,12},{12,8},{16,20},{20,16},{24,28},{28,24},{1,5},{5... | collective-permute-start | bytes 1179656 | tf_op jit(solution)/shard_map/ppermute | solution.py:100
  110.9 0.6 collective-permute-start.14
  111.5 8.8 %collective-permute-done.16 = bf16[8,192,128]{2,1,0:T(8,128)(2,1)S(1)} collective-permute-done((bf16[8,192,128]{2,1,0:T(8,128)(2,1)S(1)}, bf16[8,192,128]{2,1,0:T(8,128)(2,1)S(1)}, u32[]{:S(2)}, u32[]{:S(2)}) %collective-permute-start.16) | collective-permute-done | bytes 393248 | tf_op jit(solution)/shard_map/ppermute | solution.py:100
  120.4 0.6 collective-permute-start.17
  121.0 1.5 %collective-permute-done.14 = bf16[8,208,128]{2,1,0:T(8,128)(2,1)S(1)} collective-permute-done((bf16[8,208,128]{2,1,0:T(8,128)(2,1)S(1)}, bf16[8,208,128]{2,1,0:T(8,128)(2,1)S(1)}, u32[]{:S(2)}, u32[]{:S(2)}) %collective-permute-start.14) | collective-permute-done | bytes 426016 | tf_op jit(solution)/shard_map/ppermute | solution.py:100
  123.0 3.9 %collective-permute-done.17 = bf16[4,192,128]{2,1,0:T(8,128)(2,1)S(1)} collective-permute-done((bf16[4,192,128]{2,1,0:T(8,128)(2,1)S(1)}, bf16[4,192,128]{2,1,0:T(8,128)(2,1)S(1)}, u32[]{:S(2)}, u32[]{:S(2)}) %collective-permute-start.17) | collective-permute-done | bytes 196640 | tf_op jit(solution)/shard_map/ppermute | solution.py:100
  126.9 1.9 %collective-permute-done.15 = bf16[4,208,128]{2,1,0:T(8,128)(2,1)S(1)} collective-permute-done((bf16[4,208,128]{2,1,0:T(8,128)(2,1)S(1)}, bf16[4,208,128]{2,1,0:T(8,128)(2,1)S(1)}, u32[]{:S(2)}, u32[]{:S(2)}) %collective-permute-start.15) | collective-permute-done | bytes 213024 | tf_op jit(solution)/shard_map/ppermute | solution.py:100
  129.0 0.7 collective-permute-start.18
  129.7 1.9 %collective-permute-start.19 = (bf16[1,400,128]{2,1,0:T(8,128)(2,1)S(1)}, bf16[1,400,128]{2,1,0:T(8,128)(2,1)S(1)}, u32[]{:S(2)}, u32[]{:S(2)}) collective-permute-start(bf16[1,400,128]{2,1,0:T(8,128)(2,1)S(1)} %get-tuple-element.99), channel_id=1, source_target_pairs={{0,16},{4,20},{8,24},{12,28},{16,0},{20,4},{24,8},{28,12},{1,17},{... | collective-permute-start | bytes 307208 | tf_op jit(solution)/shard_map/ppermute | solution.py:100
  131.6 1.9 %collective-permute-start.20 = (bf16[1,400,128]{2,1,0:T(8,128)(2,1)S(1)}, bf16[1,400,128]{2,1,0:T(8,128)(2,1)S(1)}, u32[]{:S(2)}, u32[]{:S(2)}) collective-permute-start(bf16[1,400,128]{2,1,0:T(8,128)(2,1)S(1)} %get-tuple-element.98), channel_id=1, source_target_pairs={{0,24},{4,28},{8,16},{12,20},{16,8},{20,12},{24,0},{28,4},{1,25},{... | collective-permute-start | bytes 307208 | tf_op jit(solution)/shard_map/ppermute | solution.py:100
  134.2 0.5 slice.117
  134.7 3.9 %collective-permute-done.19 = bf16[1,400,128]{2,1,0:T(8,128)(2,1)S(1)} collective-permute-done((bf16[1,400,128]{2,1,0:T(8,128)(2,1)S(1)}, bf16[1,400,128]{2,1,0:T(8,128)(2,1)S(1)}, u32[]{:S(2)}, u32[]{:S(2)}) %collective-permute-start.19) | collective-permute-done | bytes 102432 | tf_op jit(solution)/shard_map/ppermute | solution.py:100
  139.0 1.0 multiply_subtract_fusion
  (87 shorter events, 3.3 us)
Async XLA Ops:
  0.6 22.0 %copy-start.19 = (bf16[2,1,77,768]{3,0,2,1:T(2,128)(2,1)S(1)}, bf16[2,1,77,768]{3,0,2,1:T(2,128)(2,1)}, u32[]{:S(2)}) copy-start(bf16[2,1,77,768]{3,0,2,1:T(2,128)(2,1)} %param.17) | copy-start | bytes 709636
  2.0 11.8 %collective-permute-start = (bf16[1,400,128]{2,1,0:T(8,128)(2,1)S(1)}, bf16[1,400,128]{2,1,0:T(8,128)(2,1)S(1)}, u32[]{:S(2)}, u32[]{:S(2)}) collective-permute-start(bf16[1,400,128]{2,1,0:T(8,128)(2,1)S(1)} %maximum_bitcast_fusion), channel_id=1, source_target_pairs={{0,8},{4,12},{8,0},{12,4},{16,24},{20,28},{24,16},{28,20},{1,9},{5... | collective-permute-start | bytes 307208 | tf_op jit(solution)/shard_map/ppermute | solution.py:100
  5.1 10.7 %collective-permute-start.1 = (bf16[1,400,128]{2,1,0:T(8,128)(2,1)S(1)}, bf16[1,400,128]{2,1,0:T(8,128)(2,1)S(1)}, u32[]{:S(2)}, u32[]{:S(2)}) collective-permute-start(bf16[1,400,128]{2,1,0:T(8,128)(2,1)S(1)} %maximum_bitcast_fusion), channel_id=1, source_target_pairs={{0,16},{4,20},{8,24},{12,28},{16,0},{20,4},{24,8},{28,12},{1,17},{... | collective-permute-start | bytes 307208 | tf_op jit(solution)/shard_map/ppermute | solution.py:100
  7.7 8.1 %collective-permute-start.2 = (bf16[1,400,128]{2,1,0:T(8,128)(2,1)S(1)}, bf16[1,400,128]{2,1,0:T(8,128)(2,1)S(1)}, u32[]{:S(2)}, u32[]{:S(2)}) collective-permute-start(bf16[1,400,128]{2,1,0:T(8,128)(2,1)S(1)} %maximum_bitcast_fusion), channel_id=1, source_target_pairs={{0,24},{4,28},{8,16},{12,20},{16,8},{20,12},{24,0},{28,4},{1,25},{... | collective-permute-start | bytes 307208 | tf_op jit(solution)/shard_map/ppermute | solution.py:100
  8.7 7.2 %collective-permute-start.3 = (bf16[2,2,64,192]{3,2,1,0:T(8,128)(2,1)S(1)}, bf16[2,2,64,192]{3,2,1,0:T(8,128)(2,1)S(1)}, u32[]{:S(2)}, u32[]{:S(2)}) collective-permute-start(bf16[2,2,64,192]{3,2,1,0:T(8,128)(2,1)S(1)} %get-tuple-element.96), channel_id=1, source_target_pairs={{0,4},{4,8},{8,12},{12,16},{16,20},{20,24},{24,28},{1,5},{5,9},{9,... | collective-permute-start | bytes 294920 | tf_op jit(solution)/shard_map/ppermute | solution.py:534
  12.3 17.0 %copy-start = (bf16[2,8,64,192]{3,2,1,0:T(8,128)(2,1)S(1)}, bf16[2,8,64,192]{3,2,1,0:T(8,128)(2,1)}, u32[]{:S(2)}) copy-start(bf16[2,8,64,192]{3,2,1,0:T(8,128)(2,1)} %param.15) | copy-start | bytes 1179652
  12.3 17.0 %copy-start.1 = (bf16[2,8,64,320]{3,2,1,0:T(8,128)(2,1)S(1)}, bf16[2,8,64,320]{3,2,1,0:T(8,128)(2,1)}, u32[]{:S(2)}) copy-start(bf16[2,8,64,320]{3,2,1,0:T(8,128)(2,1)} %param.16) | copy-start | bytes 1966084
  12.3 17.0 %copy-start.2 = (bf16[768,320]{0,1:T(8,128)(2,1)S(1)}, bf16[768,320]{0,1:T(8,128)(2,1)}, u32[]{:S(2)}) copy-start(bf16[768,320]{0,1:T(8,128)(2,1)} %param.22) | copy-start | bytes 1474564
  12.3 17.0 %copy-start.3 = (bf16[768,320]{0,1:T(8,128)(2,1)S(1)}, bf16[768,320]{0,1:T(8,128)(2,1)}, u32[]{:S(2)}) copy-start(bf16[768,320]{0,1:T(8,128)(2,1)} %param.23) | copy-start | bytes 1474564
  12.3 17.0 %copy-start.4 = (bf16[320,320]{1,0:T(8,128)(2,1)S(1)}, bf16[320,320]{1,0:T(8,128)(2,1)}, u32[]{:S(2)}) copy-start(bf16[320,320]{1,0:T(8,128)(2,1)} %wq_far.1) | copy-start | bytes 614404
  12.4 17.0 %copy-start.5 = (bf16[320,320]{1,0:T(8,128)(2,1)S(1)}, bf16[320,320]{1,0:T(8,128)(2,1)}, u32[]{:S(2)}) copy-start(bf16[320,320]{1,0:T(8,128)(2,1)} %wo_far.1) | copy-start | bytes 614404
  12.4 7.0 %collective-permute-start.4 = (bf16[2,2,64,192]{3,2,1,0:T(8,128)(2,1)S(1)}, bf16[2,2,64,192]{3,2,1,0:T(8,128)(2,1)S(1)}, u32[]{:S(2)}, u32[]{:S(2)}) collective-permute-start(bf16[2,2,64,192]{3,2,1,0:T(8,128)(2,1)S(1)} %get-tuple-element.95), channel_id=1, source_target_pairs={{4,0},{8,4},{12,8},{16,12},{20,16},{24,20},{28,24},{5,1},{9,5},{13... | collective-permute-start | bytes 294920 | tf_op jit(solution)/shard_map/ppermute | solution.py:534
  19.4 5.7 %collective-permute-start.7 = (bf16[4,192,128]{2,1,0:T(8,128)(2,1)S(1)}, bf16[4,192,128]{2,1,0:T(8,128)(2,1)S(1)}, u32[]{:S(2)}, u32[]{:S(2)}) collective-permute-start(bf16[4,192,128]{2,1,0:T(8,128)(2,1)S(1)} %slice.116), channel_id=1, source_target_pairs={{0,2},{1,3},{2,0},{3,1},{4,6},{5,7},{6,4},{7,5},{8,10},{9,11},{10,... | collective-permute-start | bytes 589832 | tf_op jit(solution)/shard_map/ppermute | solution.py:100
  21.0 8.2 %collective-permute-start.5 = (bf16[4,208,128]{2,1,0:T(8,128)(2,1)S(1)}, bf16[4,208,128]{2,1,0:T(8,128)(2,1)S(1)}, u32[]{:S(2)}, u32[]{:S(2)}) collective-permute-start(bf16[4,208,128]{2,1,0:T(8,128)(2,1)S(1)} %slice.115), channel_id=1, source_target_pairs={{0,4},{4,0},{8,12},{12,8},{16,20},{20,16},{24,28},{28,24},{1,5},{5... | collective-permute-start | bytes 638984 | tf_op jit(solution)/shard_map/ppermute | solution.py:100
  25.2 9.8 %collective-permute-start.8 = (bf16[8,192,128]{2,1,0:T(8,128)(2,1)S(1)}, bf16[8,192,128]{2,1,0:T(8,128)(2,1)S(1)}, u32[]{:S(2)}, u32[]{:S(2)}) collective-permute-start(bf16[8,192,128]{2,1,0:T(8,128)(2,1)S(1)} %pad_maximum_fusion.5), channel_id=1, source_target_pairs={{0,4},{4,0},{8,12},{12,8},{16,20},{20,16},{24,28},{28,24},{1,5},{5... | collective-permute-start | bytes 1179656 | tf_op jit(solution)/shard_map/ppermute | solution.py:100
  29.2 8.2 %collective-permute-start.6 = (bf16[8,208,128]{2,1,0:T(8,128)(2,1)S(1)}, bf16[8,208,128]{2,1,0:T(8,128)(2,1)S(1)}, u32[]{:S(2)}, u32[]{:S(2)}) collective-permute-start(bf16[8,208,128]{2,1,0:T(8,128)(2,1)S(1)} %pad_maximum_fusion.3), channel_id=1, source_target_pairs={{0,2},{1,3},{2,0},{3,1},{4,6},{5,7},{6,4},{7,5},{8,10},{9,11},{10,... | collective-permute-start | bytes 1277960 | tf_op jit(solution)/shard_map/ppermute | solution.py:100
  30.7 0.7 copy-start.14
  31.4 0.7 copy-start.15
  32.1 0.7 copy-start.16
  32.7 0.7 copy-start.17
  33.4 4.1 %copy-start.10 = (bf16[2,768,576]{2,1,0:T(8,128)(2,1)}, bf16[2,768,576]{2,1,0:T(8,128)(2,1)S(1)}, u32[]{:S(2)}) copy-start(bf16[2,768,576]{2,1,0:T(8,128)(2,1)S(1)} %get-tuple-element.60.c3_far) | copy-start | bytes 5308420
  33.4 4.2 %copy-start.11 = (bf16[2,320,512]{2,1,0:T(8,128)(2,1)}, bf16[2,320,512]{2,1,0:T(8,128)(2,1)S(1)}, u32[]{:S(2)}) copy-start(bf16[2,320,512]{2,1,0:T(8,128)(2,1)S(1)} %get-tuple-element.64.resid_far) | copy-start | bytes 1966084
  33.4 4.2 %copy-start.12 = (bf16[2,8,80,40]{3,2,1,0:T(8,128)(2,1)}, bf16[2,8,80,40]{3,2,1,0:T(8,128)(2,1)S(1)}, u32[]{:S(2)}) copy-start(bf16[2,8,80,40]{3,2,1,0:T(8,128)(2,1)S(1)} %get-tuple-element.66.keys_far) | copy-start | bytes 307204
  33.4 4.2 %copy-start.13 = (bf16[2,8,80,40]{3,2,1,0:T(8,128)(2,1)}, bf16[2,8,80,40]{3,2,1,0:T(8,128)(2,1)S(1)}, u32[]{:S(2)}) copy-start(bf16[2,8,80,40]{3,2,1,0:T(8,128)(2,1)S(1)} %get-tuple-element.69.values_far) | copy-start | bytes 307204
  33.4 4.8 %copy-start.22 = (f32[1000]{0:T(1024)S(1)}, f32[1000]{0:T(1024)}, u32[]{:S(2)}) copy-start(f32[1000]{0:T(1024)} %constant.43.clone) | copy-start | bytes 12004
  33.4 4.8 %copy-start.23 = (s32[2,1]{0,1:T(1,128)S(1)}, s32[2,1]{0,1:T(1,128)}, u32[]{:S(2)}) copy-start(s32[2,1]{0,1:T(1,128)} %param.19) | copy-start | bytes 28
  37.5 3.7 %collective-permute-start.9 = (bf16[16,208,128]{2,1,0:T(8,128)(2,1)S(1)}, bf16[16,208,128]{2,1,0:T(8,128)(2,1)S(1)}, u32[]{:S(2)}, u32[]{:S(2)}) collective-permute-start(bf16[16,208,128]{2,1,0:T(8,128)(2,1)S(1)} %pad_maximum_fusion.1.own_a), channel_id=1, source_target_pairs={{0,1},{1,0},{2,3},{3,2},{4,5},{5,4},{6,7},{7,6},{8,9},{9,8},{10,11... | collective-permute-start | bytes 2555912 | tf_op jit(solution)/shard_map/ppermute | solution.py:100
  37.6 3.6 %collective-permute-start.10 = (bf16[16,192,128]{2,1,0:T(8,128)(2,1)S(1)}, bf16[16,192,128]{2,1,0:T(8,128)(2,1)}, u32[]{:S(2)}, u32[]{:S(2)}) collective-permute-start(bf16[16,192,128]{2,1,0:T(8,128)(2,1)S(1)} %pad_maximum_fusion.2.own_b), channel_id=1, source_target_pairs={{0,1},{1,0},{2,3},{3,2},{4,5},{5,4},{6,7},{7,6},{8,9},{9,8},{10,11... | collective-permute-start | bytes 2359304 | tf_op jit(solution)/shard_map/ppermute | solution.py:100
  38.4 28.3 %copy-start.6 = (f32[2,8,64,4]{2,3,1,0:T(4,128)S(1)}, f32[2,8,64,4]{2,3,1,0:T(4,128)}, u32[]{:S(2)}) copy-start(f32[2,8,64,4]{2,3,1,0:T(4,128)} %param.18) | copy-start | bytes 49156
  38.4 28.3 %copy-start.7 = (bf16[320,4]{0,1:T(4,128)(2,1)S(1)}, bf16[320,4]{0,1:T(4,128)(2,1)}, u32[]{:S(2)}) copy-start(bf16[320,4]{0,1:T(4,128)(2,1)} %param.25) | copy-start | bytes 7684
  76.2 9.6 %all-to-all-start.1 = ((f32[32,1,128]{2,1,0:T(1,128)}), f32[32,1,128]{2,1,0:T(1,128)S(1)}, u32[]{:S(2)}, u32[]{:S(2)}) async-start(f32[32,1,128]{2,1,0:T(1,128)} %get-tuple-element.71), calls=%async_computation.1 | async-start | bytes 32768 | tf_op jit(solution)/shard_map/all_to_all | solution.py:538
  81.9 1.5 %copy-start.8 = (bf16[2,640,960]{2,1,0:T(8,128)(2,1)}, bf16[2,640,960]{2,1,0:T(8,128)(2,1)S(1)}, u32[]{:S(2)}) copy-start(bf16[2,640,960]{2,1,0:T(8,128)(2,1)S(1)} %get-tuple-element.83.x3) | copy-start | bytes 7372804
  85.8 4.4 %copy-start.9 = (bf16[2,640,960]{2,1,0:T(8,128)(2,1)S(1)}, bf16[2,640,960]{2,1,0:T(8,128)(2,1)}, u32[]{:S(2)}) copy-start(bf16[2,640,960]{2,1,0:T(8,128)(2,1)} %copy-done.8) | copy-start | bytes 7372804
  86.3 8.1 %collective-permute-start.11 = (bf16[2,64,320]{2,1,0:T(8,128)(2,1)S(1)}, bf16[2,64,320]{2,1,0:T(8,128)(2,1)S(1)}, u32[]{:S(2)}, u32[]{:S(2)}) collective-permute-start(bf16[2,64,320]{2,1,0:T(8,128)(2,1)S(1)} %get-tuple-element.80), channel_id=1, source_target_pairs={{0,4},{4,8},{8,12},{12,16},{16,20},{20,24},{24,28},{1,5},{5,9},{9,... | collective-permute-start | bytes 245768 | tf_op jit(solution)/shard_map/ppermute | solution.py:534
  88.9 6.5 %collective-permute-start.12 = (bf16[2,64,320]{2,1,0:T(8,128)(2,1)S(1)}, bf16[2,64,320]{2,1,0:T(8,128)(2,1)S(1)}, u32[]{:S(2)}, u32[]{:S(2)}) collective-permute-start(bf16[2,64,320]{2,1,0:T(8,128)(2,1)S(1)} %get-tuple-element.81), channel_id=1, source_target_pairs={{4,0},{8,4},{12,8},{16,12},{20,16},{24,20},{28,24},{5,1},{9,5},{13... | collective-permute-start | bytes 245768 | tf_op jit(solution)/shard_map/ppermute | solution.py:534
  104.2 3.7 %collective-permute-start.13 = (bf16[17,400,128]{2,1,0:T(8,128)(2,1)S(1)}, bf16[17,400,128]{2,1,0:T(8,128)(2,1)S(1)}, u32[]{:S(2)}, u32[]{:S(2)}) collective-permute-start(bf16[17,400,128]{2,1,0:T(8,128)(2,1)S(1)} %get-tuple-element.89), channel_id=1, source_target_pairs={{0,1},{1,0},{2,3},{3,2},{4,5},{5,4},{6,7},{7,6},{8,9},{9,8},{10,11... | collective-permute-start | bytes 5222408 | tf_op jit(solution)/shard_map/ppermute | solution.py:100
  108.4 11.9 %collective-permute-start.16 = (bf16[8,192,128]{2,1,0:T(8,128)(2,1)S(1)}, bf16[8,192,128]{2,1,0:T(8,128)(2,1)S(1)}, u32[]{:S(2)}, u32[]{:S(2)}) collective-permute-start(bf16[8,192,128]{2,1,0:T(8,128)(2,1)S(1)} %slice.150), channel_id=1, source_target_pairs={{0,4},{4,0},{8,12},{12,8},{16,20},{20,16},{24,28},{28,24},{1,5},{5... | collective-permute-start | bytes 1179656 | tf_op jit(solution)/shard_map/ppermute | solution.py:100
  110.9 11.6 %collective-permute-start.14 = (bf16[8,208,128]{2,1,0:T(8,128)(2,1)S(1)}, bf16[8,208,128]{2,1,0:T(8,128)(2,1)S(1)}, u32[]{:S(2)}, u32[]{:S(2)}) collective-permute-start(bf16[8,208,128]{2,1,0:T(8,128)(2,1)S(1)} %slice.146), channel_id=1, source_target_pairs={{0,2},{1,3},{2,0},{3,1},{4,6},{5,7},{6,4},{7,5},{8,10},{9,11},{10,... | collective-permute-start | bytes 1277960 | tf_op jit(solution)/shard_map/ppermute | solution.py:100
  120.4 6.5 %collective-permute-start.17 = (bf16[4,192,128]{2,1,0:T(8,128)(2,1)S(1)}, bf16[4,192,128]{2,1,0:T(8,128)(2,1)S(1)}, u32[]{:S(2)}, u32[]{:S(2)}) collective-permute-start(bf16[4,192,128]{2,1,0:T(8,128)(2,1)S(1)} %slice.191), channel_id=1, source_target_pairs={{0,2},{1,3},{2,0},{3,1},{4,6},{5,7},{6,4},{7,5},{8,10},{9,11},{10,... | collective-permute-start | bytes 589832 | tf_op jit(solution)/shard_map/ppermute | solution.py:100
  122.6 6.2 %collective-permute-start.15 = (bf16[4,208,128]{2,1,0:T(8,128)(2,1)S(1)}, bf16[4,208,128]{2,1,0:T(8,128)(2,1)S(1)}, u32[]{:S(2)}, u32[]{:S(2)}) collective-permute-start(bf16[4,208,128]{2,1,0:T(8,128)(2,1)S(1)} %slice.190), channel_id=1, source_target_pairs={{0,4},{4,0},{8,12},{12,8},{16,20},{20,16},{24,28},{28,24},{1,5},{5... | collective-permute-start | bytes 638984 | tf_op jit(solution)/shard_map/ppermute | solution.py:100
  129.0 10.0 %copy-start.18 = (f32[49320]{0:T(1024)S(1)}, f32[49320]{0:T(1024)}, u32[]{:S(2)}) copy-start(f32[49320]{0:T(1024)} %param.26) | copy-start | bytes 591844
  129.0 10.0 %copy-start.20 = (f32[49320]{0:T(1024)S(1)}, f32[49320]{0:T(1024)}, u32[]{:S(2)}) copy-start(f32[49320]{0:T(1024)} %param.28) | copy-start | bytes 591844
  129.0 10.0 %copy-start.21 = (f32[49320]{0:T(1024)S(1)}, f32[49320]{0:T(1024)}, u32[]{:S(2)}) copy-start(f32[49320]{0:T(1024)} %param.27) | copy-start | bytes 591844
  129.0 5.7 %collective-permute-start.18 = (bf16[1,400,128]{2,1,0:T(8,128)(2,1)S(1)}, bf16[1,400,128]{2,1,0:T(8,128)(2,1)S(1)}, u32[]{:S(2)}, u32[]{:S(2)}) collective-permute-start(bf16[1,400,128]{2,1,0:T(8,128)(2,1)S(1)} %get-tuple-element.97), channel_id=1, source_target_pairs={{0,8},{4,12},{8,0},{12,4},{16,24},{20,28},{24,16},{28,20},{1,9},{5... | collective-permute-start | bytes 307208 | tf_op jit(solution)/shard_map/ppermute | solution.py:100
  129.7 9.0 %collective-permute-start.19 = (bf16[1,400,128]{2,1,0:T(8,128)(2,1)S(1)}, bf16[1,400,128]{2,1,0:T(8,128)(2,1)S(1)}, u32[]{:S(2)}, u32[]{:S(2)}) collective-permute-start(bf16[1,400,128]{2,1,0:T(8,128)(2,1)S(1)} %get-tuple-element.99), channel_id=1, source_target_pairs={{0,16},{4,20},{8,24},{12,28},{16,0},{20,4},{24,8},{28,12},{1,17},{... | collective-permute-start | bytes 307208 | tf_op jit(solution)/shard_map/ppermute | solution.py:100
  131.6 7.0 %collective-permute-start.20 = (bf16[1,400,128]{2,1,0:T(8,128)(2,1)S(1)}, bf16[1,400,128]{2,1,0:T(8,128)(2,1)S(1)}, u32[]{:S(2)}, u32[]{:S(2)}) collective-permute-start(bf16[1,400,128]{2,1,0:T(8,128)(2,1)S(1)} %get-tuple-element.98), channel_id=1, source_target_pairs={{0,24},{4,28},{8,16},{12,20},{16,8},{20,12},{24,0},{28,4},{1,25},{... | collective-permute-start | bytes 307208 | tf_op jit(solution)/shard_map/ppermute | solution.py:100

commit v3 on v2

--- a/solution.py
+++ b/solution.py
@@ -134,8 +134,8 @@
     flat = lax.dynamic_slice(flat, (plan.channels - shift,), (total,))
     packed = pack_rows(flat.reshape(plan.rows, plan.channels).astype(BF))[None]
     packed = spread(packed, plan.group_z)
-    packed, edges = lax.optimization_barrier((packed, edges()))
     part_a, part_b = packed[:, : plan.part_a], packed[:, plan.part_a :]
+    part_a, edges = lax.optimization_barrier((part_a, edges()))
     part_a, part_b = spread(part_a, plan.group_x), spread(part_b, plan.group_y)
     part_a, part_b = spread(part_a, plan.group_y), spread(part_b, plan.group_x)
     part_a, part_b, ready = lax.optimization_barrier((part_a, part_b, prepare(*edges)))
@@ -170,6 +170,11 @@
     return jnp.concatenate([left, values, right], axis=1).astype(BF)
 
 
+def neighbours(place, first, second):
+    even = jnp.full((1, 1), place[3], jnp.int32) == 0
+    return jnp.where(even, second, first), jnp.where(even, first, second)
+
+
 def lane_pick(row, lane):
     ids = lax.broadcasted_iota(jnp.int32, row.shape, 1)
     return jnp.sum(jnp.where(ids == lane, row, 0.0))
@@ -184,7 +189,7 @@
 
 
 def prepare_kernel(
-    cols, heads, cond, low, high, context, wk_t, wv_t, resid, wq, wo,
+    cols, heads, place, cond, first, second, context, wk_t, wv_t, resid, wq, wo,
     c3, keys, keys_t, values, values_t, resid_t, wq_t, wo_t,
 ):
     images = cond.shape[0]
@@ -192,7 +197,8 @@
     room = keys.shape[2]
     pad = jnp.zeros((channels, LANES - words), F32)
     for i in range(images):
-        wide = jnp.concatenate([low[i], cond[i], high[i]], axis=0).astype(F32)
+        low, high = neighbours(place, first[i].astype(F32), second[i].astype(F32))
+        wide = jnp.concatenate([low, cond[i].astype(F32), high], axis=0)
         c3[i] = three_columns(wide, cols)
         for weight, flat, tall in ((wk_t, keys, keys_t), (wv_t, values, values_t)):
             turned = jnp.concatenate([mm_nt(weight[...], context[i]), pad], axis=1)
@@ -247,9 +253,9 @@
     for copy in load:
         copy.wait()
     a_one = [
-        sum(
-            mm(c3[i, dy * cols : dy * cols + more], weights[dy * kept_in : (dy + 1) * kept_in])
-            for dy in range(3)
+        mm(
+            jnp.concatenate([c3[i, dy * cols : dy * cols + more] for dy in range(3)], axis=1),
+            weights[:n_in],
         )
         for i in range(images)
     ]
@@ -408,7 +414,7 @@
 
 
 def solve_kernel(
-    cols, elements, sums, sums_two, by_g, by_feature, scalars, gz, edge_top, edge_bottom
+    cols, elements, place, sums, sums_two, by_g, by_feature, scalars, gz, to_pair, to_other
 ):
     images, tokens, channels = gz.shape
     scale = norm_of(jnp.sum(sums[...], axis=0), elements)
@@ -417,10 +423,11 @@
     pairs = [(0, jnp.full((1, 1), lane_pick(line, 0), F32)), (1, pull), (2, scale)]
     scalars[...] = jnp.broadcast_to(lane_row(pairs), scalars.shape)
     for i in range(images):
-        back = (by_g[i] - pull * by_feature[i]).astype(BF)
-        gz[i] = back
-        edge_top[i] = back[:cols]
-        edge_bottom[i] = back[tokens - cols :]
+        back = by_g[i] - pull * by_feature[i]
+        gz[i] = back.astype(BF)
+        top, bottom = back[:cols], back[tokens - cols :]
+        pair, other = neighbours(place, top, bottom)
+        to_pair[i], to_other[i] = pair.astype(BF), other.astype(BF)
 
 
 def block_weight_kernel(
@@ -471,7 +478,7 @@
 
 
 def input_kernel(
-    plan, cols, place, gz, above, below, g_f, d_block, d_rows, w1t_far, c3_far,
+    plan, cols, place, gz, first, second, g_f, d_block, d_rows, w1t_far, c3_far,
     keep, send, table, w1t, c3, sems,
 ):
     me = place[0]
@@ -494,7 +501,8 @@
             table[low:high] = d_block[low - n_in : high - n_in]
     wide = []
     for i in range(images):
-        part = jnp.concatenate([above[i], gz[i], below[i]], axis=0).astype(F32)
+        above, below = neighbours(place, first[i].astype(F32), second[i].astype(F32))
+        part = jnp.concatenate([above, gz[i].astype(F32), below], axis=0)
         wide.append(three_columns(part, cols))
     load.wait()
     db_in = jnp.zeros((1, channels), F32)
@@ -528,10 +536,12 @@
     return jnp.sum(jnp.where(hit_table, lookup[None, :], 0.0), axis=1)
 
 
-def shift_rows(value, step):
+def trade_rows(first, second):
     count = lax.axis_size("sp")
-    pairs = [(i, i + step) for i in range(count) if 0 <= i + step < count]
-    return lax.ppermute(value, "sp", pairs)
+    near = [(i, i ^ 1) for i in range(count)]
+    far = [(i, i + 1 if i % 2 else i - 1) for i in range(count)]
+    far = [(i, j) for i, j in far if 0 <= j < count]
+    return lax.ppermute(first, "sp", near), lax.ppermute(second, "sp", far)
 
 
 def everywhere(payload):
@@ -560,17 +570,19 @@
             at_sp * hd + lax.axis_index("hd"),
             (at_sp == 0).astype(jnp.int32),
             (at_sp == sp - 1).astype(jnp.int32),
+            at_sp % 2,
         ]
     )
     snr = snr_weights(timesteps.reshape(-1))
     wide, kept, kept_in = tokens + 2 * cols, 3 * channels, 3 * in_chan
 
     def edges():
-        low = shift_rows(cond[:, row_count - 2 :], 1).reshape(images, 2 * cols, in_chan)
-        high = shift_rows(cond[:, :2], -1).reshape(images, 2 * cols, in_chan)
-        return low, high
-
-    def prepare(low, high):
+        top, bottom = cond[:, :2], cond[:, row_count - 2 :]
+        even = at_sp % 2 == 0
+        pair = trade_rows(jnp.where(even, bottom, top), jnp.where(even, top, bottom))
+        return [rows.reshape(images, 2 * cols, in_chan) for rows in pair]
+
+    def prepare(first, second):
         return call(
             functools.partial(prepare_kernel, cols, heads),
             [
@@ -584,11 +596,12 @@
                 ((channels, channels), BF),
             ],
             [
-                cond.reshape(images, tokens, in_chan), low, high,
+                place, cond.reshape(images, tokens, in_chan), first, second,
                 context.reshape(images, words, -1), key_weight.T, value_weight.T,
                 resid.reshape(images, tokens, channels), query_weight, out_weight,
             ],
-            free=(0, 3, 4, 5, 6, 7, 8),
+            smem=(0,),
+            free=(1, 4, 5, 6, 7, 8, 9),
             far_like=(0, 1, 2, 3, 4, 5, 6, 7),
             flops=4 << 30,
         )
@@ -670,7 +683,7 @@
         far=(0, 1, 2, 3, 4),
         flops=4 << 30,
     )
-    scalars, gz, edge_top, edge_bottom = call(
+    scalars, gz, to_pair, to_other = call(
         functools.partial(solve_kernel, cols, elements),
         [
             ((8, LANES), F32),
@@ -678,11 +691,11 @@
             ((images, cols, channels), BF),
             ((images, cols, channels), BF),
         ],
-        [sums, sums_two, by_g, by_feature],
+        [place, sums, sums_two, by_g, by_feature],
+        smem=(0,),
         flops=1 << 29,
     )
-    above = shift_rows(edge_bottom, 1)
-    below = shift_rows(edge_top, -1)
+    first, second = trade_rows(to_pair, to_other)
     d_block, d_rows, g_f = call(
         functools.partial(block_weight_kernel, cols),
         [((n_one + n_two, channels), F32), ((8, channels), F32), (per_image, F32)],
@@ -702,7 +715,7 @@
             ((plan.half + 1, plan.packed, LANES), BF),
             ((plan.half + 1, plan.packed, LANES), BF),
         ],
-        [place, gz, above, below, g_f, d_block, d_rows, w1t, c3],
+        [place, gz, first, second, g_f, d_block, d_rows, w1t, c3],
         scratch=[
             VMEM((plan.table, channels), F32),
             VMEM((n_one, channels), BF),

time: 140 us -> 134 us (0.957)
  starting transfers between devices: 31.1 us -> 28.9 us
  waiting for transfers between devices: 44.2 us -> 42 us
  local copies, waits for them, and re-layouts: 7.51 us -> 5.78 us
  blocking collectives: 13.4 us -> 12 us
    ppermute x4, starting transfers between devices: 8.94 us -> 3.71 us  [trade_rows(): return (lax.ppermute(first, 'sp', near), lax.ppermute(second, 'sp', far))]
    ppermute x4, waiting for transfers between devices: 4.53 us -> 0.01 us  [trade_rows(): return (lax.ppermute(first, 'sp', near), lax.ppermute(second, 'sp', far))]
    ppermute x17, starting transfers between devices: 19.6 us -> 22.6 us  [swap(): lax.ppermute(value, axis, [(i, i ^ step * stride) for i in range(count)])]
    ppermute x17, waiting for transfers between devices: 37.3 us -> 39.5 us  [swap(): lax.ppermute(value, axis, [(i, i ^ step * stride) for i in range(count)])]
    all_to_all x1, blocking collectives: 13.4 us -> 12 us  [everywhere(): return lax.all_to_all(payload, ('sp', 'hd'), 0, 0, tiled=True)]
  transfers between devices with their start and end apart: 22 -> 22, of which waited for: 15 -> 13; matrix products, arithmetic and copies ran while one was open for 2% -> 2% of each run, Pallas kernels for 6% -> 7%
where the time goes in v3:
time: 134 us
  waiting for transfers between devices  42 us (31%)
  Pallas kernels  39.8 us (30%)
  starting transfers between devices  28.9 us (22%)
  blocking collectives  12 us (9%)
  local copies, waits for them, and re-layouts  5.78 us (4%)
  other arithmetic  3.54 us (3%)
  between operations  1.91 us (1%)
    pallas_call x7, Pallas kernels, call(): pl.pallas_call(kernel, out_shape=[jax.ShapeDtypeStruct(*o) if i in far_li...  39.8 us
    ppermute x17, waiting for transfers between devices, swap(): lax.ppermute(value, axis, [(i, i ^ step * stride) for i in range(count)])  39.5 us
    ppermute x17, starting transfers between devices, swap(): lax.ppermute(value, axis, [(i, i ^ step * stride) for i in range(count)])  22.6 us
    all_to_all x1, blocking collectives, everywhere(): return lax.all_to_all(payload, ('sp', 'hd'), 0, 0, tiled=True)  12 us
    ppermute x4, starting transfers between devices, trade_rows(): return (lax.ppermute(first, 'sp', near), lax.ppermute(second, 'sp', far))  3.71 us
    unnamed x49, local copies, waits for them, and re-layouts  3.6 us
  transfers between devices with their start and end apart: 22, of which 13 were waited for; matrix products, arithmetic and copies ran while one was open for 2% of the time, Pallas kernels for 7%

profile of v3, /device:TPU:0, one launch (start us, length us, event | category | flops | bytes accessed | tf_op | source)
XLA Modules:
  0.0 133.9 jit_solution(6877848122675403256)
XLA Ops:
  0.7 1.1 fusion.1
  2.0 3.0 %collective-permute-start = (bf16[1,400,128]{2,1,0:T(8,128)(2,1)S(1)}, bf16[1,400,128]{2,1,0:T(8,128)(2,1)S(1)}, u32[]{:S(2)}, u32[]{:S(2)}) collective-permute-start(bf16[1,400,128]{2,1,0:T(8,128)(2,1)S(1)} %maximum_bitcast_fusion), channel_id=1, source_target_pairs={{0,8},{4,12},{8,0},{12,4},{16,24},{20,28},{24,16},{28,20},{1,9},{5... | collective-permute-start | bytes 307208 | tf_op jit(solution)/shard_map/ppermute | solution.py:100
  5.1 2.6 %collective-permute-start.1 = (bf16[1,400,128]{2,1,0:T(8,128)(2,1)S(1)}, bf16[1,400,128]{2,1,0:T(8,128)(2,1)S(1)}, u32[]{:S(2)}, u32[]{:S(2)}) collective-permute-start(bf16[1,400,128]{2,1,0:T(8,128)(2,1)S(1)} %maximum_bitcast_fusion), channel_id=1, source_target_pairs={{0,16},{4,20},{8,24},{12,28},{16,0},{20,4},{24,8},{28,12},{1,17},{... | collective-permute-start | bytes 307208 | tf_op jit(solution)/shard_map/ppermute | solution.py:100
  7.7 1.0 broadcast_select_fusion
  8.7 1.8 %collective-permute-start.3 = (bf16[2,2,64,192]{3,2,1,0:T(8,128)(2,1)S(1)}, bf16[2,2,64,192]{3,2,1,0:T(8,128)(2,1)S(1)}, u32[]{:S(2)}, u32[]{:S(2)}) collective-permute-start(bf16[2,2,64,192]{3,2,1,0:T(8,128)(2,1)S(1)} %get-tuple-element.96), channel_id=1, source_target_pairs={{0,4},{4,0},{8,12},{12,8},{16,20},{20,16},{24,28},{28,24},{1,5},{5... | collective-permute-start | bytes 294920 | tf_op jit(solution)/shard_map/ppermute | solution.py:544
  10.4 0.7 collective-permute-start.4
  11.2 4.7 %collective-permute-done.1 = bf16[1,400,128]{2,1,0:T(8,128)(2,1)S(1)} collective-permute-done((bf16[1,400,128]{2,1,0:T(8,128)(2,1)S(1)}, bf16[1,400,128]{2,1,0:T(8,128)(2,1)S(1)}, u32[]{:S(2)}, u32[]{:S(2)}) %collective-permute-start.1) | collective-permute-done | bytes 102432 | tf_op jit(solution)/shard_map/ppermute | solution.py:100
  15.9 1.6 %collective-permute-start.7 = (bf16[4,192,128]{2,1,0:T(8,128)(2,1)S(1)}, bf16[4,192,128]{2,1,0:T(8,128)(2,1)S(1)}, u32[]{:S(2)}, u32[]{:S(2)}) collective-permute-start(bf16[4,192,128]{2,1,0:T(8,128)(2,1)S(1)} %pad_maximum_fusion.6), channel_id=1, source_target_pairs={{0,2},{1,3},{2,0},{3,1},{4,6},{5,7},{6,4},{7,5},{8,10},{9,11},{10,... | collective-permute-start | bytes 589832 | tf_op jit(solution)/shard_map/ppermute | solution.py:100
  17.6 1.9 %collective-permute-start.5 = (bf16[4,208,128]{2,1,0:T(8,128)(2,1)S(1)}, bf16[4,208,128]{2,1,0:T(8,128)(2,1)S(1)}, u32[]{:S(2)}, u32[]{:S(2)}) collective-permute-start(bf16[4,208,128]{2,1,0:T(8,128)(2,1)S(1)} %slice.144), channel_id=1, source_target_pairs={{0,4},{4,0},{8,12},{12,8},{16,20},{20,16},{24,28},{28,24},{1,5},{5... | collective-permute-start | bytes 638984 | tf_op jit(solution)/shard_map/ppermute | solution.py:100
  19.6 2.1 %collective-permute-done.7 = bf16[4,192,128]{2,1,0:T(8,128)(2,1)S(1)} collective-permute-done((bf16[4,192,128]{2,1,0:T(8,128)(2,1)S(1)}, bf16[4,192,128]{2,1,0:T(8,128)(2,1)S(1)}, u32[]{:S(2)}, u32[]{:S(2)}) %collective-permute-start.7) | collective-permute-done | bytes 196640 | tf_op jit(solution)/shard_map/ppermute | solution.py:100
  21.7 1.5 %collective-permute-start.8 = (bf16[8,192,128]{2,1,0:T(8,128)(2,1)S(1)}, bf16[8,192,128]{2,1,0:T(8,128)(2,1)S(1)}, u32[]{:S(2)}, u32[]{:S(2)}) collective-permute-start(bf16[8,192,128]{2,1,0:T(8,128)(2,1)S(1)} %pad_maximum_fusion.5), channel_id=1, source_target_pairs={{0,4},{4,0},{8,12},{12,8},{16,20},{20,16},{24,28},{28,24},{1,5},{5... | collective-permute-start | bytes 1179656 | tf_op jit(solution)/shard_map/ppermute | solution.py:100
  23.2 2.7 %collective-permute-done.5 = bf16[4,208,128]{2,1,0:T(8,128)(2,1)S(1)} collective-permute-done((bf16[4,208,128]{2,1,0:T(8,128)(2,1)S(1)}, bf16[4,208,128]{2,1,0:T(8,128)(2,1)S(1)}, u32[]{:S(2)}, u32[]{:S(2)}) %collective-permute-start.5) | collective-permute-done | bytes 213024 | tf_op jit(solution)/shard_map/ppermute | solution.py:100
  25.9 1.4 %collective-permute-start.6 = (bf16[8,208,128]{2,1,0:T(8,128)(2,1)S(1)}, bf16[8,208,128]{2,1,0:T(8,128)(2,1)S(1)}, u32[]{:S(2)}, u32[]{:S(2)}) collective-permute-start(bf16[8,208,128]{2,1,0:T(8,128)(2,1)S(1)} %pad_maximum_fusion.3), channel_id=1, source_target_pairs={{0,2},{1,3},{2,0},{3,1},{4,6},{5,7},{6,4},{7,5},{8,10},{9,11},{10,... | collective-permute-start | bytes 1277960 | tf_op jit(solution)/shard_map/ppermute | solution.py:100
  27.3 1.9 %shard_map.174 = (bf16[2,768,576]{2,1,0:T(8,128)(2,1)S(1)}, bf16[2,8,80,40]{3,2,1,0:T(8,128)(2,1)S(1)}, bf16[2,8,40,80]{3,2,1,0:T(8,128)(2,1)S(1)}, bf16[2,8,80,...) custom-call(s32[4]{0:T(128)S(1)} %pad_add_fusion.place, ...), custom_call_target="tpu_custom_call" | custom-call | flops 4294967296 | bytes 1048576 | tf_op jit(solution)/shard_map/pallas_call | solution.py:47
  29.2 1.3 copy-done.10
  30.5 0.7 copy-done.15
  31.3 1.6 %collective-permute-done.8 = bf16[8,192,128]{2,1,0:T(8,128)(2,1)S(1)} collective-permute-done((bf16[8,192,128]{2,1,0:T(8,128)(2,1)S(1)}, bf16[8,192,128]{2,1,0:T(8,128)(2,1)S(1)}, u32[]{:S(2)}, u32[]{:S(2)}) %collective-permute-start.8) | collective-permute-done | bytes 393248 | tf_op jit(solution)/shard_map/ppermute | solution.py:100
  32.9 2.0 %collective-permute-done.6 = bf16[8,208,128]{2,1,0:T(8,128)(2,1)S(1)} collective-permute-done((bf16[8,208,128]{2,1,0:T(8,128)(2,1)S(1)}, bf16[8,208,128]{2,1,0:T(8,128)(2,1)S(1)}, u32[]{:S(2)}, u32[]{:S(2)}) %collective-permute-start.6) | collective-permute-done | bytes 426016 | tf_op jit(solution)/shard_map/ppermute | solution.py:100
  35.1 0.5 collective-permute-start.10
  35.8 2.8 %collective-permute-done.10.other_b = bf16[16,192,128]{2,1,0:T(8,128)(2,1)S(1)} collective-permute-done((bf16[16,192,128]{2,1,0:T(8,128)(2,1)S(1)}, bf16[16,192,128]{2,1,0:T(8,128)(2,1)S(1)}, u32[]{:S(2)}, u32[]{:S(2)}) %collective-permute-start.10) | collective-permute-done | bytes 786464 | tf_op jit(solution)/shard_map/ppermute | solution.py:100
  38.6 11.2 %shard_map.175 = (bf16[2880,320]{1,0:T(8,128)(2,1)}, bf16[320,320]{1,0:T(8,128)(2,1)}, f32[8,320]{1,0:T(8,128)S(1)}, f32[2,512,320]{2,1,0:T(8,128)}, bf16[2,512,...) custom-call(s32[4]{0:T(128)S(1)} %pad_add_fusion.place, f32[2]{0:T(128)S(1)} %fusion.7.snr, ...), custom_call_target="tpu_custom_call" | custom-call | flops 4294967296 | bytes 1048576 | tf_op jit(solution)/shard_map/pallas_call | solution.py:47
  49.8 12.0 %all_to_all.10.sums = f32[32,1,128]{2,1,0:T(1,128)S(1)} all-to-all(f32[32,1,128]{2,1,0:T(1,128)S(1)} %get-tuple-element.61), channel_id=1, replica_groups=mesh['sp'=8,'hd'=4] {'sp','hd'}, dimensions={0} | all-to-all | bytes 32768 | tf_op jit(solution)/shard_map/all_to_all | solution.py:548
  61.8 9.5 %shard_map.176 = (f32[2,512,320]{2,1,0:T(8,128)}, f32[8,320]{1,0:T(8,128)S(1)}, f32[32,1,128]{2,1,0:T(1,128)}) custom-call(f32[2]{0:T(128)S(1)} %fusion.7.snr, f32[32,1,128]{2,1,0:T(1,128)S(1)} %all_to_all.10.sums, f32[8,320]{1,0:T(8,128)S(1)} %get-tuple-element.62.trailing, f32[2,8,4,64]{3,2,1,0:T(4,128)S(1)} %bitcast.33, bf16[4,320]{1,0:T(4,128)(2,1)S(1)} %bitcast.34, ...), custom_call_target="tpu_custom_call" | custom-call | flops 4294967296 | bytes 1048576 | tf_op jit(solution)/shard_map/pallas_call | solution.py:47
  71.3 2.6 %all-to-all-start.1 = ((f32[32,1,128]{2,1,0:T(1,128)}), f32[32,1,128]{2,1,0:T(1,128)S(1)}, u32[]{:S(2)}, u32[]{:S(2)}) async-start(f32[32,1,128]{2,1,0:T(1,128)} %get-tuple-element.71), calls=%async_computation.1 | async-start | bytes 32768 | tf_op jit(solution)/shard_map/all_to_all | solution.py:548
  73.9 3.1 %shard_map.177 = (f32[2,512,320]{2,1,0:T(8,128)S(1)}, f32[2,512,320]{2,1,0:T(8,128)S(1)}, bf16[2,640,960]{2,1,0:T(8,128)(2,1)S(1)}) custom-call(f32[2,512,320]{2,1,0:T(8,128)} %get-tuple-element.72.g_far, f32[2,512,320]{2,1,0:T(8,128)} %get-tuple-element.63.feature_far, bf16[2,512,320]{2,1,0:T(8,128)(2,1)} %get-tuple-element.73.relu_far, ...), custom_call_target="tpu_custom_call" | custom-call | flops 4294967296 | bytes 1048576 | tf_op jit(solution)/shard_map/pallas_call | solution.py:47
  77.0 1.5 %copy-done.8 = bf16[2,640,960]{2,1,0:T(8,128)(2,1)} copy-done((bf16[2,640,960]{2,1,0:T(8,128)(2,1)}, bf16[2,640,960]{2,1,0:T(8,128)(2,1)S(1)}, u32[]{:S(2)}) %copy-start.8) | copy-done | bytes 2457624
  78.5 2.5 %all-to-all-done.1.sums_two = f32[32,1,128]{2,1,0:T(1,128)S(1)} async-done(((f32[32,1,128]{2,1,0:T(1,128)}), f32[32,1,128]{2,1,0:T(1,128)S(1)}, u32[]{:S(2)}, u32[]{:S(2)}) %all-to-all-start.1) | async-done | bytes 16416 | tf_op jit(solution)/shard_map/all_to_all | solution.py:548
  80.9 1.0 shard_map.178
  82.0 0.6 collective-permute-start.11
  82.6 0.7 collective-permute-start.12
  83.3 4.1 %shard_map.179 = (f32[3200,320]{1,0:T(8,128)S(1)}, f32[8,320]{1,0:T(8,128)S(1)}, f32[2,512,320]{2,1,0:T(8,128)S(1)}) custom-call(f32[8,128]{1,0:T(8,128)S(1)} %get-tuple-element.78.scalars, f32[8,320]{1,0:T(8,128)S(1)} %get-tuple-element.82.u, bf16[2,512,320]{2,1,0:T(8,128)(2,1)S(1)} %get-tuple-element.79.gz, bf16[2,640,960]{2,1,0:T(8,128)(2,1)S(1)} %copy-done.9, ...), custom_call_target="tpu_custom_call" | custom-call | flops 2147483648 | bytes 1048576 | tf_op jit(solution)/shard_map/pallas_call | solution.py:47
  87.4 8.9 %shard_map.180 = (bf16[17,400,128]{2,1,0:T(8,128)(2,1)S(1)}, bf16[17,400,128]{2,1,0:T(8,128)(2,1)S(1)}) custom-call(s32[4]{0:T(128)S(1)} %pad_add_fusion.place, bf16[2,512,320]{2,1,0:T(8,128)(2,1)S(1)} %get-tuple-element.79.gz, bf16[2,64,320]{2,1,0:T(8,128)(2,1)S(1)} %collective-permute-done.11.first, ...), custom_call_target="tpu_custom_call" | custom-call | flops 4294967296 | bytes 1048576 | tf_op jit(solution)/shard_map/pallas_call | solution.py:47
  96.5 3.6 %collective-permute-done.13 = bf16[17,400,128]{2,1,0:T(8,128)(2,1)S(1)} collective-permute-done((bf16[17,400,128]{2,1,0:T(8,128)(2,1)S(1)}, bf16[17,400,128]{2,1,0:T(8,128)(2,1)S(1)}, u32[]{:S(2)}, u32[]{:S(2)}) %collective-permute-start.13) | collective-permute-done | bytes 1740832 | tf_op jit(solution)/shard_map/ppermute | solution.py:100
  100.1 0.5 fusion.8
  100.6 4.1 %collective-permute-start.16 = (bf16[8,192,128]{2,1,0:T(8,128)(2,1)S(1)}, bf16[8,192,128]{2,1,0:T(8,128)(2,1)S(1)}, u32[]{:S(2)}, u32[]{:S(2)}) collective-permute-start(bf16[8,192,128]{2,1,0:T(8,128)(2,1)S(1)} %slice.151), channel_id=1, source_target_pairs={{0,4},{4,0},{8,12},{12,8},{16,20},{20,16},{24,28},{28,24},{1,5},{5... | collective-permute-start | bytes 1179656 | tf_op jit(solution)/shard_map/ppermute | solution.py:100
  104.7 0.6 collective-permute-start.14
  105.3 8.8 %collective-permute-done.16 = bf16[8,192,128]{2,1,0:T(8,128)(2,1)S(1)} collective-permute-done((bf16[8,192,128]{2,1,0:T(8,128)(2,1)S(1)}, bf16[8,192,128]{2,1,0:T(8,128)(2,1)S(1)}, u32[]{:S(2)}, u32[]{:S(2)}) %collective-permute-start.16) | collective-permute-done | bytes 393248 | tf_op jit(solution)/shard_map/ppermute | solution.py:100
  114.2 0.6 collective-permute-start.17
  114.8 1.6 %collective-permute-done.14 = bf16[8,208,128]{2,1,0:T(8,128)(2,1)S(1)} collective-permute-done((bf16[8,208,128]{2,1,0:T(8,128)(2,1)S(1)}, bf16[8,208,128]{2,1,0:T(8,128)(2,1)S(1)}, u32[]{:S(2)}, u32[]{:S(2)}) %collective-permute-start.14) | collective-permute-done | bytes 426016 | tf_op jit(solution)/shard_map/ppermute | solution.py:100
  116.5 0.4 collective-permute-start.15
  116.9 3.9 %collective-permute-done.17 = bf16[4,192,128]{2,1,0:T(8,128)(2,1)S(1)} collective-permute-done((bf16[4,192,128]{2,1,0:T(8,128)(2,1)S(1)}, bf16[4,192,128]{2,1,0:T(8,128)(2,1)S(1)}, u32[]{:S(2)}, u32[]{:S(2)}) %collective-permute-start.17) | collective-permute-done | bytes 196640 | tf_op jit(solution)/shard_map/ppermute | solution.py:100
  120.8 1.9 %collective-permute-done.15 = bf16[4,208,128]{2,1,0:T(8,128)(2,1)S(1)} collective-permute-done((bf16[4,208,128]{2,1,0:T(8,128)(2,1)S(1)}, bf16[4,208,128]{2,1,0:T(8,128)(2,1)S(1)}, u32[]{:S(2)}, u32[]{:S(2)}) %collective-permute-start.15) | collective-permute-done | bytes 213024 | tf_op jit(solution)/shard_map/ppermute | solution.py:100
  122.9 0.6 collective-permute-start.18
  123.5 1.8 %collective-permute-start.19 = (bf16[1,400,128]{2,1,0:T(8,128)(2,1)S(1)}, bf16[1,400,128]{2,1,0:T(8,128)(2,1)S(1)}, u32[]{:S(2)}, u32[]{:S(2)}) collective-permute-start(bf16[1,400,128]{2,1,0:T(8,128)(2,1)S(1)} %get-tuple-element.99), channel_id=1, source_target_pairs={{0,16},{4,20},{8,24},{12,28},{16,0},{20,4},{24,8},{28,12},{1,17},{... | collective-permute-start | bytes 307208 | tf_op jit(solution)/shard_map/ppermute | solution.py:100
  125.3 2.0 %collective-permute-start.20 = (bf16[1,400,128]{2,1,0:T(8,128)(2,1)S(1)}, bf16[1,400,128]{2,1,0:T(8,128)(2,1)S(1)}, u32[]{:S(2)}, u32[]{:S(2)}) collective-permute-start(bf16[1,400,128]{2,1,0:T(8,128)(2,1)S(1)} %get-tuple-element.98), channel_id=1, source_target_pairs={{0,24},{4,28},{8,16},{12,20},{16,8},{20,12},{24,0},{28,4},{1,25},{... | collective-permute-start | bytes 307208 | tf_op jit(solution)/shard_map/ppermute | solution.py:100
  128.0 0.5 slice.117
  128.6 3.9 %collective-permute-done.19 = bf16[1,400,128]{2,1,0:T(8,128)(2,1)S(1)} collective-permute-done((bf16[1,400,128]{2,1,0:T(8,128)(2,1)S(1)}, bf16[1,400,128]{2,1,0:T(8,128)(2,1)S(1)}, u32[]{:S(2)}, u32[]{:S(2)}) %collective-permute-start.19) | collective-permute-done | bytes 102432 | tf_op jit(solution)/shard_map/ppermute | solution.py:100
  132.9 1.0 multiply_subtract_fusion
  (87 shorter events, 1.9 us)
Async XLA Ops:
  0.6 10.5 %copy-start.19 = (bf16[2,1,77,768]{3,0,2,1:T(2,128)(2,1)S(1)}, bf16[2,1,77,768]{3,0,2,1:T(2,128)(2,1)}, u32[]{:S(2)}) copy-start(bf16[2,1,77,768]{3,0,2,1:T(2,128)(2,1)} %param.17) | copy-start | bytes 709636
  2.0 9.2 %collective-permute-start = (bf16[1,400,128]{2,1,0:T(8,128)(2,1)S(1)}, bf16[1,400,128]{2,1,0:T(8,128)(2,1)S(1)}, u32[]{:S(2)}, u32[]{:S(2)}) collective-permute-start(bf16[1,400,128]{2,1,0:T(8,128)(2,1)S(1)} %maximum_bitcast_fusion), channel_id=1, source_target_pairs={{0,8},{4,12},{8,0},{12,4},{16,24},{20,28},{24,16},{28,20},{1,9},{5... | collective-permute-start | bytes 307208 | tf_op jit(solution)/shard_map/ppermute | solution.py:100
  5.1 10.8 %collective-permute-start.1 = (bf16[1,400,128]{2,1,0:T(8,128)(2,1)S(1)}, bf16[1,400,128]{2,1,0:T(8,128)(2,1)S(1)}, u32[]{:S(2)}, u32[]{:S(2)}) collective-permute-start(bf16[1,400,128]{2,1,0:T(8,128)(2,1)S(1)} %maximum_bitcast_fusion), channel_id=1, source_target_pairs={{0,16},{4,20},{8,24},{12,28},{16,0},{20,4},{24,8},{28,12},{1,17},{... | collective-permute-start | bytes 307208 | tf_op jit(solution)/shard_map/ppermute | solution.py:100
  7.7 8.2 %collective-permute-start.2 = (bf16[1,400,128]{2,1,0:T(8,128)(2,1)S(1)}, bf16[1,400,128]{2,1,0:T(8,128)(2,1)S(1)}, u32[]{:S(2)}, u32[]{:S(2)}) collective-permute-start(bf16[1,400,128]{2,1,0:T(8,128)(2,1)S(1)} %maximum_bitcast_fusion), channel_id=1, source_target_pairs={{0,24},{4,28},{8,16},{12,20},{16,8},{20,12},{24,0},{28,4},{1,25},{... | collective-permute-start | bytes 307208 | tf_op jit(solution)/shard_map/ppermute | solution.py:100
  8.7 8.9 %collective-permute-start.3 = (bf16[2,2,64,192]{3,2,1,0:T(8,128)(2,1)S(1)}, bf16[2,2,64,192]{3,2,1,0:T(8,128)(2,1)S(1)}, u32[]{:S(2)}, u32[]{:S(2)}) collective-permute-start(bf16[2,2,64,192]{3,2,1,0:T(8,128)(2,1)S(1)} %get-tuple-element.96), channel_id=1, source_target_pairs={{0,4},{4,0},{8,12},{12,8},{16,20},{20,16},{24,28},{28,24},{1,5},{5... | collective-permute-start | bytes 294920 | tf_op jit(solution)/shard_map/ppermute | solution.py:544
  10.4 7.2 %collective-permute-start.4 = (bf16[2,2,64,192]{3,2,1,0:T(8,128)(2,1)S(1)}, bf16[2,2,64,192]{3,2,1,0:T(8,128)(2,1)S(1)}, u32[]{:S(2)}, u32[]{:S(2)}) collective-permute-start(bf16[2,2,64,192]{3,2,1,0:T(8,128)(2,1)S(1)} %get-tuple-element.95), channel_id=1, source_target_pairs={{4,8},{8,4},{12,16},{16,12},{20,24},{24,20},{5,9},{9,5},{13,17},{1... | collective-permute-start | bytes 294920 | tf_op jit(solution)/shard_map/ppermute | solution.py:544
  11.2 16.1 %copy-start = (bf16[2,8,64,192]{3,2,1,0:T(8,128)(2,1)S(1)}, bf16[2,8,64,192]{3,2,1,0:T(8,128)(2,1)}, u32[]{:S(2)}) copy-start(bf16[2,8,64,192]{3,2,1,0:T(8,128)(2,1)} %param.15) | copy-start | bytes 1179652
  11.2 16.1 %copy-start.1 = (bf16[2,8,64,320]{3,2,1,0:T(8,128)(2,1)S(1)}, bf16[2,8,64,320]{3,2,1,0:T(8,128)(2,1)}, u32[]{:S(2)}) copy-start(bf16[2,8,64,320]{3,2,1,0:T(8,128)(2,1)} %param.16) | copy-start | bytes 1966084
  11.2 16.1 %copy-start.2 = (bf16[768,320]{0,1:T(8,128)(2,1)S(1)}, bf16[768,320]{0,1:T(8,128)(2,1)}, u32[]{:S(2)}) copy-start(bf16[768,320]{0,1:T(8,128)(2,1)} %param.22) | copy-start | bytes 1474564
  11.2 16.1 %copy-start.3 = (bf16[768,320]{0,1:T(8,128)(2,1)S(1)}, bf16[768,320]{0,1:T(8,128)(2,1)}, u32[]{:S(2)}) copy-start(bf16[768,320]{0,1:T(8,128)(2,1)} %param.23) | copy-start | bytes 1474564
  11.2 16.1 %copy-start.4 = (bf16[320,320]{1,0:T(8,128)(2,1)S(1)}, bf16[320,320]{1,0:T(8,128)(2,1)}, u32[]{:S(2)}) copy-start(bf16[320,320]{1,0:T(8,128)(2,1)} %wq_far.1) | copy-start | bytes 614404
  11.2 16.1 %copy-start.5 = (bf16[320,320]{1,0:T(8,128)(2,1)S(1)}, bf16[320,320]{1,0:T(8,128)(2,1)}, u32[]{:S(2)}) copy-start(bf16[320,320]{1,0:T(8,128)(2,1)} %wo_far.1) | copy-start | bytes 614404
  15.9 5.7 %collective-permute-start.7 = (bf16[4,192,128]{2,1,0:T(8,128)(2,1)S(1)}, bf16[4,192,128]{2,1,0:T(8,128)(2,1)S(1)}, u32[]{:S(2)}, u32[]{:S(2)}) collective-permute-start(bf16[4,192,128]{2,1,0:T(8,128)(2,1)S(1)} %pad_maximum_fusion.6), channel_id=1, source_target_pairs={{0,2},{1,3},{2,0},{3,1},{4,6},{5,7},{6,4},{7,5},{8,10},{9,11},{10,... | collective-permute-start | bytes 589832 | tf_op jit(solution)/shard_map/ppermute | solution.py:100
  17.6 8.2 %collective-permute-start.5 = (bf16[4,208,128]{2,1,0:T(8,128)(2,1)S(1)}, bf16[4,208,128]{2,1,0:T(8,128)(2,1)S(1)}, u32[]{:S(2)}, u32[]{:S(2)}) collective-permute-start(bf16[4,208,128]{2,1,0:T(8,128)(2,1)S(1)} %slice.144), channel_id=1, source_target_pairs={{0,4},{4,0},{8,12},{12,8},{16,20},{20,16},{24,28},{28,24},{1,5},{5... | collective-permute-start | bytes 638984 | tf_op jit(solution)/shard_map/ppermute | solution.py:100
  21.7 11.1 %collective-permute-start.8 = (bf16[8,192,128]{2,1,0:T(8,128)(2,1)S(1)}, bf16[8,192,128]{2,1,0:T(8,128)(2,1)S(1)}, u32[]{:S(2)}, u32[]{:S(2)}) collective-permute-start(bf16[8,192,128]{2,1,0:T(8,128)(2,1)S(1)} %pad_maximum_fusion.5), channel_id=1, source_target_pairs={{0,4},{4,0},{8,12},{12,8},{16,20},{20,16},{24,28},{28,24},{1,5},{5... | collective-permute-start | bytes 1179656 | tf_op jit(solution)/shard_map/ppermute | solution.py:100
  25.9 9.0 %collective-permute-start.6 = (bf16[8,208,128]{2,1,0:T(8,128)(2,1)S(1)}, bf16[8,208,128]{2,1,0:T(8,128)(2,1)S(1)}, u32[]{:S(2)}, u32[]{:S(2)}) collective-permute-start(bf16[8,208,128]{2,1,0:T(8,128)(2,1)S(1)} %pad_maximum_fusion.3), channel_id=1, source_target_pairs={{0,2},{1,3},{2,0},{3,1},{4,6},{5,7},{6,4},{7,5},{8,10},{9,11},{10,... | collective-permute-start | bytes 1277960 | tf_op jit(solution)/shard_map/ppermute | solution.py:100
  29.2 1.3 copy-start.10
  30.5 0.7 copy-start.15
  31.2 18.6 %copy-start.11 = (bf16[2,320,512]{2,1,0:T(8,128)(2,1)}, bf16[2,320,512]{2,1,0:T(8,128)(2,1)S(1)}, u32[]{:S(2)}) copy-start(bf16[2,320,512]{2,1,0:T(8,128)(2,1)S(1)} %get-tuple-element.64.resid_far) | copy-start | bytes 1966084
  31.2 18.6 %copy-start.12 = (bf16[2,8,80,40]{3,2,1,0:T(8,128)(2,1)}, bf16[2,8,80,40]{3,2,1,0:T(8,128)(2,1)S(1)}, u32[]{:S(2)}) copy-start(bf16[2,8,80,40]{3,2,1,0:T(8,128)(2,1)S(1)} %get-tuple-element.66.keys_far) | copy-start | bytes 307204
  31.2 18.6 %copy-start.13 = (bf16[2,8,80,40]{3,2,1,0:T(8,128)(2,1)}, bf16[2,8,80,40]{3,2,1,0:T(8,128)(2,1)S(1)}, u32[]{:S(2)}) copy-start(bf16[2,8,80,40]{3,2,1,0:T(8,128)(2,1)S(1)} %get-tuple-element.69.values_far) | copy-start | bytes 307204
  31.2 18.6 %copy-start.14 = (bf16[320,320]{1,0:T(8,128)(2,1)}, bf16[320,320]{1,0:T(8,128)(2,1)S(1)}, u32[]{:S(2)}) copy-start(bf16[320,320]{1,0:T(8,128)(2,1)S(1)} %get-tuple-element.65.wqt_far) | copy-start | bytes 614404
  31.2 18.6 %copy-start.16 = (bf16[2,8,40,80]{3,2,1,0:T(8,128)(2,1)}, bf16[2,8,40,80]{3,2,1,0:T(8,128)(2,1)S(1)}, u32[]{:S(2)}) copy-start(bf16[2,8,40,80]{3,2,1,0:T(8,128)(2,1)S(1)} %get-tuple-element.70.keyst_far) | copy-start | bytes 307204
  31.2 18.6 %copy-start.17 = (bf16[2,8,40,80]{3,2,1,0:T(8,128)(2,1)}, bf16[2,8,40,80]{3,2,1,0:T(8,128)(2,1)S(1)}, u32[]{:S(2)}) copy-start(bf16[2,8,40,80]{3,2,1,0:T(8,128)(2,1)S(1)} %get-tuple-element.67.valuest_far) | copy-start | bytes 307204
  31.2 4.3 %copy-start.22 = (f32[1000]{0:T(1024)S(1)}, f32[1000]{0:T(1024)}, u32[]{:S(2)}) copy-start(f32[1000]{0:T(1024)} %constant.57.clone) | copy-start | bytes 12004
  31.3 4.3 %copy-start.23 = (s32[2,1]{0,1:T(1,128)S(1)}, s32[2,1]{0,1:T(1,128)}, u32[]{:S(2)}) copy-start(s32[2,1]{0,1:T(1,128)} %param.19) | copy-start | bytes 28
  35.0 3.6 %collective-permute-start.9 = (bf16[16,208,128]{2,1,0:T(8,128)(2,1)S(1)}, bf16[16,208,128]{2,1,0:T(8,128)(2,1)S(1)}, u32[]{:S(2)}, u32[]{:S(2)}) collective-permute-start(bf16[16,208,128]{2,1,0:T(8,128)(2,1)S(1)} %pad_maximum_fusion.1.own_a), channel_id=1, source_target_pairs={{0,1},{1,0},{2,3},{3,2},{4,5},{5,4},{6,7},{7,6},{8,9},{9,8},{10,11... | collective-permute-start | bytes 2555912 | tf_op jit(solution)/shard_map/ppermute | solution.py:100
  35.1 3.5 %collective-permute-start.10 = (bf16[16,192,128]{2,1,0:T(8,128)(2,1)S(1)}, bf16[16,192,128]{2,1,0:T(8,128)(2,1)S(1)}, u32[]{:S(2)}, u32[]{:S(2)}) collective-permute-start(bf16[16,192,128]{2,1,0:T(8,128)(2,1)S(1)} %pad_maximum_fusion.2.own_b), channel_id=1, source_target_pairs={{0,1},{1,0},{2,3},{3,2},{4,5},{5,4},{6,7},{7,6},{8,9},{9,8},{10,11... | collective-permute-start | bytes 2359304 | tf_op jit(solution)/shard_map/ppermute | solution.py:100
  35.8 26.1 %copy-start.6 = (f32[2,8,64,4]{2,3,1,0:T(4,128)S(1)}, f32[2,8,64,4]{2,3,1,0:T(4,128)}, u32[]{:S(2)}) copy-start(f32[2,8,64,4]{2,3,1,0:T(4,128)} %param.18) | copy-start | bytes 49156
  35.8 26.1 %copy-start.7 = (bf16[320,4]{0,1:T(4,128)(2,1)S(1)}, bf16[320,4]{0,1:T(4,128)(2,1)}, u32[]{:S(2)}) copy-start(bf16[320,4]{0,1:T(4,128)(2,1)} %param.25) | copy-start | bytes 7684
  71.3 9.6 %all-to-all-start.1 = ((f32[32,1,128]{2,1,0:T(1,128)}), f32[32,1,128]{2,1,0:T(1,128)S(1)}, u32[]{:S(2)}, u32[]{:S(2)}) async-start(f32[32,1,128]{2,1,0:T(1,128)} %get-tuple-element.71), calls=%async_computation.1 | async-start | bytes 32768 | tf_op jit(solution)/shard_map/all_to_all | solution.py:548
  77.0 1.5 %copy-start.8 = (bf16[2,640,960]{2,1,0:T(8,128)(2,1)}, bf16[2,640,960]{2,1,0:T(8,128)(2,1)S(1)}, u32[]{:S(2)}) copy-start(bf16[2,640,960]{2,1,0:T(8,128)(2,1)S(1)} %get-tuple-element.83.x3) | copy-start | bytes 7372804
  80.9 2.3 %copy-start.9 = (bf16[2,640,960]{2,1,0:T(8,128)(2,1)S(1)}, bf16[2,640,960]{2,1,0:T(8,128)(2,1)}, u32[]{:S(2)}) copy-start(bf16[2,640,960]{2,1,0:T(8,128)(2,1)} %copy-done.8) | copy-start | bytes 7372804
  82.0 5.4 %collective-permute-start.11 = (bf16[2,64,320]{2,1,0:T(8,128)(2,1)S(1)}, bf16[2,64,320]{2,1,0:T(8,128)(2,1)S(1)}, u32[]{:S(2)}, u32[]{:S(2)}) collective-permute-start(bf16[2,64,320]{2,1,0:T(8,128)(2,1)S(1)} %get-tuple-element.80), channel_id=1, source_target_pairs={{0,4},{4,0},{8,12},{12,8},{16,20},{20,16},{24,28},{28,24},{1,5},{5... | collective-permute-start | bytes 245768 | tf_op jit(solution)/shard_map/ppermute | solution.py:544
  82.6 4.8 %collective-permute-start.12 = (bf16[2,64,320]{2,1,0:T(8,128)(2,1)S(1)}, bf16[2,64,320]{2,1,0:T(8,128)(2,1)S(1)}, u32[]{:S(2)}, u32[]{:S(2)}) collective-permute-start(bf16[2,64,320]{2,1,0:T(8,128)(2,1)S(1)} %get-tuple-element.81), channel_id=1, source_target_pairs={{4,8},{8,4},{12,16},{16,12},{20,24},{24,20},{5,9},{9,5},{13,17},{1... | collective-permute-start | bytes 245768 | tf_op jit(solution)/shard_map/ppermute | solution.py:544
  96.4 3.7 %collective-permute-start.13 = (bf16[17,400,128]{2,1,0:T(8,128)(2,1)S(1)}, bf16[17,400,128]{2,1,0:T(8,128)(2,1)S(1)}, u32[]{:S(2)}, u32[]{:S(2)}) collective-permute-start(bf16[17,400,128]{2,1,0:T(8,128)(2,1)S(1)} %get-tuple-element.89), channel_id=1, source_target_pairs={{0,1},{1,0},{2,3},{3,2},{4,5},{5,4},{6,7},{7,6},{8,9},{9,8},{10,11... | collective-permute-start | bytes 5222408 | tf_op jit(solution)/shard_map/ppermute | solution.py:100
  100.6 13.5 %collective-permute-start.16 = (bf16[8,192,128]{2,1,0:T(8,128)(2,1)S(1)}, bf16[8,192,128]{2,1,0:T(8,128)(2,1)S(1)}, u32[]{:S(2)}, u32[]{:S(2)}) collective-permute-start(bf16[8,192,128]{2,1,0:T(8,128)(2,1)S(1)} %slice.151), channel_id=1, source_target_pairs={{0,4},{4,0},{8,12},{12,8},{16,20},{20,16},{24,28},{28,24},{1,5},{5... | collective-permute-start | bytes 1179656 | tf_op jit(solution)/shard_map/ppermute | solution.py:100
  104.7 11.6 %collective-permute-start.14 = (bf16[8,208,128]{2,1,0:T(8,128)(2,1)S(1)}, bf16[8,208,128]{2,1,0:T(8,128)(2,1)S(1)}, u32[]{:S(2)}, u32[]{:S(2)}) collective-permute-start(bf16[8,208,128]{2,1,0:T(8,128)(2,1)S(1)} %slice.147), channel_id=1, source_target_pairs={{0,2},{1,3},{2,0},{3,1},{4,6},{5,7},{6,4},{7,5},{8,10},{9,11},{10,... | collective-permute-start | bytes 1277960 | tf_op jit(solution)/shard_map/ppermute | solution.py:100
  114.2 6.5 %collective-permute-start.17 = (bf16[4,192,128]{2,1,0:T(8,128)(2,1)S(1)}, bf16[4,192,128]{2,1,0:T(8,128)(2,1)S(1)}, u32[]{:S(2)}, u32[]{:S(2)}) collective-permute-start(bf16[4,192,128]{2,1,0:T(8,128)(2,1)S(1)} %slice.196), channel_id=1, source_target_pairs={{0,2},{1,3},{2,0},{3,1},{4,6},{5,7},{6,4},{7,5},{8,10},{9,11},{10,... | collective-permute-start | bytes 589832 | tf_op jit(solution)/shard_map/ppermute | solution.py:100
  116.5 6.2 %collective-permute-start.15 = (bf16[4,208,128]{2,1,0:T(8,128)(2,1)S(1)}, bf16[4,208,128]{2,1,0:T(8,128)(2,1)S(1)}, u32[]{:S(2)}, u32[]{:S(2)}) collective-permute-start(bf16[4,208,128]{2,1,0:T(8,128)(2,1)S(1)} %slice.195), channel_id=1, source_target_pairs={{0,4},{4,0},{8,12},{12,8},{16,20},{20,16},{24,28},{28,24},{1,5},{5... | collective-permute-start | bytes 638984 | tf_op jit(solution)/shard_map/ppermute | solution.py:100
  122.8 10.0 %copy-start.18 = (f32[49320]{0:T(1024)S(1)}, f32[49320]{0:T(1024)}, u32[]{:S(2)}) copy-start(f32[49320]{0:T(1024)} %param.26) | copy-start | bytes 591844
  122.8 10.0 %copy-start.20 = (f32[49320]{0:T(1024)S(1)}, f32[49320]{0:T(1024)}, u32[]{:S(2)}) copy-start(f32[49320]{0:T(1024)} %param.28) | copy-start | bytes 591844
  122.9 10.0 %copy-start.21 = (f32[49320]{0:T(1024)S(1)}, f32[49320]{0:T(1024)}, u32[]{:S(2)}) copy-start(f32[49320]{0:T(1024)} %param.27) | copy-start | bytes 591844
  122.9 5.7 %collective-permute-start.18 = (bf16[1,400,128]{2,1,0:T(8,128)(2,1)S(1)}, bf16[1,400,128]{2,1,0:T(8,128)(2,1)S(1)}, u32[]{:S(2)}, u32[]{:S(2)}) collective-permute-start(bf16[1,400,128]{2,1,0:T(8,128)(2,1)S(1)} %get-tuple-element.97), channel_id=1, source_target_pairs={{0,8},{4,12},{8,0},{12,4},{16,24},{20,28},{24,16},{28,20},{1,9},{5... | collective-permute-start | bytes 307208 | tf_op jit(solution)/shard_map/ppermute | solution.py:100
  123.5 9.0 %collective-permute-start.19 = (bf16[1,400,128]{2,1,0:T(8,128)(2,1)S(1)}, bf16[1,400,128]{2,1,0:T(8,128)(2,1)S(1)}, u32[]{:S(2)}, u32[]{:S(2)}) collective-permute-start(bf16[1,400,128]{2,1,0:T(8,128)(2,1)S(1)} %get-tuple-element.99), channel_id=1, source_target_pairs={{0,16},{4,20},{8,24},{12,28},{16,0},{20,4},{24,8},{28,12},{1,17},{... | collective-permute-start | bytes 307208 | tf_op jit(solution)/shard_map/ppermute | solution.py:100
  125.3 7.1 %collective-permute-start.20 = (bf16[1,400,128]{2,1,0:T(8,128)(2,1)S(1)}, bf16[1,400,128]{2,1,0:T(8,128)(2,1)S(1)}, u32[]{:S(2)}, u32[]{:S(2)}) collective-permute-start(bf16[1,400,128]{2,1,0:T(8,128)(2,1)S(1)} %get-tuple-element.98), channel_id=1, source_target_pairs={{0,24},{4,28},{8,16},{12,20},{16,8},{20,12},{24,0},{28,4},{1,25},{... | collective-permute-start | bytes 307208 | tf_op jit(solution)/shard_map/ppermute | solution.py:100

commit v4 on v3

--- a/solution.py
+++ b/solution.py
@@ -170,8 +170,8 @@
     return jnp.concatenate([left, values, right], axis=1).astype(BF)
 
 
-def neighbours(place, first, second):
-    even = jnp.full((1, 1), place[3], jnp.int32) == 0
+def neighbours(odd, first, second):
+    even = jnp.full((1, 1), odd, jnp.int32) == 0
     return jnp.where(even, second, first), jnp.where(even, first, second)
 
 
@@ -197,7 +197,7 @@
     room = keys.shape[2]
     pad = jnp.zeros((channels, LANES - words), F32)
     for i in range(images):
-        low, high = neighbours(place, first[i].astype(F32), second[i].astype(F32))
+        low, high = neighbours(place[3], first[i].astype(F32), second[i].astype(F32))
         wide = jnp.concatenate([low, cond[i].astype(F32), high], axis=0)
         c3[i] = three_columns(wide, cols)
         for weight, flat, tall in ((wk_t, keys, keys_t), (wv_t, values, values_t)):
@@ -414,7 +414,7 @@
 
 
 def solve_kernel(
-    cols, elements, place, sums, sums_two, by_g, by_feature, scalars, gz, to_pair, to_other
+    cols, elements, sums, sums_two, by_g, by_feature, scalars, gz, to_pair, to_other
 ):
     images, tokens, channels = gz.shape
     scale = norm_of(jnp.sum(sums[...], axis=0), elements)
@@ -422,12 +422,13 @@
     pull = scale * scale * scale * (lane_pick(line, 1) / elements)
     pairs = [(0, jnp.full((1, 1), lane_pick(line, 0), F32)), (1, pull), (2, scale)]
     scalars[...] = jnp.broadcast_to(lane_row(pairs), scalars.shape)
-    for i in range(images):
-        back = by_g[i] - pull * by_feature[i]
-        gz[i] = back.astype(BF)
-        top, bottom = back[:cols], back[tokens - cols :]
-        pair, other = neighbours(place, top, bottom)
-        to_pair[i], to_other[i] = pair.astype(BF), other.astype(BF)
+    odd = lax.rem(lax.axis_index("sp"), 2)
+    top = pl.multiple_of(odd * (tokens - cols), cols)
+    bottom = pl.multiple_of((1 - odd) * (tokens - cols), cols)
+    for i in range(images):
+        gz[i] = (by_g[i] - pull * by_feature[i]).astype(BF)
+        to_pair[i] = gz[i, pl.ds(bottom, cols)]
+        to_other[i] = gz[i, pl.ds(top, cols)]
 
 
 def block_weight_kernel(
@@ -478,10 +479,10 @@
 
 
 def input_kernel(
-    plan, cols, place, gz, first, second, g_f, d_block, d_rows, w1t_far, c3_far,
+    plan, cols, gz, first, second, g_f, d_block, d_rows, w1t_far, c3_far,
     keep, send, table, w1t, c3, sems,
 ):
-    me = place[0]
+    me = lax.axis_index("sp") * plan.hd + lax.axis_index("hd")
     images, tokens, channels = gz.shape
     kept, kept_in = 3 * channels, c3.shape[2]
     load = start(w1t_far, w1t, sems.at[0])
@@ -501,7 +502,7 @@
             table[low:high] = d_block[low - n_in : high - n_in]
     wide = []
     for i in range(images):
-        above, below = neighbours(place, first[i].astype(F32), second[i].astype(F32))
+        above, below = neighbours(lax.rem(lax.axis_index("sp"), 2), first[i].astype(F32), second[i].astype(F32))
         part = jnp.concatenate([above, gz[i].astype(F32), below], axis=0)
         wide.append(three_columns(part, cols))
     load.wait()
@@ -691,8 +692,7 @@
             ((images, cols, channels), BF),
             ((images, cols, channels), BF),
         ],
-        [place, sums, sums_two, by_g, by_feature],
-        smem=(0,),
+        [sums, sums_two, by_g, by_feature],
         flops=1 << 29,
     )
     first, second = trade_rows(to_pair, to_other)
@@ -715,15 +715,14 @@
             ((plan.half + 1, plan.packed, LANES), BF),
             ((plan.half + 1, plan.packed, LANES), BF),
         ],
-        [place, gz, first, second, g_f, d_block, d_rows, w1t, c3],
+        [gz, first, second, g_f, d_block, d_rows, w1t, c3],
         scratch=[
             VMEM((plan.table, channels), F32),
             VMEM((n_one, channels), BF),
             VMEM((images, wide + 2 * cols, kept_in), BF),
             DMA((2,)),
         ],
-        smem=(0,),
-        far=(7, 8),
+        far=(6, 7),
         flops=4 << 30,
     )
     grad_share = scatter_gradient(plan, keep, send)

time: 134 us -> 133 us (level)
  no operation moved by 1% of the time
where the time goes in v4:
time: 133 us
  waiting for transfers between devices  42 us (32%)
  Pallas kernels  38.5 us (29%)
  starting transfers between devices  28.9 us (22%)
  blocking collectives  12 us (9%)
  local copies, waits for them, and re-layouts  5.78 us (4%)
  other arithmetic  3.51 us (3%)
  between operations  1.91 us (1%)
    ppermute x17, waiting for transfers between devices, swap(): lax.ppermute(value, axis, [(i, i ^ step * stride) for i in range(count)])  39.5 us
    pallas_call x7, Pallas kernels, call(): pl.pallas_call(kernel, out_shape=[jax.ShapeDtypeStruct(*o) if i in far_li...  38.5 us
    ppermute x17, starting transfers between devices, swap(): lax.ppermute(value, axis, [(i, i ^ step * stride) for i in range(count)])  22.6 us
    all_to_all x1, blocking collectives, everywhere(): return lax.all_to_all(payload, ('sp', 'hd'), 0, 0, tiled=True)  12 us
    ppermute x4, starting transfers between devices, trade_rows(): return (lax.ppermute(first, 'sp', near), lax.ppermute(second, 'sp', far))  3.71 us
    unnamed x49, local copies, waits for them, and re-layouts  3.6 us
  transfers between devices with their start and end apart: 22, of which 13 were waited for; matrix products, arithmetic and copies ran while one was open for 2% of the time, Pallas kernels for 7%

profile of v4, /device:TPU:0, one launch (start us, length us, event | category | flops | bytes accessed | tf_op | source)
XLA Modules:
  0.0 132.6 jit_solution(13694451382495274513)
XLA Ops:
  0.7 1.1 fusion.1
  2.0 3.0 %collective-permute-start = (bf16[1,400,128]{2,1,0:T(8,128)(2,1)S(1)}, bf16[1,400,128]{2,1,0:T(8,128)(2,1)S(1)}, u32[]{:S(2)}, u32[]{:S(2)}) collective-permute-start(bf16[1,400,128]{2,1,0:T(8,128)(2,1)S(1)} %maximum_bitcast_fusion), channel_id=1, source_target_pairs={{0,8},{4,12},{8,0},{12,4},{16,24},{20,28},{24,16},{28,20},{1,9},{5... | collective-permute-start | bytes 307208 | tf_op jit(solution)/shard_map/ppermute | solution.py:100
  5.1 2.6 %collective-permute-start.1 = (bf16[1,400,128]{2,1,0:T(8,128)(2,1)S(1)}, bf16[1,400,128]{2,1,0:T(8,128)(2,1)S(1)}, u32[]{:S(2)}, u32[]{:S(2)}) collective-permute-start(bf16[1,400,128]{2,1,0:T(8,128)(2,1)S(1)} %maximum_bitcast_fusion), channel_id=1, source_target_pairs={{0,16},{4,20},{8,24},{12,28},{16,0},{20,4},{24,8},{28,12},{1,17},{... | collective-permute-start | bytes 307208 | tf_op jit(solution)/shard_map/ppermute | solution.py:100
  7.7 1.0 broadcast_select_fusion
  8.7 1.8 %collective-permute-start.3 = (bf16[2,2,64,192]{3,2,1,0:T(8,128)(2,1)S(1)}, bf16[2,2,64,192]{3,2,1,0:T(8,128)(2,1)S(1)}, u32[]{:S(2)}, u32[]{:S(2)}) collective-permute-start(bf16[2,2,64,192]{3,2,1,0:T(8,128)(2,1)S(1)} %get-tuple-element.96), channel_id=1, source_target_pairs={{0,4},{4,0},{8,12},{12,8},{16,20},{20,16},{24,28},{28,24},{1,5},{5... | collective-permute-start | bytes 294920 | tf_op jit(solution)/shard_map/ppermute | solution.py:545
  10.4 0.7 collective-permute-start.4
  11.2 4.7 %collective-permute-done.1 = bf16[1,400,128]{2,1,0:T(8,128)(2,1)S(1)} collective-permute-done((bf16[1,400,128]{2,1,0:T(8,128)(2,1)S(1)}, bf16[1,400,128]{2,1,0:T(8,128)(2,1)S(1)}, u32[]{:S(2)}, u32[]{:S(2)}) %collective-permute-start.1) | collective-permute-done | bytes 102432 | tf_op jit(solution)/shard_map/ppermute | solution.py:100
  15.9 1.6 %collective-permute-start.7 = (bf16[4,192,128]{2,1,0:T(8,128)(2,1)S(1)}, bf16[4,192,128]{2,1,0:T(8,128)(2,1)S(1)}, u32[]{:S(2)}, u32[]{:S(2)}) collective-permute-start(bf16[4,192,128]{2,1,0:T(8,128)(2,1)S(1)} %pad_maximum_fusion.6), channel_id=1, source_target_pairs={{0,2},{1,3},{2,0},{3,1},{4,6},{5,7},{6,4},{7,5},{8,10},{9,11},{10,... | collective-permute-start | bytes 589832 | tf_op jit(solution)/shard_map/ppermute | solution.py:100
  17.6 1.9 %collective-permute-start.5 = (bf16[4,208,128]{2,1,0:T(8,128)(2,1)S(1)}, bf16[4,208,128]{2,1,0:T(8,128)(2,1)S(1)}, u32[]{:S(2)}, u32[]{:S(2)}) collective-permute-start(bf16[4,208,128]{2,1,0:T(8,128)(2,1)S(1)} %slice.144), channel_id=1, source_target_pairs={{0,4},{4,0},{8,12},{12,8},{16,20},{20,16},{24,28},{28,24},{1,5},{5... | collective-permute-start | bytes 638984 | tf_op jit(solution)/shard_map/ppermute | solution.py:100
  19.6 2.1 %collective-permute-done.7 = bf16[4,192,128]{2,1,0:T(8,128)(2,1)S(1)} collective-permute-done((bf16[4,192,128]{2,1,0:T(8,128)(2,1)S(1)}, bf16[4,192,128]{2,1,0:T(8,128)(2,1)S(1)}, u32[]{:S(2)}, u32[]{:S(2)}) %collective-permute-start.7) | collective-permute-done | bytes 196640 | tf_op jit(solution)/shard_map/ppermute | solution.py:100
  21.7 1.5 %collective-permute-start.8 = (bf16[8,192,128]{2,1,0:T(8,128)(2,1)S(1)}, bf16[8,192,128]{2,1,0:T(8,128)(2,1)S(1)}, u32[]{:S(2)}, u32[]{:S(2)}) collective-permute-start(bf16[8,192,128]{2,1,0:T(8,128)(2,1)S(1)} %pad_maximum_fusion.5), channel_id=1, source_target_pairs={{0,4},{4,0},{8,12},{12,8},{16,20},{20,16},{24,28},{28,24},{1,5},{5... | collective-permute-start | bytes 1179656 | tf_op jit(solution)/shard_map/ppermute | solution.py:100
  23.2 2.7 %collective-permute-done.5 = bf16[4,208,128]{2,1,0:T(8,128)(2,1)S(1)} collective-permute-done((bf16[4,208,128]{2,1,0:T(8,128)(2,1)S(1)}, bf16[4,208,128]{2,1,0:T(8,128)(2,1)S(1)}, u32[]{:S(2)}, u32[]{:S(2)}) %collective-permute-start.5) | collective-permute-done | bytes 213024 | tf_op jit(solution)/shard_map/ppermute | solution.py:100
  25.9 1.4 %collective-permute-start.6 = (bf16[8,208,128]{2,1,0:T(8,128)(2,1)S(1)}, bf16[8,208,128]{2,1,0:T(8,128)(2,1)S(1)}, u32[]{:S(2)}, u32[]{:S(2)}) collective-permute-start(bf16[8,208,128]{2,1,0:T(8,128)(2,1)S(1)} %pad_maximum_fusion.3), channel_id=1, source_target_pairs={{0,2},{1,3},{2,0},{3,1},{4,6},{5,7},{6,4},{7,5},{8,10},{9,11},{10,... | collective-permute-start | bytes 1277960 | tf_op jit(solution)/shard_map/ppermute | solution.py:100
  27.3 1.9 %shard_map.174 = (bf16[2,768,576]{2,1,0:T(8,128)(2,1)S(1)}, bf16[2,8,80,40]{3,2,1,0:T(8,128)(2,1)S(1)}, bf16[2,8,40,80]{3,2,1,0:T(8,128)(2,1)S(1)}, bf16[2,8,80,...) custom-call(s32[4]{0:T(128)S(1)} %pad_add_fusion.place, ...), custom_call_target="tpu_custom_call" | custom-call | flops 4294967296 | bytes 1048576 | tf_op jit(solution)/shard_map/pallas_call | solution.py:47
  29.2 1.3 copy-done.10
  30.5 0.7 copy-done.15
  31.3 1.6 %collective-permute-done.8 = bf16[8,192,128]{2,1,0:T(8,128)(2,1)S(1)} collective-permute-done((bf16[8,192,128]{2,1,0:T(8,128)(2,1)S(1)}, bf16[8,192,128]{2,1,0:T(8,128)(2,1)S(1)}, u32[]{:S(2)}, u32[]{:S(2)}) %collective-permute-start.8) | collective-permute-done | bytes 393248 | tf_op jit(solution)/shard_map/ppermute | solution.py:100
  32.9 2.0 %collective-permute-done.6 = bf16[8,208,128]{2,1,0:T(8,128)(2,1)S(1)} collective-permute-done((bf16[8,208,128]{2,1,0:T(8,128)(2,1)S(1)}, bf16[8,208,128]{2,1,0:T(8,128)(2,1)S(1)}, u32[]{:S(2)}, u32[]{:S(2)}) %collective-permute-start.6) | collective-permute-done | bytes 426016 | tf_op jit(solution)/shard_map/ppermute | solution.py:100
  35.1 0.5 collective-permute-start.10
  35.8 2.8 %collective-permute-done.10.other_b = bf16[16,192,128]{2,1,0:T(8,128)(2,1)S(1)} collective-permute-done((bf16[16,192,128]{2,1,0:T(8,128)(2,1)S(1)}, bf16[16,192,128]{2,1,0:T(8,128)(2,1)S(1)}, u32[]{:S(2)}, u32[]{:S(2)}) %collective-permute-start.10) | collective-permute-done | bytes 786464 | tf_op jit(solution)/shard_map/ppermute | solution.py:100
  38.6 11.2 %shard_map.175 = (bf16[2880,320]{1,0:T(8,128)(2,1)}, bf16[320,320]{1,0:T(8,128)(2,1)}, f32[8,320]{1,0:T(8,128)S(1)}, f32[2,512,320]{2,1,0:T(8,128)}, bf16[2,512,...) custom-call(s32[4]{0:T(128)S(1)} %pad_add_fusion.place, f32[2]{0:T(128)S(1)} %fusion.7.snr, ...), custom_call_target="tpu_custom_call" | custom-call | flops 4294967296 | bytes 1048576 | tf_op jit(solution)/shard_map/pallas_call | solution.py:47
  49.8 12.0 %all_to_all.10.sums = f32[32,1,128]{2,1,0:T(1,128)S(1)} all-to-all(f32[32,1,128]{2,1,0:T(1,128)S(1)} %get-tuple-element.61), channel_id=1, replica_groups=mesh['sp'=8,'hd'=4] {'sp','hd'}, dimensions={0} | all-to-all | bytes 32768 | tf_op jit(solution)/shard_map/all_to_all | solution.py:549
  61.8 9.4 %shard_map.176 = (f32[2,512,320]{2,1,0:T(8,128)}, f32[8,320]{1,0:T(8,128)S(1)}, f32[32,1,128]{2,1,0:T(1,128)}) custom-call(f32[2]{0:T(128)S(1)} %fusion.7.snr, f32[32,1,128]{2,1,0:T(1,128)S(1)} %all_to_all.10.sums, f32[8,320]{1,0:T(8,128)S(1)} %get-tuple-element.62.trailing, f32[2,8,4,64]{3,2,1,0:T(4,128)S(1)} %bitcast.33, bf16[4,320]{1,0:T(4,128)(2,1)S(1)} %bitcast.34, ...), custom_call_target="tpu_custom_call" | custom-call | flops 4294967296 | bytes 1048576 | tf_op jit(solution)/shard_map/pallas_call | solution.py:47
  71.3 2.6 %all-to-all-start.1 = ((f32[32,1,128]{2,1,0:T(1,128)}), f32[32,1,128]{2,1,0:T(1,128)S(1)}, u32[]{:S(2)}, u32[]{:S(2)}) async-start(f32[32,1,128]{2,1,0:T(1,128)} %get-tuple-element.71), calls=%async_computation.1 | async-start | bytes 32768 | tf_op jit(solution)/shard_map/all_to_all | solution.py:549
  73.9 3.1 %shard_map.177 = (f32[2,512,320]{2,1,0:T(8,128)S(1)}, f32[2,512,320]{2,1,0:T(8,128)S(1)}, bf16[2,640,960]{2,1,0:T(8,128)(2,1)S(1)}) custom-call(f32[2,512,320]{2,1,0:T(8,128)} %get-tuple-element.72.g_far, f32[2,512,320]{2,1,0:T(8,128)} %get-tuple-element.63.feature_far, bf16[2,512,320]{2,1,0:T(8,128)(2,1)} %get-tuple-element.73.relu_far, ...), custom_call_target="tpu_custom_call" | custom-call | flops 4294967296 | bytes 1048576 | tf_op jit(solution)/shard_map/pallas_call | solution.py:47
  77.0 1.5 %copy-done.8 = bf16[2,640,960]{2,1,0:T(8,128)(2,1)} copy-done((bf16[2,640,960]{2,1,0:T(8,128)(2,1)}, bf16[2,640,960]{2,1,0:T(8,128)(2,1)S(1)}, u32[]{:S(2)}) %copy-start.8) | copy-done | bytes 2457624
  78.5 2.5 %all-to-all-done.1.sums_two = f32[32,1,128]{2,1,0:T(1,128)S(1)} async-done(((f32[32,1,128]{2,1,0:T(1,128)}), f32[32,1,128]{2,1,0:T(1,128)S(1)}, u32[]{:S(2)}, u32[]{:S(2)}) %all-to-all-start.1) | async-done | bytes 16416 | tf_op jit(solution)/shard_map/all_to_all | solution.py:549
  80.9 0.5 shard_map.178
  81.4 0.6 collective-permute-start.11
  82.1 0.7 collective-permute-start.12
  82.7 4.1 %shard_map.179 = (f32[3200,320]{1,0:T(8,128)S(1)}, f32[8,320]{1,0:T(8,128)S(1)}, f32[2,512,320]{2,1,0:T(8,128)S(1)}) custom-call(f32[8,128]{1,0:T(8,128)S(1)} %get-tuple-element.78.scalars, f32[8,320]{1,0:T(8,128)S(1)} %get-tuple-element.82.u, bf16[2,512,320]{2,1,0:T(8,128)(2,1)S(1)} %get-tuple-element.79.gz, bf16[2,640,960]{2,1,0:T(8,128)(2,1)S(1)} %copy-done.9, ...), custom_call_target="tpu_custom_call" | custom-call | flops 2147483648 | bytes 1048576 | tf_op jit(solution)/shard_map/pallas_call | solution.py:47
  86.9 8.2 %shard_map.180 = (bf16[17,400,128]{2,1,0:T(8,128)(2,1)S(1)}, bf16[17,400,128]{2,1,0:T(8,128)(2,1)S(1)}) custom-call(bf16[2,512,320]{2,1,0:T(8,128)(2,1)S(1)} %get-tuple-element.79.gz, bf16[2,64,320]{2,1,0:T(8,128)(2,1)S(1)} %collective-permute-done.11.first, bf16[2,64,320]{2,1,0:T(8,128)(2,1)S(1)} %collective-permute-done.12.second, ...), custom_call_target="tpu_custom_call" | custom-call | flops 4294967296 | bytes 1048576 | tf_op jit(solution)/shard_map/pallas_call | solution.py:47
  95.2 3.6 %collective-permute-done.13 = bf16[17,400,128]{2,1,0:T(8,128)(2,1)S(1)} collective-permute-done((bf16[17,400,128]{2,1,0:T(8,128)(2,1)S(1)}, bf16[17,400,128]{2,1,0:T(8,128)(2,1)S(1)}, u32[]{:S(2)}, u32[]{:S(2)}) %collective-permute-start.13) | collective-permute-done | bytes 1740832 | tf_op jit(solution)/shard_map/ppermute | solution.py:100
  98.8 0.5 fusion.8
  99.4 4.1 %collective-permute-start.16 = (bf16[8,192,128]{2,1,0:T(8,128)(2,1)S(1)}, bf16[8,192,128]{2,1,0:T(8,128)(2,1)S(1)}, u32[]{:S(2)}, u32[]{:S(2)}) collective-permute-start(bf16[8,192,128]{2,1,0:T(8,128)(2,1)S(1)} %slice.151), channel_id=1, source_target_pairs={{0,4},{4,0},{8,12},{12,8},{16,20},{20,16},{24,28},{28,24},{1,5},{5... | collective-permute-start | bytes 1179656 | tf_op jit(solution)/shard_map/ppermute | solution.py:100
  103.5 0.6 collective-permute-start.14
  104.1 8.8 %collective-permute-done.16 = bf16[8,192,128]{2,1,0:T(8,128)(2,1)S(1)} collective-permute-done((bf16[8,192,128]{2,1,0:T(8,128)(2,1)S(1)}, bf16[8,192,128]{2,1,0:T(8,128)(2,1)S(1)}, u32[]{:S(2)}, u32[]{:S(2)}) %collective-permute-start.16) | collective-permute-done | bytes 393248 | tf_op jit(solution)/shard_map/ppermute | solution.py:100
  113.0 0.6 collective-permute-start.17
  113.6 1.6 %collective-permute-done.14 = bf16[8,208,128]{2,1,0:T(8,128)(2,1)S(1)} collective-permute-done((bf16[8,208,128]{2,1,0:T(8,128)(2,1)S(1)}, bf16[8,208,128]{2,1,0:T(8,128)(2,1)S(1)}, u32[]{:S(2)}, u32[]{:S(2)}) %collective-permute-start.14) | collective-permute-done | bytes 426016 | tf_op jit(solution)/shard_map/ppermute | solution.py:100
  115.2 0.4 collective-permute-start.15
  115.6 3.9 %collective-permute-done.17 = bf16[4,192,128]{2,1,0:T(8,128)(2,1)S(1)} collective-permute-done((bf16[4,192,128]{2,1,0:T(8,128)(2,1)S(1)}, bf16[4,192,128]{2,1,0:T(8,128)(2,1)S(1)}, u32[]{:S(2)}, u32[]{:S(2)}) %collective-permute-start.17) | collective-permute-done | bytes 196640 | tf_op jit(solution)/shard_map/ppermute | solution.py:100
  119.5 1.9 %collective-permute-done.15 = bf16[4,208,128]{2,1,0:T(8,128)(2,1)S(1)} collective-permute-done((bf16[4,208,128]{2,1,0:T(8,128)(2,1)S(1)}, bf16[4,208,128]{2,1,0:T(8,128)(2,1)S(1)}, u32[]{:S(2)}, u32[]{:S(2)}) %collective-permute-start.15) | collective-permute-done | bytes 213024 | tf_op jit(solution)/shard_map/ppermute | solution.py:100
  121.6 0.6 collective-permute-start.18
  122.3 1.8 %collective-permute-start.19 = (bf16[1,400,128]{2,1,0:T(8,128)(2,1)S(1)}, bf16[1,400,128]{2,1,0:T(8,128)(2,1)S(1)}, u32[]{:S(2)}, u32[]{:S(2)}) collective-permute-start(bf16[1,400,128]{2,1,0:T(8,128)(2,1)S(1)} %get-tuple-element.99), channel_id=1, source_target_pairs={{0,16},{4,20},{8,24},{12,28},{16,0},{20,4},{24,8},{28,12},{1,17},{... | collective-permute-start | bytes 307208 | tf_op jit(solution)/shard_map/ppermute | solution.py:100
  124.1 2.0 %collective-permute-start.20 = (bf16[1,400,128]{2,1,0:T(8,128)(2,1)S(1)}, bf16[1,400,128]{2,1,0:T(8,128)(2,1)S(1)}, u32[]{:S(2)}, u32[]{:S(2)}) collective-permute-start(bf16[1,400,128]{2,1,0:T(8,128)(2,1)S(1)} %get-tuple-element.98), channel_id=1, source_target_pairs={{0,24},{4,28},{8,16},{12,20},{16,8},{20,12},{24,0},{28,4},{1,25},{... | collective-permute-start | bytes 307208 | tf_op jit(solution)/shard_map/ppermute | solution.py:100
  126.8 0.5 slice.117
  127.3 3.9 %collective-permute-done.19 = bf16[1,400,128]{2,1,0:T(8,128)(2,1)S(1)} collective-permute-done((bf16[1,400,128]{2,1,0:T(8,128)(2,1)S(1)}, bf16[1,400,128]{2,1,0:T(8,128)(2,1)S(1)}, u32[]{:S(2)}, u32[]{:S(2)}) %collective-permute-start.19) | collective-permute-done | bytes 102432 | tf_op jit(solution)/shard_map/ppermute | solution.py:100
  131.6 1.0 multiply_subtract_fusion
  (87 shorter events, 1.9 us)
Async XLA Ops:
  0.6 10.5 %copy-start.19 = (bf16[2,1,77,768]{3,0,2,1:T(2,128)(2,1)S(1)}, bf16[2,1,77,768]{3,0,2,1:T(2,128)(2,1)}, u32[]{:S(2)}) copy-start(bf16[2,1,77,768]{3,0,2,1:T(2,128)(2,1)} %param.17) | copy-start | bytes 709636
  2.0 9.2 %collective-permute-start = (bf16[1,400,128]{2,1,0:T(8,128)(2,1)S(1)}, bf16[1,400,128]{2,1,0:T(8,128)(2,1)S(1)}, u32[]{:S(2)}, u32[]{:S(2)}) collective-permute-start(bf16[1,400,128]{2,1,0:T(8,128)(2,1)S(1)} %maximum_bitcast_fusion), channel_id=1, source_target_pairs={{0,8},{4,12},{8,0},{12,4},{16,24},{20,28},{24,16},{28,20},{1,9},{5... | collective-permute-start | bytes 307208 | tf_op jit(solution)/shard_map/ppermute | solution.py:100
  5.1 10.8 %collective-permute-start.1 = (bf16[1,400,128]{2,1,0:T(8,128)(2,1)S(1)}, bf16[1,400,128]{2,1,0:T(8,128)(2,1)S(1)}, u32[]{:S(2)}, u32[]{:S(2)}) collective-permute-start(bf16[1,400,128]{2,1,0:T(8,128)(2,1)S(1)} %maximum_bitcast_fusion), channel_id=1, source_target_pairs={{0,16},{4,20},{8,24},{12,28},{16,0},{20,4},{24,8},{28,12},{1,17},{... | collective-permute-start | bytes 307208 | tf_op jit(solution)/shard_map/ppermute | solution.py:100
  7.7 8.2 %collective-permute-start.2 = (bf16[1,400,128]{2,1,0:T(8,128)(2,1)S(1)}, bf16[1,400,128]{2,1,0:T(8,128)(2,1)S(1)}, u32[]{:S(2)}, u32[]{:S(2)}) collective-permute-start(bf16[1,400,128]{2,1,0:T(8,128)(2,1)S(1)} %maximum_bitcast_fusion), channel_id=1, source_target_pairs={{0,24},{4,28},{8,16},{12,20},{16,8},{20,12},{24,0},{28,4},{1,25},{... | collective-permute-start | bytes 307208 | tf_op jit(solution)/shard_map/ppermute | solution.py:100
  8.7 8.9 %collective-permute-start.3 = (bf16[2,2,64,192]{3,2,1,0:T(8,128)(2,1)S(1)}, bf16[2,2,64,192]{3,2,1,0:T(8,128)(2,1)S(1)}, u32[]{:S(2)}, u32[]{:S(2)}) collective-permute-start(bf16[2,2,64,192]{3,2,1,0:T(8,128)(2,1)S(1)} %get-tuple-element.96), channel_id=1, source_target_pairs={{0,4},{4,0},{8,12},{12,8},{16,20},{20,16},{24,28},{28,24},{1,5},{5... | collective-permute-start | bytes 294920 | tf_op jit(solution)/shard_map/ppermute | solution.py:545
  10.4 7.2 %collective-permute-start.4 = (bf16[2,2,64,192]{3,2,1,0:T(8,128)(2,1)S(1)}, bf16[2,2,64,192]{3,2,1,0:T(8,128)(2,1)S(1)}, u32[]{:S(2)}, u32[]{:S(2)}) collective-permute-start(bf16[2,2,64,192]{3,2,1,0:T(8,128)(2,1)S(1)} %get-tuple-element.95), channel_id=1, source_target_pairs={{4,8},{8,4},{12,16},{16,12},{20,24},{24,20},{5,9},{9,5},{13,17},{1... | collective-permute-start | bytes 294920 | tf_op jit(solution)/shard_map/ppermute | solution.py:545
  11.2 16.1 %copy-start = (bf16[2,8,64,192]{3,2,1,0:T(8,128)(2,1)S(1)}, bf16[2,8,64,192]{3,2,1,0:T(8,128)(2,1)}, u32[]{:S(2)}) copy-start(bf16[2,8,64,192]{3,2,1,0:T(8,128)(2,1)} %param.15) | copy-start | bytes 1179652
  11.2 16.1 %copy-start.1 = (bf16[2,8,64,320]{3,2,1,0:T(8,128)(2,1)S(1)}, bf16[2,8,64,320]{3,2,1,0:T(8,128)(2,1)}, u32[]{:S(2)}) copy-start(bf16[2,8,64,320]{3,2,1,0:T(8,128)(2,1)} %param.16) | copy-start | bytes 1966084
  11.2 16.1 %copy-start.2 = (bf16[768,320]{0,1:T(8,128)(2,1)S(1)}, bf16[768,320]{0,1:T(8,128)(2,1)}, u32[]{:S(2)}) copy-start(bf16[768,320]{0,1:T(8,128)(2,1)} %param.22) | copy-start | bytes 1474564
  11.2 16.1 %copy-start.3 = (bf16[768,320]{0,1:T(8,128)(2,1)S(1)}, bf16[768,320]{0,1:T(8,128)(2,1)}, u32[]{:S(2)}) copy-start(bf16[768,320]{0,1:T(8,128)(2,1)} %param.23) | copy-start | bytes 1474564
  11.2 16.1 %copy-start.4 = (bf16[320,320]{1,0:T(8,128)(2,1)S(1)}, bf16[320,320]{1,0:T(8,128)(2,1)}, u32[]{:S(2)}) copy-start(bf16[320,320]{1,0:T(8,128)(2,1)} %wq_far.1) | copy-start | bytes 614404
  11.2 16.1 %copy-start.5 = (bf16[320,320]{1,0:T(8,128)(2,1)S(1)}, bf16[320,320]{1,0:T(8,128)(2,1)}, u32[]{:S(2)}) copy-start(bf16[320,320]{1,0:T(8,128)(2,1)} %wo_far.1) | copy-start | bytes 614404
  15.9 5.7 %collective-permute-start.7 = (bf16[4,192,128]{2,1,0:T(8,128)(2,1)S(1)}, bf16[4,192,128]{2,1,0:T(8,128)(2,1)S(1)}, u32[]{:S(2)}, u32[]{:S(2)}) collective-permute-start(bf16[4,192,128]{2,1,0:T(8,128)(2,1)S(1)} %pad_maximum_fusion.6), channel_id=1, source_target_pairs={{0,2},{1,3},{2,0},{3,1},{4,6},{5,7},{6,4},{7,5},{8,10},{9,11},{10,... | collective-permute-start | bytes 589832 | tf_op jit(solution)/shard_map/ppermute | solution.py:100
  17.6 8.2 %collective-permute-start.5 = (bf16[4,208,128]{2,1,0:T(8,128)(2,1)S(1)}, bf16[4,208,128]{2,1,0:T(8,128)(2,1)S(1)}, u32[]{:S(2)}, u32[]{:S(2)}) collective-permute-start(bf16[4,208,128]{2,1,0:T(8,128)(2,1)S(1)} %slice.144), channel_id=1, source_target_pairs={{0,4},{4,0},{8,12},{12,8},{16,20},{20,16},{24,28},{28,24},{1,5},{5... | collective-permute-start | bytes 638984 | tf_op jit(solution)/shard_map/ppermute | solution.py:100
  21.7 11.1 %collective-permute-start.8 = (bf16[8,192,128]{2,1,0:T(8,128)(2,1)S(1)}, bf16[8,192,128]{2,1,0:T(8,128)(2,1)S(1)}, u32[]{:S(2)}, u32[]{:S(2)}) collective-permute-start(bf16[8,192,128]{2,1,0:T(8,128)(2,1)S(1)} %pad_maximum_fusion.5), channel_id=1, source_target_pairs={{0,4},{4,0},{8,12},{12,8},{16,20},{20,16},{24,28},{28,24},{1,5},{5... | collective-permute-start | bytes 1179656 | tf_op jit(solution)/shard_map/ppermute | solution.py:100
  25.9 9.0 %collective-permute-start.6 = (bf16[8,208,128]{2,1,0:T(8,128)(2,1)S(1)}, bf16[8,208,128]{2,1,0:T(8,128)(2,1)S(1)}, u32[]{:S(2)}, u32[]{:S(2)}) collective-permute-start(bf16[8,208,128]{2,1,0:T(8,128)(2,1)S(1)} %pad_maximum_fusion.3), channel_id=1, source_target_pairs={{0,2},{1,3},{2,0},{3,1},{4,6},{5,7},{6,4},{7,5},{8,10},{9,11},{10,... | collective-permute-start | bytes 1277960 | tf_op jit(solution)/shard_map/ppermute | solution.py:100
  29.2 1.3 copy-start.10
  30.5 0.7 copy-start.15
  31.2 18.6 %copy-start.11 = (bf16[2,320,512]{2,1,0:T(8,128)(2,1)}, bf16[2,320,512]{2,1,0:T(8,128)(2,1)S(1)}, u32[]{:S(2)}) copy-start(bf16[2,320,512]{2,1,0:T(8,128)(2,1)S(1)} %get-tuple-element.64.resid_far) | copy-start | bytes 1966084
  31.2 18.6 %copy-start.12 = (bf16[2,8,80,40]{3,2,1,0:T(8,128)(2,1)}, bf16[2,8,80,40]{3,2,1,0:T(8,128)(2,1)S(1)}, u32[]{:S(2)}) copy-start(bf16[2,8,80,40]{3,2,1,0:T(8,128)(2,1)S(1)} %get-tuple-element.66.keys_far) | copy-start | bytes 307204
  31.2 18.6 %copy-start.13 = (bf16[2,8,80,40]{3,2,1,0:T(8,128)(2,1)}, bf16[2,8,80,40]{3,2,1,0:T(8,128)(2,1)S(1)}, u32[]{:S(2)}) copy-start(bf16[2,8,80,40]{3,2,1,0:T(8,128)(2,1)S(1)} %get-tuple-element.69.values_far) | copy-start | bytes 307204
  31.2 18.6 %copy-start.14 = (bf16[320,320]{1,0:T(8,128)(2,1)}, bf16[320,320]{1,0:T(8,128)(2,1)S(1)}, u32[]{:S(2)}) copy-start(bf16[320,320]{1,0:T(8,128)(2,1)S(1)} %get-tuple-element.65.wqt_far) | copy-start | bytes 614404
  31.2 18.6 %copy-start.16 = (bf16[2,8,40,80]{3,2,1,0:T(8,128)(2,1)}, bf16[2,8,40,80]{3,2,1,0:T(8,128)(2,1)S(1)}, u32[]{:S(2)}) copy-start(bf16[2,8,40,80]{3,2,1,0:T(8,128)(2,1)S(1)} %get-tuple-element.70.keyst_far) | copy-start | bytes 307204
  31.2 18.6 %copy-start.17 = (bf16[2,8,40,80]{3,2,1,0:T(8,128)(2,1)}, bf16[2,8,40,80]{3,2,1,0:T(8,128)(2,1)S(1)}, u32[]{:S(2)}) copy-start(bf16[2,8,40,80]{3,2,1,0:T(8,128)(2,1)S(1)} %get-tuple-element.67.valuest_far) | copy-start | bytes 307204
  31.2 4.3 %copy-start.22 = (f32[1000]{0:T(1024)S(1)}, f32[1000]{0:T(1024)}, u32[]{:S(2)}) copy-start(f32[1000]{0:T(1024)} %constant.57.clone) | copy-start | bytes 12004
  31.3 4.3 %copy-start.23 = (s32[2,1]{0,1:T(1,128)S(1)}, s32[2,1]{0,1:T(1,128)}, u32[]{:S(2)}) copy-start(s32[2,1]{0,1:T(1,128)} %param.19) | copy-start | bytes 28
  35.0 3.6 %collective-permute-start.9 = (bf16[16,208,128]{2,1,0:T(8,128)(2,1)S(1)}, bf16[16,208,128]{2,1,0:T(8,128)(2,1)S(1)}, u32[]{:S(2)}, u32[]{:S(2)}) collective-permute-start(bf16[16,208,128]{2,1,0:T(8,128)(2,1)S(1)} %pad_maximum_fusion.1.own_a), channel_id=1, source_target_pairs={{0,1},{1,0},{2,3},{3,2},{4,5},{5,4},{6,7},{7,6},{8,9},{9,8},{10,11... | collective-permute-start | bytes 2555912 | tf_op jit(solution)/shard_map/ppermute | solution.py:100
  35.1 3.5 %collective-permute-start.10 = (bf16[16,192,128]{2,1,0:T(8,128)(2,1)S(1)}, bf16[16,192,128]{2,1,0:T(8,128)(2,1)S(1)}, u32[]{:S(2)}, u32[]{:S(2)}) collective-permute-start(bf16[16,192,128]{2,1,0:T(8,128)(2,1)S(1)} %pad_maximum_fusion.2.own_b), channel_id=1, source_target_pairs={{0,1},{1,0},{2,3},{3,2},{4,5},{5,4},{6,7},{7,6},{8,9},{9,8},{10,11... | collective-permute-start | bytes 2359304 | tf_op jit(solution)/shard_map/ppermute | solution.py:100
  35.8 26.1 %copy-start.6 = (f32[2,8,64,4]{2,3,1,0:T(4,128)S(1)}, f32[2,8,64,4]{2,3,1,0:T(4,128)}, u32[]{:S(2)}) copy-start(f32[2,8,64,4]{2,3,1,0:T(4,128)} %param.18) | copy-start | bytes 49156
  35.8 26.1 %copy-start.7 = (bf16[320,4]{0,1:T(4,128)(2,1)S(1)}, bf16[320,4]{0,1:T(4,128)(2,1)}, u32[]{:S(2)}) copy-start(bf16[320,4]{0,1:T(4,128)(2,1)} %param.25) | copy-start | bytes 7684
  71.3 9.6 %all-to-all-start.1 = ((f32[32,1,128]{2,1,0:T(1,128)}), f32[32,1,128]{2,1,0:T(1,128)S(1)}, u32[]{:S(2)}, u32[]{:S(2)}) async-start(f32[32,1,128]{2,1,0:T(1,128)} %get-tuple-element.71), calls=%async_computation.1 | async-start | bytes 32768 | tf_op jit(solution)/shard_map/all_to_all | solution.py:549
  77.0 1.5 %copy-start.8 = (bf16[2,640,960]{2,1,0:T(8,128)(2,1)}, bf16[2,640,960]{2,1,0:T(8,128)(2,1)S(1)}, u32[]{:S(2)}) copy-start(bf16[2,640,960]{2,1,0:T(8,128)(2,1)S(1)} %get-tuple-element.83.x3) | copy-start | bytes 7372804
  80.9 1.8 %copy-start.9 = (bf16[2,640,960]{2,1,0:T(8,128)(2,1)S(1)}, bf16[2,640,960]{2,1,0:T(8,128)(2,1)}, u32[]{:S(2)}) copy-start(bf16[2,640,960]{2,1,0:T(8,128)(2,1)} %copy-done.8) | copy-start | bytes 7372804
  81.4 5.5 %collective-permute-start.11 = (bf16[2,64,320]{2,1,0:T(8,128)(2,1)S(1)}, bf16[2,64,320]{2,1,0:T(8,128)(2,1)S(1)}, u32[]{:S(2)}, u32[]{:S(2)}) collective-permute-start(bf16[2,64,320]{2,1,0:T(8,128)(2,1)S(1)} %get-tuple-element.80), channel_id=1, source_target_pairs={{0,4},{4,0},{8,12},{12,8},{16,20},{20,16},{24,28},{28,24},{1,5},{5... | collective-permute-start | bytes 245768 | tf_op jit(solution)/shard_map/ppermute | solution.py:545
  82.1 4.8 %collective-permute-start.12 = (bf16[2,64,320]{2,1,0:T(8,128)(2,1)S(1)}, bf16[2,64,320]{2,1,0:T(8,128)(2,1)S(1)}, u32[]{:S(2)}, u32[]{:S(2)}) collective-permute-start(bf16[2,64,320]{2,1,0:T(8,128)(2,1)S(1)} %get-tuple-element.81), channel_id=1, source_target_pairs={{4,8},{8,4},{12,16},{16,12},{20,24},{24,20},{5,9},{9,5},{13,17},{1... | collective-permute-start | bytes 245768 | tf_op jit(solution)/shard_map/ppermute | solution.py:545
  95.1 3.7 %collective-permute-start.13 = (bf16[17,400,128]{2,1,0:T(8,128)(2,1)S(1)}, bf16[17,400,128]{2,1,0:T(8,128)(2,1)S(1)}, u32[]{:S(2)}, u32[]{:S(2)}) collective-permute-start(bf16[17,400,128]{2,1,0:T(8,128)(2,1)S(1)} %get-tuple-element.89), channel_id=1, source_target_pairs={{0,1},{1,0},{2,3},{3,2},{4,5},{5,4},{6,7},{7,6},{8,9},{9,8},{10,11... | collective-permute-start | bytes 5222408 | tf_op jit(solution)/shard_map/ppermute | solution.py:100
  99.4 13.5 %collective-permute-start.16 = (bf16[8,192,128]{2,1,0:T(8,128)(2,1)S(1)}, bf16[8,192,128]{2,1,0:T(8,128)(2,1)S(1)}, u32[]{:S(2)}, u32[]{:S(2)}) collective-permute-start(bf16[8,192,128]{2,1,0:T(8,128)(2,1)S(1)} %slice.151), channel_id=1, source_target_pairs={{0,4},{4,0},{8,12},{12,8},{16,20},{20,16},{24,28},{28,24},{1,5},{5... | collective-permute-start | bytes 1179656 | tf_op jit(solution)/shard_map/ppermute | solution.py:100
  103.5 11.6 %collective-permute-start.14 = (bf16[8,208,128]{2,1,0:T(8,128)(2,1)S(1)}, bf16[8,208,128]{2,1,0:T(8,128)(2,1)S(1)}, u32[]{:S(2)}, u32[]{:S(2)}) collective-permute-start(bf16[8,208,128]{2,1,0:T(8,128)(2,1)S(1)} %slice.147), channel_id=1, source_target_pairs={{0,2},{1,3},{2,0},{3,1},{4,6},{5,7},{6,4},{7,5},{8,10},{9,11},{10,... | collective-permute-start | bytes 1277960 | tf_op jit(solution)/shard_map/ppermute | solution.py:100
  113.0 6.5 %collective-permute-start.17 = (bf16[4,192,128]{2,1,0:T(8,128)(2,1)S(1)}, bf16[4,192,128]{2,1,0:T(8,128)(2,1)S(1)}, u32[]{:S(2)}, u32[]{:S(2)}) collective-permute-start(bf16[4,192,128]{2,1,0:T(8,128)(2,1)S(1)} %slice.196), channel_id=1, source_target_pairs={{0,2},{1,3},{2,0},{3,1},{4,6},{5,7},{6,4},{7,5},{8,10},{9,11},{10,... | collective-permute-start | bytes 589832 | tf_op jit(solution)/shard_map/ppermute | solution.py:100
  115.2 6.2 %collective-permute-start.15 = (bf16[4,208,128]{2,1,0:T(8,128)(2,1)S(1)}, bf16[4,208,128]{2,1,0:T(8,128)(2,1)S(1)}, u32[]{:S(2)}, u32[]{:S(2)}) collective-permute-start(bf16[4,208,128]{2,1,0:T(8,128)(2,1)S(1)} %slice.195), channel_id=1, source_target_pairs={{0,4},{4,0},{8,12},{12,8},{16,20},{20,16},{24,28},{28,24},{1,5},{5... | collective-permute-start | bytes 638984 | tf_op jit(solution)/shard_map/ppermute | solution.py:100
  121.6 10.0 %copy-start.18 = (f32[49320]{0:T(1024)S(1)}, f32[49320]{0:T(1024)}, u32[]{:S(2)}) copy-start(f32[49320]{0:T(1024)} %param.26) | copy-start | bytes 591844
  121.6 10.0 %copy-start.20 = (f32[49320]{0:T(1024)S(1)}, f32[49320]{0:T(1024)}, u32[]{:S(2)}) copy-start(f32[49320]{0:T(1024)} %param.28) | copy-start | bytes 591844
  121.6 10.0 %copy-start.21 = (f32[49320]{0:T(1024)S(1)}, f32[49320]{0:T(1024)}, u32[]{:S(2)}) copy-start(f32[49320]{0:T(1024)} %param.27) | copy-start | bytes 591844
  121.6 5.7 %collective-permute-start.18 = (bf16[1,400,128]{2,1,0:T(8,128)(2,1)S(1)}, bf16[1,400,128]{2,1,0:T(8,128)(2,1)S(1)}, u32[]{:S(2)}, u32[]{:S(2)}) collective-permute-start(bf16[1,400,128]{2,1,0:T(8,128)(2,1)S(1)} %get-tuple-element.97), channel_id=1, source_target_pairs={{0,8},{4,12},{8,0},{12,4},{16,24},{20,28},{24,16},{28,20},{1,9},{5... | collective-permute-start | bytes 307208 | tf_op jit(solution)/shard_map/ppermute | solution.py:100
  122.3 9.0 %collective-permute-start.19 = (bf16[1,400,128]{2,1,0:T(8,128)(2,1)S(1)}, bf16[1,400,128]{2,1,0:T(8,128)(2,1)S(1)}, u32[]{:S(2)}, u32[]{:S(2)}) collective-permute-start(bf16[1,400,128]{2,1,0:T(8,128)(2,1)S(1)} %get-tuple-element.99), channel_id=1, source_target_pairs={{0,16},{4,20},{8,24},{12,28},{16,0},{20,4},{24,8},{28,12},{1,17},{... | collective-permute-start | bytes 307208 | tf_op jit(solution)/shard_map/ppermute | solution.py:100
  124.1 7.2 %collective-permute-start.20 = (bf16[1,400,128]{2,1,0:T(8,128)(2,1)S(1)}, bf16[1,400,128]{2,1,0:T(8,128)(2,1)S(1)}, u32[]{:S(2)}, u32[]{:S(2)}) collective-permute-start(bf16[1,400,128]{2,1,0:T(8,128)(2,1)S(1)} %get-tuple-element.98), channel_id=1, source_target_pairs={{0,24},{4,28},{8,16},{12,20},{16,8},{20,12},{24,0},{28,4},{1,25},{... | collective-permute-start | bytes 307208 | tf_op jit(solution)/shard_map/ppermute | solution.py:100
